TPU v7x, 512 devices: a whole 4x4x16 slice. The times are simulated.
512 devices in a mesh: nx: 32 (over z_hi, y, x), ny: 16 (over z_lo, core).
Axes of the slice: x: 4, y: 4, z: 16 (z_hi: 2, z_lo: 8; z = z_hi * 8 + z_lo), core: 2. Of those that a mesh axis runs over, the one named last changes fastest.
Arguments:
- state: float32 [16, 1536, 6144], P(None, 'nx', 'ny'), may hold values from -6 to 6
- diffuse: float32 [16, 1536, 6144], P(None, 'nx', 'ny'), may hold values from 0.02 to 0.12
- vertical: float32 [1536, 6144], P('nx', 'ny'), may hold values from 0.1 to 2
- rows_we: float32 [3, 2, 16, 2048], P(None, None, None, 'ny'), may hold values from -6 to 6
- rows_sn: float32 [3, 2, 16, 512], P(None, None, None, 'nx'), may hold values from -6 to 6
- fill_we: float32 [2, 16, 2048], P(None, None, 'ny'), may hold values from -6 to 6
- fill_sn: float32 [2, 16, 512], P(None, None, 'nx'), may hold values from -6 to 6
- index_we: int32 [6144], P('ny'), may hold values from 0 to 2046
- weight_we: float32 [6144], P('ny'), may hold values from 0 to 1
- index_sn: int32 [1536], P('nx'), may hold values from 0 to 510
- weight_sn: float32 [1536], P('nx'), may hold values from 0 to 1
- jump: int32 [2], replicated, may hold values from -1 to 1
Outputs:
- final_state: float32 [16, 1536, 6144], P(None, 'nx', 'ny')
Inputs may be any that keep to these rules, and one draw needn't show every extreme that they name: Each entry of the jump is -1, 0 or 1. index_we[j] and index_sn[i] follow the nest ratio: they are nondecreasing, and index_we[j] - j // 3 and index_sn[i] - i // 3 each stay within ±2 of one fixed offset.
All inputs are finite; a program needn't handle non-finite values.
Results may differ from a plain program's by a relative error of at most 0.00002.
Values sent between devices are 32-bit elements; how exact they have to be, the bound alone decides.
No kernel may reach another device: no remote copies, remote signals or barrier semaphores. Data moves between devices by JAX's collectives and lax.ppermute only.
A program may use at most 64 MiB of HBM per device.

v0:
```python
import jax
import jax.numpy as jnp
from jax import lax
from jax.sharding import PartitionSpec as P


def with_halo(block, sides, width):
    for axis, dim in sides:
        count = lax.axis_size(axis)
        forward = [(i, i + 1) for i in range(count - 1)]
        backward = [(target, source) for source, target in forward]
        low = lax.ppermute(
            lax.slice_in_dim(block, block.shape[dim] - width, None, axis=dim), axis, forward
        )
        high = lax.ppermute(lax.slice_in_dim(block, 0, width, axis=dim), axis, backward)
        block = jnp.concatenate([low, block, high], axis=dim)
    return block


def column_solve(explicit, vertical):
    layers = explicit.shape[0]
    factors = []
    sources = []
    for layer_index in range(layers):
        if layer_index == 0 or layer_index == layers - 1:
            diagonal_term = 1.0 + vertical
        else:
            diagonal_term = 1.0 + 2.0 * vertical
        if layer_index == 0:
            pivot_value = diagonal_term
            source_term = explicit[layer_index]
        else:
            pivot_value = diagonal_term + vertical * factors[-1]
            source_term = explicit[layer_index] + vertical * sources[-1]
        factors.append(-vertical / pivot_value)
        sources.append(source_term / pivot_value)
    result = [sources[-1]]
    for layer_index in range(layers - 2, -1, -1):
        result.append(sources[layer_index] - factors[layer_index] * result[-1])
    return jnp.stack(result[::-1], axis=0)


def blend(rows, index, weight):
    lower = rows[..., index]
    upper = rows[..., index + 1]
    return (1.0 - weight) * lower + weight * upper


def neighbours(field):
    return with_halo(field, (("nx", 1), ("ny", 2)), 1)


def on_device(
    state,
    diffuse,
    vertical,
    rows_we,
    rows_sn,
    fill_we,
    fill_sn,
    index_we,
    weight_we,
    index_sn,
    weight_sn,
    jump,
):
    layers, width_x, width_y = state.shape
    count_x = lax.axis_size("nx")
    count_y = lax.axis_size("ny")
    total_x = width_x * count_x
    total_y = width_y * count_y
    place_x = lax.axis_index("nx")
    place_y = lax.axis_index("ny")
    parent_y, filler_y = (
        lax.all_gather(rows_we, "ny", axis=3, tiled=True),
        lax.all_gather(fill_we, "ny", axis=2, tiled=True),
    )
    parent_x, filler_x = (
        lax.all_gather(rows_sn, "nx", axis=3, tiled=True),
        lax.all_gather(fill_sn, "nx", axis=2, tiled=True),
    )
    edge_y = blend(parent_y, index_we, weight_we)
    edge_x = blend(parent_x, index_sn, weight_sn)

    def advance(padded, step_index):
        west_side = place_x == 0
        east_side = place_x == count_x - 1
        south_side = place_y == 0
        north_side = place_y == count_y - 1
        padded = padded.at[:, 0, 1:-1].set(
            jnp.where(west_side, edge_y[step_index, 0], padded[:, 0, 1:-1])
        )
        padded = padded.at[:, -1, 1:-1].set(
            jnp.where(east_side, edge_y[step_index, 1], padded[:, -1, 1:-1])
        )
        padded = padded.at[:, 1:-1, 0].set(
            jnp.where(south_side, edge_x[step_index, 0], padded[:, 1:-1, 0])
        )
        padded = padded.at[:, 1:-1, -1].set(
            jnp.where(north_side, edge_x[step_index, 1], padded[:, 1:-1, -1])
        )
        center = padded[:, 1:-1, 1:-1]
        laplace = (
            padded[:, 2:, 1:-1]
            + padded[:, :-2, 1:-1]
            + padded[:, 1:-1, 2:]
            + padded[:, 1:-1, :-2]
            - 4.0 * center
        )
        explicit = center + diffuse * laplace
        return column_solve(explicit, vertical)

    shift_x = jump[0]
    shift_y = jump[1]
    first = advance(neighbours(state), 0)
    extended = with_halo(first, (("nx", 1), ("ny", 2)), 3)
    span_x = width_x + 2 * 0
    span_y = width_y + 2 * 0
    region = lax.dynamic_slice(
        extended, (jnp.int32(0), 3 - 0 + 3 * shift_x, 3 - 0 + 3 * shift_y), (layers, span_x, span_y)
    )
    source_x = place_x * width_x - 0 + jnp.arange(span_x, dtype=jnp.int32) + 3 * shift_x
    source_y = place_y * width_y - 0 + jnp.arange(span_y, dtype=jnp.int32) + 3 * shift_y
    coarse_y = jnp.clip(source_y, 0, total_y - 1) // 3
    coarse_x = jnp.clip(source_x, 0, total_x - 1) // 3
    west = filler_y[0][:, coarse_y][:, None, :]
    east = filler_y[1][:, coarse_y][:, None, :]
    south = filler_x[0][:, coarse_x][:, :, None]
    north = filler_x[1][:, coarse_x][:, :, None]
    below_x = (source_x < 0)[None, :, None]
    above_x = (source_x >= total_x)[None, :, None]
    below_y = (source_y < 0)[None, None, :]
    above_y = (source_y >= total_y)[None, None, :]
    moved = jnp.where(
        below_x,
        west,
        jnp.where(above_x, east, jnp.where(below_y, south, jnp.where(above_y, north, region))),
    )
    second = advance(neighbours(moved), 1)
    return advance(neighbours(second), 2)


def solution(mesh):
    return jax.shard_map(
        on_device,
        mesh=mesh,
        in_specs=(
            P(None, "nx", "ny"),
            P(None, "nx", "ny"),
            P("nx", "ny"),
            P(None, None, None, "ny"),
            P(None, None, None, "nx"),
            P(None, None, "ny"),
            P(None, None, "nx"),
            P("ny"),
            P("ny"),
            P("nx"),
            P("nx"),
            P(),
        ),
        out_specs=P(None, "nx", "ny"),
        check_vma=False,
    )
```

profile of v0, /device:TPU:31, one launch (start us, length us, event | category | flops | bytes accessed | tf_op | source)
XLA Modules:
  0.0 661.2 jit_solution(5612297855299217869)
XLA Ops:
  0.0 1.7 fusion.154
  1.7 15.0 %collective-permute-start = (f32[16,1,384]{2,1,0:T(1,128)}, f32[16,1,384]{2,1,0:T(1,128)}, u32[]{:S(2)}, u32[]{:S(2)}) collective-permute-start(f32[16,1,384]{2,1,0:T(1,128)} %get-tuple-element.210), channel_id=1, source_target_pairs={{0,16},{16,32},{32,48},{48,64},{64,80},{80,96},{96,112},{112,128},... | collective-permute-start | bytes 73736 | tf_op jit(solution)/shard_map/ppermute | solution.py:12
  16.7 1.9 collective-permute-start.1
  20.3 74.8 %all_gather.14 = f32[3,2,16,2048]{2,1,3,0:T(2,128)} all-gather(f32[3,2,16,128]{2,1,3,0:T(2,128)S(1)} %copy.1584), channel_id=1, replica_groups=mesh['nx'=32,'ny'=16] {'ny'}, dimensions={3}, use_global_device_ids=true | all-gather | bytes 835584 | tf_op jit(solution)/shard_map/all_gather | solution.py:75
  95.1 5.1 gather_fusion.4
  100.3 5.1 gather_fusion.5
  106.9 1.8 fusion.150
  108.8 154.9 %all_gather.15 = f32[3,2,16,512]{2,1,3,0:T(2,128)S(1)} all-gather(f32[3,2,16,16]{2,1,3,0:T(2,128)S(1)} %copy.1587), channel_id=1, replica_groups=mesh['nx'=32,'ny'=16] {'nx'}, dimensions={3}, use_global_device_ids=true | all-gather | bytes 202752 | tf_op jit(solution)/shard_map/all_gather | solution.py:79
  268.0 30.5 %all_gather.12 = f32[2,16,2048]{2,1,0:T(8,128)S(1)} all-gather(f32[2,16,128]{2,1,0:T(8,128)S(1)} %copy-done.18), channel_id=1, replica_groups=mesh['nx'=32,'ny'=16] {'ny'}, dimensions={2}, use_global_device_ids=true | all-gather | bytes 278528 | tf_op jit(solution)/shard_map/all_gather | solution.py:76
  299.3 135.0 %all_gather.13 = f32[2,16,512]{1,0,2:T(2,128)S(1)} all-gather(f32[2,16,16]{1,0,2:T(2,128)S(1)} %copy.1581), channel_id=1, replica_groups=mesh['nx'=32,'ny'=16] {'nx'}, dimensions={2}, use_global_device_ids=true | all-gather | bytes 67584 | tf_op jit(solution)/shard_map/all_gather | solution.py:80
  439.6 17.9 %collective-permute-start.2 = (f32[16,50,1]{2,1,0:T(8,128)S(1)}, f32[16,50,1]{2,1,0:T(8,128)S(1)}, u32[]{:S(2)}, u32[]{:S(2)}) collective-permute-start(f32[16,50,1]{2,1,0:T(8,128)S(1)} %get-tuple-element.196), channel_id=1, source_target_pairs={{0,1},{1,2},{2,3},{3,4},{4,5},{5,6},{6,7},{7,8},{8,9},{9,10},{10,1... | collective-permute-start | bytes 9608 | tf_op jit(solution)/shard_map/ppermute | solution.py:12
  457.5 2.1 collective-permute-start.3
  460.4 2.5 collective-permute-done.2
  462.9 4.4 collective-permute-done.3
  468.9 4.2 scatter.40
  473.2 2.9 scatter.41
  476.2 4.7 scatter.44
  481.8 6.7 %scatter.45 = f32[16,50,386]{2,1,0:T(8,128)S(1)} dynamic-update-slice(f32[16,50,386]{2,1,0:T(8,128)S(1)} %scatter.44, f32[16,48,1]{2,1,0:T(8,128)} %slice_select_fusion.4, s32[]{:T(128)} %constant.338.clone.1, s32[]{:T(128)} %constant.342.clone.1, s32[]{:T(128)} %constant.356.clone.1) | dynamic-update-slice | bytes 6148 | tf_op jit(solution)/shard_map/scatter | solution.py:99
  491.1 14.7 %collective-permute-start.4 = (f32[16,3,384]{2,1,0:T(4,128)S(1)}, f32[16,3,384]{2,1,0:T(4,128)S(1)}, u32[]{:S(2)}, u32[]{:S(2)}) collective-permute-start(f32[16,3,384]{2,1,0:T(4,128)S(1)} %get-tuple-element.208), channel_id=1, source_target_pairs={{0,16},{16,32},{32,48},{48,64},{64,80},{80,96},{96,112},{112,128},... | collective-permute-start | bytes 221192 | tf_op jit(solution)/shard_map/ppermute | solution.py:12
  505.8 1.9 collective-permute-start.5
  507.7 16.6 %collective-permute-done.5 = f32[16,3,384]{2,1,0:T(4,128)S(1)} collective-permute-done((f32[16,3,384]{2,1,0:T(4,128)S(1)}, f32[16,3,384]{2,1,0:T(4,128)S(1)}, u32[]{:S(2)}, u32[]{:S(2)}) %collective-permute-start.5) | collective-permute-done | bytes 73760 | tf_op jit(solution)/shard_map/ppermute | solution.py:15
  525.4 4.0 collective-permute-start.6
  529.4 1.9 collective-permute-start.7
  537.4 1.7 gather_fusion.2
  541.6 2.9 fusion.5
  544.6 1.9 collective-permute-start.8
  546.5 3.4 collective-permute-start.9
  552.3 11.8 %collective-permute-done.9 = f32[16,1,384]{2,1,0:T(1,128)S(1)} collective-permute-done((f32[16,1,384]{2,1,0:T(1,128)S(1)}, f32[16,1,384]{2,1,0:T(1,128)S(1)}, u32[]{:S(2)}, u32[]{:S(2)}) %collective-permute-start.9) | collective-permute-done | bytes 24608 | tf_op jit(solution)/shard_map/ppermute | solution.py:15
  564.4 4.7 collective-permute-start.10
  569.0 2.1 collective-permute-start.11
  571.2 3.2 collective-permute-done.10
  574.4 4.4 collective-permute-done.11
  579.7 4.2 scatter.46
  584.0 2.9 scatter.49
  587.0 4.7 scatter.50
  592.6 6.7 %scatter.51 = f32[16,50,386]{2,1,0:T(8,128)S(1)} dynamic-update-slice(f32[16,50,386]{2,1,0:T(8,128)S(1)} %scatter.50, f32[16,48,1]{2,1,0:T(8,128)} %slice_select_fusion.2, s32[]{:T(128)} %constant.338.clone.1, s32[]{:T(128)} %constant.342.clone.1, s32[]{:T(128)} %constant.356.clone.1) | dynamic-update-slice | bytes 6148 | tf_op jit(solution)/shard_map/scatter | solution.py:99
  601.8 2.3 collective-permute-start.12
  604.2 3.0 collective-permute-start.13
  609.6 12.2 %collective-permute-done.13 = f32[16,1,384]{2,1,0:T(1,128)S(1)} collective-permute-done((f32[16,1,384]{2,1,0:T(1,128)S(1)}, f32[16,1,384]{2,1,0:T(1,128)S(1)}, u32[]{:S(2)}, u32[]{:S(2)}) %collective-permute-start.13) | collective-permute-done | bytes 24608 | tf_op jit(solution)/shard_map/ppermute | solution.py:15
  622.0 3.0 collective-permute-start.14
  625.1 2.2 collective-permute-start.15
  627.3 3.2 collective-permute-done.14
  630.5 4.4 collective-permute-done.15
  634.9 2.2 pad_maximum_fusion.2
  637.0 4.2 scatter.54
  641.3 2.9 scatter.55
  645.0 4.4 scatter.56
  650.4 6.7 %scatter.59 = f32[16,50,386]{2,1,0:T(8,128)S(1)} dynamic-update-slice(f32[16,50,386]{2,1,0:T(8,128)S(1)} %scatter.56, f32[16,48,1]{2,1,0:T(8,128)} %slice_select_fusion, s32[]{:T(128)} %constant.338.clone.1, s32[]{:T(128)} %constant.342.clone.1, s32[]{:T(128)} %constant.356.clone.1) | dynamic-update-slice | bytes 6148 | tf_op jit(solution)/shard_map/scatter | solution.py:99
  (174 shorter events, 43.7 us)
Async XLA Ops:
  1.7 436.9 %collective-permute-start = (f32[16,1,384]{2,1,0:T(1,128)}, f32[16,1,384]{2,1,0:T(1,128)}, u32[]{:S(2)}, u32[]{:S(2)}) collective-permute-start(f32[16,1,384]{2,1,0:T(1,128)} %get-tuple-element.210), channel_id=1, source_target_pairs={{0,16},{16,32},{32,48},{48,64},{64,80},{80,96},{96,112},{112,128},... | collective-permute-start | bytes 73736 | tf_op jit(solution)/shard_map/ppermute | solution.py:12
  16.7 421.9 %collective-permute-start.1 = (f32[16,1,384]{2,1,0:T(1,128)}, f32[16,1,384]{2,1,0:T(1,128)}, u32[]{:S(2)}, u32[]{:S(2)}) collective-permute-start(f32[16,1,384]{2,1,0:T(1,128)} %get-tuple-element.211), channel_id=1, source_target_pairs={{16,0},{32,16},{48,32},{64,48},{80,64},{96,80},{112,96},{128,112},... | collective-permute-start | bytes 73736 | tf_op jit(solution)/shard_map/ppermute | solution.py:15
  20.3 85.1 %copy-start.20 = (f32[384]{0:T(512)S(1)}, f32[384]{0:T(512)}, u32[]{:S(2)}) copy-start(f32[384]{0:T(512)} %param.44) | copy-start | bytes 4612
  106.9 1.8 copy-start.24
  106.9 1.8 copy-start.16
  108.7 156.5 %copy-start.23 = (f32[48]{0:T(128)S(1)}, f32[48]{0:T(128)}, u32[]{:S(2)}) copy-start(f32[48]{0:T(128)} %param.46) | copy-start | bytes 580
  108.8 157.4 %copy-start.22 = (s32[2]{0:T(128)S(1)}, s32[2]{0:T(128)}, u32[]{:S(2)}) copy-start(s32[2]{0:T(128)} %param.47) | copy-start | bytes 28
  108.8 159.2 %copy-start.18 = (f32[2,16,128]{2,1,0:T(8,128)S(1)}, f32[2,16,128]{2,1,0:T(8,128)}, u32[]{:S(2)}) copy-start(f32[2,16,128]{2,1,0:T(8,128)} %param.41) | copy-start | bytes 49156
  263.7 35.6 %copy-start.19 = (f32[2,16,16]{2,1,0:T(8,128)S(1)}, f32[2,16,16]{2,1,0:T(8,128)}, u32[]{:S(2)}) copy-start(f32[2,16,16]{2,1,0:T(8,128)} %param.42) | copy-start | bytes 6148
  434.3 4.3 copy-start.4
  439.6 23.3 %collective-permute-start.2 = (f32[16,50,1]{2,1,0:T(8,128)S(1)}, f32[16,50,1]{2,1,0:T(8,128)S(1)}, u32[]{:S(2)}, u32[]{:S(2)}) collective-permute-start(f32[16,50,1]{2,1,0:T(8,128)S(1)} %get-tuple-element.196), channel_id=1, source_target_pairs={{0,1},{1,2},{2,3},{3,4},{4,5},{5,6},{6,7},{7,8},{8,9},{9,10},{10,1... | collective-permute-start | bytes 9608 | tf_op jit(solution)/shard_map/ppermute | solution.py:12
  457.5 9.8 %collective-permute-start.3 = (f32[16,50,1]{2,1,0:T(8,128)S(1)}, f32[16,50,1]{2,1,0:T(8,128)S(1)}, u32[]{:S(2)}, u32[]{:S(2)}) collective-permute-start(f32[16,50,1]{2,1,0:T(8,128)S(1)} %get-tuple-element.197), channel_id=1, source_target_pairs={{1,0},{2,1},{3,2},{4,3},{5,4},{6,5},{7,6},{8,7},{9,8},{10,9},{11,1... | collective-permute-start | bytes 9608 | tf_op jit(solution)/shard_map/ppermute | solution.py:15
  480.9 7.6 %copy-start.1 = (f32[16,48,384]{2,1,0:T(8,128)S(1)}, f32[16,48,384]{2,1,0:T(8,128)}, u32[]{:S(2)}) copy-start(f32[16,48,384]{2,1,0:T(8,128)} %param.37) | copy-start | bytes 3538948
  488.5 1.3 copy-start
  491.0 40.3 %copy-start.10 = (f32[1,16,2048]{2,1,0:T(8,128)S(1)}, f32[1,16,2048]{2,1,0:T(8,128)}, u32[]{:S(2)}) copy-start(f32[1,16,2048]{2,1,0:T(8,128)} %get-tuple-element.214) | copy-start | bytes 393220
  491.1 16.7 %collective-permute-start.4 = (f32[16,3,384]{2,1,0:T(4,128)S(1)}, f32[16,3,384]{2,1,0:T(4,128)S(1)}, u32[]{:S(2)}, u32[]{:S(2)}) collective-permute-start(f32[16,3,384]{2,1,0:T(4,128)S(1)} %get-tuple-element.208), channel_id=1, source_target_pairs={{0,16},{16,32},{32,48},{48,64},{64,80},{80,96},{96,112},{112,128},... | collective-permute-start | bytes 221192 | tf_op jit(solution)/shard_map/ppermute | solution.py:12
  505.8 18.5 %collective-permute-start.5 = (f32[16,3,384]{2,1,0:T(4,128)S(1)}, f32[16,3,384]{2,1,0:T(4,128)S(1)}, u32[]{:S(2)}, u32[]{:S(2)}) collective-permute-start(f32[16,3,384]{2,1,0:T(4,128)S(1)} %get-tuple-element.209), channel_id=1, source_target_pairs={{16,0},{32,16},{48,32},{64,48},{80,64},{96,80},{112,96},{128,112},... | collective-permute-start | bytes 221192 | tf_op jit(solution)/shard_map/ppermute | solution.py:15
  507.7 24.0 %copy-start.17 = (s32[1024]{0:T(1024)S(1)}, s32[1024]{0:T(1024)}, u32[]{:S(2)}) copy-start(s32[1024]{0:T(1024)} %get-tuple-element.235) | copy-start | bytes 12292
  525.4 9.0 %copy-start.9 = (f32[1,16,2048]{2,1,0:T(8,128)S(1)}, f32[1,16,2048]{2,1,0:T(8,128)}, u32[]{:S(2)}) copy-start(f32[1,16,2048]{2,1,0:T(8,128)} %get-tuple-element.215) | copy-start | bytes 393220
  525.4 15.4 %collective-permute-start.6 = (f32[16,54,3]{2,1,0:T(8,128)}, f32[16,54,3]{2,1,0:T(8,128)S(1)}, u32[]{:S(2)}, u32[]{:S(2)}) collective-permute-start(f32[16,54,3]{2,1,0:T(8,128)} %get-tuple-element.191), channel_id=1, source_target_pairs={{0,1},{1,2},{2,3},{3,4},{4,5},{5,6},{6,7},{7,8},{8,9},{9,10},{10,1... | collective-permute-start | bytes 31112 | tf_op jit(solution)/shard_map/ppermute | solution.py:12
  529.4 11.4 %collective-permute-start.7 = (f32[16,54,3]{2,1,0:T(8,128)}, f32[16,54,3]{2,1,0:T(8,128)}, u32[]{:S(2)}, u32[]{:S(2)}) collective-permute-start(f32[16,54,3]{2,1,0:T(8,128)} %get-tuple-element.190), channel_id=1, source_target_pairs={{1,0},{2,1},{3,2},{4,3},{5,4},{6,5},{7,6},{8,7},{9,8},{10,9},{11,1... | collective-permute-start | bytes 31112 | tf_op jit(solution)/shard_map/ppermute | solution.py:15
  540.8 0.8 copy-start.11
  541.6 8.2 %copy-start.8 = (f32[1,1,16,384]{2,1,0,3:T(1,128)S(1)}, f32[1,1,16,384]{2,1,0,3:T(1,128)}, u32[]{:S(2)}) copy-start(f32[1,1,16,384]{2,1,0,3:T(1,128)} %get-tuple-element.201) | copy-start | bytes 73732
  541.6 8.4 %copy-start.7 = (f32[1,1,16,384]{2,1,0,3:T(1,128)S(1)}, f32[1,1,16,384]{2,1,0,3:T(1,128)}, u32[]{:S(2)}) copy-start(f32[1,1,16,384]{2,1,0,3:T(1,128)} %get-tuple-element.200) | copy-start | bytes 73732
  541.6 8.5 %copy-start.15 = (f32[1,1,16,48]{2,1,0,3:T(1,128)S(1)}, f32[1,1,16,48]{2,1,0,3:T(1,128)}, u32[]{:S(2)}) copy-start(f32[1,1,16,48]{2,1,0,3:T(1,128)} %get-tuple-element.219) | copy-start | bytes 9220
  541.6 9.6 %copy-start.14 = (f32[1,1,16,48]{2,1,0,3:T(1,128)S(1)}, f32[1,1,16,48]{2,1,0,3:T(1,128)}, u32[]{:S(2)}) copy-start(f32[1,1,16,48]{2,1,0,3:T(1,128)} %get-tuple-element.218) | copy-start | bytes 9220
  544.6 7.8 %collective-permute-start.8 = (f32[16,1,384]{2,1,0:T(1,128)S(1)}, f32[16,1,384]{2,1,0:T(1,128)S(1)}, u32[]{:S(2)}, u32[]{:S(2)}) collective-permute-start(f32[16,1,384]{2,1,0:T(1,128)S(1)} %get-tuple-element.206), channel_id=1, source_target_pairs={{0,16},{16,32},{32,48},{48,64},{64,80},{80,96},{96,112},{112,128},... | collective-permute-start | bytes 73736 | tf_op jit(solution)/shard_map/ppermute | solution.py:12
  546.5 17.6 %collective-permute-start.9 = (f32[16,1,384]{2,1,0:T(1,128)S(1)}, f32[16,1,384]{2,1,0:T(1,128)S(1)}, u32[]{:S(2)}, u32[]{:S(2)}) collective-permute-start(f32[16,1,384]{2,1,0:T(1,128)S(1)} %get-tuple-element.207), channel_id=1, source_target_pairs={{16,0},{32,16},{48,32},{64,48},{80,64},{96,80},{112,96},{128,112},... | collective-permute-start | bytes 73736 | tf_op jit(solution)/shard_map/ppermute | solution.py:15
  564.4 10.1 %collective-permute-start.10 = (f32[16,50,1]{2,1,0:T(8,128)S(1)}, f32[16,50,1]{2,1,0:T(8,128)S(1)}, u32[]{:S(2)}, u32[]{:S(2)}) collective-permute-start(f32[16,50,1]{2,1,0:T(8,128)S(1)} %get-tuple-element.194), channel_id=1, source_target_pairs={{0,1},{1,2},{2,3},{3,4},{4,5},{5,6},{6,7},{7,8},{8,9},{9,10},{10,1... | collective-permute-start | bytes 9608 | tf_op jit(solution)/shard_map/ppermute | solution.py:12
  569.0 9.8 %collective-permute-start.11 = (f32[16,50,1]{2,1,0:T(8,128)S(1)}, f32[16,50,1]{2,1,0:T(8,128)S(1)}, u32[]{:S(2)}, u32[]{:S(2)}) collective-permute-start(f32[16,50,1]{2,1,0:T(8,128)S(1)} %get-tuple-element.195), channel_id=1, source_target_pairs={{1,0},{2,1},{3,2},{4,3},{5,4},{6,5},{7,6},{8,7},{9,8},{10,9},{11,1... | collective-permute-start | bytes 9608 | tf_op jit(solution)/shard_map/ppermute | solution.py:15
  591.7 7.6 %copy-start.2 = (f32[16,48,384]{2,1,0:T(8,128)S(1)}, f32[16,48,384]{2,1,0:T(8,128)}, u32[]{:S(2)}) copy-start(f32[16,48,384]{2,1,0:T(8,128)} %param.37) | copy-start | bytes 3538948
  601.3 5.9 copy-start.6
  601.3 6.0 copy-start.5
  601.4 6.0 copy-start.13
  601.4 7.1 %copy-start.12 = (f32[1,1,16,48]{2,1,0,3:T(1,128)S(1)}, f32[1,1,16,48]{2,1,0,3:T(1,128)}, u32[]{:S(2)}) copy-start(f32[1,1,16,48]{2,1,0,3:T(1,128)} %get-tuple-element.216) | copy-start | bytes 9220
  601.8 28.7 %copy-start.3 = (f32[16,48,384]{2,1,0:T(8,128)}, f32[16,48,384]{2,1,0:T(8,128)S(1)}, u32[]{:S(2)}) copy-start(f32[16,48,384]{2,1,0:T(8,128)S(1)} %constant_dynamic-update-slice_fusion.16) | copy-start | bytes 3538948
  601.8 7.8 %collective-permute-start.12 = (f32[16,1,384]{2,1,0:T(1,128)S(1)}, f32[16,1,384]{2,1,0:T(1,128)S(1)}, u32[]{:S(2)}, u32[]{:S(2)}) collective-permute-start(f32[16,1,384]{2,1,0:T(1,128)S(1)} %get-tuple-element.204), channel_id=1, source_target_pairs={{0,16},{16,32},{32,48},{48,64},{64,80},{80,96},{96,112},{112,128},... | collective-permute-start | bytes 73736 | tf_op jit(solution)/shard_map/ppermute | solution.py:12
  604.2 17.6 %collective-permute-start.13 = (f32[16,1,384]{2,1,0:T(1,128)S(1)}, f32[16,1,384]{2,1,0:T(1,128)S(1)}, u32[]{:S(2)}, u32[]{:S(2)}) collective-permute-start(f32[16,1,384]{2,1,0:T(1,128)S(1)} %get-tuple-element.205), channel_id=1, source_target_pairs={{16,0},{32,16},{48,32},{64,48},{80,64},{96,80},{112,96},{128,112},... | collective-permute-start | bytes 73736 | tf_op jit(solution)/shard_map/ppermute | solution.py:15
  622.0 8.4 %collective-permute-start.14 = (f32[16,50,1]{2,1,0:T(8,128)S(1)}, f32[16,50,1]{2,1,0:T(8,128)S(1)}, u32[]{:S(2)}, u32[]{:S(2)}) collective-permute-start(f32[16,50,1]{2,1,0:T(8,128)S(1)} %get-tuple-element.192), channel_id=1, source_target_pairs={{0,1},{1,2},{2,3},{3,4},{4,5},{5,6},{6,7},{7,8},{8,9},{9,10},{10,1... | collective-permute-start | bytes 9608 | tf_op jit(solution)/shard_map/ppermute | solution.py:12
  625.1 9.8 %collective-permute-start.15 = (f32[16,50,1]{2,1,0:T(8,128)S(1)}, f32[16,50,1]{2,1,0:T(8,128)S(1)}, u32[]{:S(2)}, u32[]{:S(2)}) collective-permute-start(f32[16,50,1]{2,1,0:T(8,128)S(1)} %get-tuple-element.193), channel_id=1, source_target_pairs={{1,0},{2,1},{3,2},{4,3},{5,4},{6,5},{7,6},{8,7},{9,8},{10,9},{11,1... | collective-permute-start | bytes 9608 | tf_op jit(solution)/shard_map/ppermute | solution.py:15
  659.4 1.0 copy-start.21
where the time goes:
time: 663 us; the launch traced here: 661 us
  blocking collectives  395 us (60%)
  local copies, waits for them, and re-layouts  93.3 us (14%)
  starting transfers between devices  82.1 us (12%)
  waiting for transfers between devices  62.7 us (9%)
  other arithmetic  25.7 us (4%)
    all_gather x1, blocking collectives, on_device(): lax.all_gather(rows_sn, 'nx', axis=3, tiled=True)  155 us
    all_gather x1, blocking collectives, on_device(): lax.all_gather(fill_sn, 'nx', axis=2, tiled=True)  135 us
    all_gather x1, blocking collectives, on_device(): lax.all_gather(rows_we, 'ny', axis=3, tiled=True)  74.8 us
    ppermute x8, starting transfers between devices, with_halo(): lax.ppermute(lax.slice_in_dim(block, block.shape[dim] - width, None, axis...  63.6 us
    ppermute x8, waiting for transfers between devices, with_halo(): lax.ppermute(lax.slice_in_dim(block, 0, width, axis=dim), axis, backward)  53.7 us
    all_gather x1, blocking collectives, on_device(): lax.all_gather(fill_we, 'ny', axis=2, tiled=True)  30.5 us
    scatter x3, local copies, waits for them, and re-layouts, advance(): padded.at[:, 1:-1, -1]  20 us
    ppermute x8, starting transfers between devices, with_halo(): lax.ppermute(lax.slice_in_dim(block, 0, width, axis=dim), axis, backward)  18.5 us
  transfers between devices with their start and end apart: 16, of which 9 were waited for; matrix products, arithmetic and copies ran while one was open for 6% of the time, Pallas kernels for 0%

commit v1 on v0

v1 whole, which is shorter than its diff:
```python
import functools

import jax
import jax.numpy as jnp
from jax import lax
from jax.experimental import pallas as pl
from jax.experimental.pallas import tpu as pltpu
from jax.sharding import PartitionSpec as P

LV = 16
WX = 48
WY = 384
NG = WY // 128
HX = 8
STATE_ROWS = 6
COEF_ROWS = 5
COEF_AT = LV * STATE_ROWS
VERT_AT = COEF_AT + LV * COEF_ROWS
XROWS = 184


def rounds_of(count):
    if count == 32:
        return [[16], [4, 8, 12], [1, 2, 3]]
    if count == 16:
        return [[8], [2, 4, 6], [1]]
    masks, bit = [], count // 2
    while bit:
        masks.append([bit])
        bit //= 2
    return masks


def masks_of(count):
    have = [0]
    for masks in rounds_of(count):
        have = [m ^ h for m in [0] + masks for h in have]
    return have


def pack_kernel(place, state, diffuse, vertical, filler, interp, xa, xb, y_low, y_high):
    def rows(ref, high):
        at = WX - STATE_ROWS if high else 0
        bt = WX - COEF_ROWS if high else 0
        for l in range(NG):
            lanes = slice(128 * l, 128 * l + 128)
            for k in range(LV):
                ref[l, k * STATE_ROWS : (k + 1) * STATE_ROWS, :] = state[k, at : at + STATE_ROWS, lanes]
                ref[l, COEF_AT + k * COEF_ROWS : COEF_AT + (k + 1) * COEF_ROWS, :] = diffuse[
                    k, bt : bt + COEF_ROWS, lanes
                ]
            ref[l, VERT_AT : VERT_AT + COEF_ROWS, :] = vertical[bt : bt + COEF_ROWS, lanes]
            ref[l, VERT_AT + COEF_ROWS :, :] = jnp.zeros((XROWS - VERT_AT - COEF_ROWS, 128), jnp.float32)

    odd = place[2] % 2 == 1

    @pl.when(odd)
    def _():
        rows(xa, True)
        rows(xb, False)

    @pl.when(jnp.logical_not(odd))
    def _():
        rows(xa, False)
        rows(xb, True)

    lane = lax.broadcasted_iota(jnp.int32, (WX, 128), 1)
    row = lax.broadcasted_iota(jnp.int32, (WX, 128), 0)
    for ref, group, first in ((y_low, 0, 0), (y_high, NG - 1, 120)):
        lanes = slice(128 * group, 128 * group + 128)
        for which, field in enumerate((state, diffuse)):
            total = jnp.zeros((WX, 128), jnp.float32)
            for k in range(LV):
                part = pltpu.roll(field[k, :, lanes], (8 * k - first) % 128, 1)
                total = jnp.where((lane >= 8 * k) & (lane < 8 * k + 8), part, total)
            ref[:, 128 * which : 128 * which + 128] = total
        last = jnp.where(lane < 8, pltpu.roll(vertical[:, lanes], (-first) % 128, 1), 0.0)
        src = filler[:, 0:128]
        last = jnp.where(
            (lane >= 8) & (lane < 16), pltpu.roll(src, (8 - first) % 128, 1), last
        )
        pair = jnp.where(row == 0, interp[0:1, lanes], interp[1:2, lanes])
        last = jnp.where(
            (lane >= 16) & (lane < 24) & (row < 2), pltpu.roll(pair, (16 - first) % 128, 1), last
        )
        ref[:, 256:384] = last


def main_kernel(
    count_x, count_y, masks_y, place, state, diffuse, vertical, ra, rb, from_low, from_high, ca, cb,
    colpack, interp, chain_y, chain_x, colid, filler, out, es, ed, ev, mv, gv, fac, strip, ey, ex, pack, sem,
):
    dx, dy, nx, ny = place[0], place[1], place[2], place[3]
    copies = []
    for which, (src, dst) in enumerate(((state, es), (diffuse, ed))):
        for l in range(NG):
            copy = pltpu.make_async_copy(
                src.at[:, :, pl.ds(128 * l, 128)], dst.at[:, l, pl.ds(HX, WX), :], sem.at[NG * which + l]
            )
            copy.start()
            copies.append(copy)
    odd = nx % 2 == 1
    lane = lax.broadcasted_iota(jnp.int32, (8, 128), 1)
    lane64 = lax.broadcasted_iota(jnp.int32, (64, 128), 1)

    def beyond(at, size, l):
        a, b = ra[l, at : at + size, :], rb[l, at : at + size, :]
        return jnp.where(odd, b, a), jnp.where(odd, a, b)

    for l in range(NG):
        for k in range(LV):
            low, high = beyond(k * STATE_ROWS, STATE_ROWS, l)
            es[k, l, HX - STATE_ROWS : HX, :] = low
            es[k, l, HX + WX : HX + WX + STATE_ROWS, :] = high
            low, high = beyond(COEF_AT + k * COEF_ROWS, COEF_ROWS, l)
            ed[k, l, HX - COEF_ROWS : HX, :] = low
            ed[k, l, HX + WX : HX + WX + COEF_ROWS, :] = high
        low, high = beyond(VERT_AT, COEF_ROWS, l)
        ev[l, HX - COEF_ROWS : HX, :] = low
        ev[l, HX + WX : HX + WX + COEF_ROWS, :] = high
        ev[l, HX : HX + WX, :] = vertical[:, 128 * l : 128 * l + 128]

    low = jnp.where(odd, cb[...], ca[...])
    high = jnp.where(odd, ca[...], cb[...])
    for side, ref in enumerate((from_low, from_high)):
        strip[side, 0:HX, :] = low[8 * side : 8 * side + 8]
        strip[side, HX : HX + WX, :] = ref[...]
        strip[side, HX + WX : 64, :] = high[8 * side : 8 * side + 8]
    pack[0:HX, :] = low[0:8, 256:384]
    pack[HX : HX + WX, :] = colpack[...]
    pack[HX + WX : 64, :] = high[0:8, 256:384]
    for which, dst in enumerate((es, ed)):
        lanes = slice(128 * which, 128 * which + 128)
        for k in range(LV):
            dst[k, NG, 0:64, :] = jnp.where(
                lane64 < 64,
                pltpu.roll(strip[1, :, lanes], (-8 * k) % 128, 1),
                pltpu.roll(strip[0, :, lanes], (120 - 8 * k) % 128, 1),
            )
    ev[NG, 0:64, :] = jnp.where(
        lane64 < 64, strip[1, :, 256:384], pltpu.roll(strip[0, :, 256:384], 120, 1)
    )

    west, east = nx == 0, nx == count_x - 1
    south, north = ny == 0, ny == count_y - 1

    @pl.when(west | east)
    def _():
        lane1 = lax.broadcasted_iota(jnp.int32, (1, 128), 1)
        for l in range(NG + 1):
            got = []
            for item in range(2):
                if l < NG:
                    got.append(interp[item : item + 1, 128 * l : 128 * l + 128])
                else:
                    got.append(
                        jnp.where(
                            lane1 < 64,
                            pltpu.roll(strip[1, HX : HX + 8, 256:384], 112, 1)[item : item + 1],
                            pltpu.roll(strip[0, HX : HX + 8, 256:384], 104, 1)[item : item + 1],
                        )
                    )
            index = jnp.broadcast_to(got[0], (48, 128)).astype(jnp.int32)
            ends = []
            for offset in range(2):
                at = index + offset
                block, inside = at >> 7, at & 127
                total = jnp.zeros((48, 128), jnp.float32)
                for piece, mask in enumerate(masks_y):
                    value = jnp.take_along_axis(chain_y[piece], inside, axis=1, mode="promise_in_bounds")
                    total = jnp.where(block == (ny ^ mask), value, total)
                ends.append(total)
            ey[l] = (1.0 - got[1]) * ends[0] + got[1] * ends[1]

    @pl.when(south | north)
    def _():
        index = pack[:, 64:65].astype(jnp.int32)
        weight = pack[:, 65:66]
        ids = colid[0:1, :]
        spread = jnp.where(ids == index, 1.0 - weight, 0.0) + jnp.where(ids == index + 1, weight, 0.0)
        ex[0:64, :] = jnp.dot(
            spread, chain_x[...], preferred_element_type=jnp.float32, precision=lax.Precision.HIGHEST
        )

    def ghosts(field, step, row_low, row_high, shift):
        @pl.when(west)
        def _():
            for k in range(LV):
                for l in range(NG + 1):
                    field[k, l, row_low : row_low + 1, :] = ey[l, 16 * step + k : 16 * step + k + 1, :]

        @pl.when(east)
        def _():
            for k in range(LV):
                for l in range(NG + 1):
                    field[k, l, row_high : row_high + 1, :] = ey[l, 16 * step + k : 16 * step + k + 1, :]

        @pl.when(south | north)
        def _():
            at = jnp.where(south, 127, 0)
            lanes = lax.broadcasted_iota(jnp.int32, (56, 128), 1)
            for k in range(LV):
                col = ex[shift : shift + 56, 16 * step + k : 16 * step + k + 1]
                field[k, NG, 0:56, :] = jnp.where(lanes == at, col, field[k, NG, 0:56, :])

    def ghost_tail(step):
        @pl.when(south | north)
        def _():
            at = jnp.where(south, 127, 0)
            for k in range(LV):
                col = ex[56:64, 16 * step + k : 16 * step + k + 1]
                es[k, NG, 56:64, :] = jnp.where(lane == at, col, es[k, NG, 56:64, :])

    for copy in copies:
        copy.wait()
    ghosts(es, 0, HX - 1, HX + WX, 0)
    ghost_tail(0)

    def sideways(c):
        lefts = [pltpu.roll(x, 1, 1) for x in c]
        rights = [pltpu.roll(x, 127, 1) for x in c]
        n = len(c)
        left = [jnp.where(lane == 0, lefts[l - 1], lefts[l]) for l in range(n)]
        right = [jnp.where(lane == 127, rights[(l + 1) % n], rights[l]) for l in range(n)]
        return left, right

    def advance(field, at, coef_at, groups, write_source, read_source, write):
        g = [ev[l, pl.ds(coef_at, 8), :] for l in range(groups)]
        factor, source = [None] * groups, [None] * groups
        for k in range(LV):
            c = [field[k, l, pl.ds(at, 8), :] for l in range(NG + 1)]
            left, right = sideways(c)
            for l in range(groups):
                lap = (
                    field[k, l, pl.ds(at + 1, 8), :]
                    + field[k, l, pl.ds(at - 1, 8), :]
                    + right[l]
                    + left[l]
                    - 4.0 * c[l]
                )
                explicit = c[l] + ed[k, l, pl.ds(coef_at, 8), :] * lap
                diagonal = 1.0 + (g[l] if k in (0, LV - 1) else 2.0 * g[l])
                if k > 0:
                    diagonal = diagonal + g[l] * factor[l]
                    explicit = explicit + g[l] * source[l]
                inverse = 1.0 / diagonal
                factor[l] = -g[l] * inverse
                source[l] = explicit * inverse
                fac[k, l] = factor[l]
                if k < LV - 1:
                    write_source(k, l, source[l])
        value = source
        write(LV - 1, value)
        for k in range(LV - 2, -1, -1):
            value = [read_source(k, l) - fac[k, l] * value[l] for l in range(groups)]
            write(k, value)

    turn = (128 - 3 * dy) % 128

    @pl.loop(0, 7)
    def _(t):
        to = pl.multiple_of(8 * t, 8)

        def put(k, l, x):
            mv[k, l, pl.ds(to, 8), :] = x

        def take(k, l):
            return mv[k, l, pl.ds(to, 8), :]

        def moved(k, values):
            turned = [pltpu.roll(x, turn, 1) for x in values]
            for l in range(NG + 1):
                x = jnp.where(lane >= 128 - 3 * dy, turned[(l + 1) % (NG + 1)], turned[l])
                put(k, l, jnp.where(lane < -3 * dy, turned[l - 1], x))

        at = HX - 2 + 3 * dx + 8 * t
        advance(es, at, at, NG + 1, put, take, moved)

    @pl.when((south & (dy < 0)) | (north & (dy > 0)))
    def _():
        row = lax.broadcasted_iota(jnp.int32, (56, 128), 0)
        cell = (((row + 4) * 21846) >> 16) - 2 + dx
        lanes = lax.broadcasted_iota(jnp.int32, (56, 128), 1)
        total = jnp.zeros((56, 128), jnp.float32)
        for q in range(-2, 18):
            r = q + 8 if q < 0 else (q + HX if q < 8 else q + 40)
            total = jnp.where(cell == q, pack[r : r + 1, :], total)

        for is_side, side, l, first in ((south, 0, 0, 0), (north, 1, NG - 1, 125)):

            @pl.when(is_side)
            def _():
                inside = (lanes >= first) & (lanes < first + 3)
                for k in range(LV):
                    n = 96 + 16 * side + k
                    mv[k, l, 0:56, :] = jnp.where(inside, total[:, n : n + 1], mv[k, l, 0:56, :])

    @pl.when((west & (dx < 0)) | (east & (dx > 0)))
    def _():
        lane16 = lax.broadcasted_iota(jnp.int32, (16, 128), 1)
        for is_side, side, first in ((west, 0, 2), (east, 1, 47)):

            @pl.when(is_side)
            def _():
                rows = slice(16 * side, 16 * side + 16)
                own = filler[rows, :]
                ring = jnp.where(
                    lane16 < 64,
                    pltpu.roll(strip[1, HX + 16 * side : HX + 16 * side + 16, 256:384], 120, 1),
                    pltpu.roll(strip[0, HX + 16 * side : HX + 16 * side + 16, 256:384], 112, 1),
                )
                for l in range(NG + 1):
                    column = lane16 + 128 * l
                    if l == NG:
                        column = jnp.where(lane16 < 64, column, lane16 - 128)
                    cell = (((column + 384) * 21846) >> 16) - 128 + dy
                    cell = jnp.clip(cell, -128 * ny, 128 * (count_y - ny) - 1)
                    inside = cell & 127
                    a = jnp.take_along_axis(own, inside, axis=1, mode="promise_in_bounds")
                    b = jnp.take_along_axis(ring, inside, axis=1, mode="promise_in_bounds")
                    ey[l, 0:16, :] = jnp.where((cell >= 0) & (cell < 128), a, b)
                    for k in range(LV):
                        mv[k, l, first : first + 3, :] = jnp.broadcast_to(ey[l, k : k + 1, :], (3, 128))

    ghosts(mv, 1, 1, WX + 2, HX - 2)

    @pl.loop(0, 7)
    def _(t):
        to = pl.multiple_of(8 * t, 8)

        def put(k, l, x):
            gv[k, l, pl.ds(to, 8), :] = x

        def take(k, l):
            return gv[k, l, pl.ds(to, 8), :]

        def keep(k, values):
            for l in range(NG + 1):
                put(k, l, values[l])

        advance(mv, 1 + 8 * t, HX - 1 + 8 * t, NG + 1, put, take, keep)

    ghosts(gv, 2, 0, WX + 1, HX - 1)

    @pl.loop(0, 6)
    def _(t):
        to = pl.multiple_of(8 * t, 8)

        def put(k, l, x):
            out[k, pl.ds(to, 8), 128 * l : 128 * l + 128] = x

        def take(k, l):
            return out[k, pl.ds(to, 8), 128 * l : 128 * l + 128]

        def keep(k, values):
            for l in range(NG):
                put(k, l, values[l])

        advance(gv, 1 + 8 * t, HX + 8 * t, NG, put, take, keep)


def on_device(
    state,
    diffuse,
    vertical,
    rows_we,
    rows_sn,
    fill_we,
    fill_sn,
    index_we,
    weight_we,
    index_sn,
    weight_sn,
    jump,
):
    f32 = jnp.float32
    count_x, count_y = lax.axis_size("nx"), lax.axis_size("ny")
    nx, ny = lax.axis_index("nx"), lax.axis_index("ny")
    both = ("nx", "ny")
    place = jnp.stack([jump[0], jump[1], nx, ny]).astype(jnp.int32)
    odd = nx % 2

    filler = fill_we.reshape(32, 128)
    interp = jnp.stack([index_we.astype(f32), weight_we])
    interp = jnp.pad(interp, ((0, 6), (0, 0)))
    vmem = pl.BlockSpec(memory_space=pltpu.VMEM)
    smem = pl.BlockSpec(memory_space=pltpu.SMEM)
    xa, xb, y_low, y_high = pl.pallas_call(
        pack_kernel,
        out_shape=(
            jax.ShapeDtypeStruct((NG, XROWS, 128), f32),
            jax.ShapeDtypeStruct((NG, XROWS, 128), f32),
            jax.ShapeDtypeStruct((WX, WY), f32),
            jax.ShapeDtypeStruct((WX, WY), f32),
        ),
        in_specs=[smem] + [vmem] * 5,
        out_specs=(vmem,) * 4,
        compiler_params=pltpu.CompilerParams(vmem_limit_bytes=40 << 20),
        name="pack",
    )(place, state, diffuse, vertical, jnp.pad(filler, ((0, 16), (0, 0))), interp)

    pairs_a = [(i, i + 1) for i in range(1, count_x - 1, 2)]
    pairs_a += [(b, a) for a, b in pairs_a]
    pairs_b = [(i, i + 1) for i in range(0, count_x, 2)]
    pairs_b += [(b, a) for a, b in pairs_b]
    up = [(i, i + 1) for i in range(count_y - 1)]
    down = [(b, a) for a, b in up]
    ra = lax.ppermute(xa, "nx", pairs_a)

    chain_x = jnp.where(ny == 0, rows_sn[:, 0], rows_sn[:, 1]).reshape(48, 16)
    chain_x = jnp.pad(chain_x.T, ((0, 0), (0, 80)))[None]
    chain_y = jnp.where(nx == 0, rows_we[:, 0], rows_we[:, 1]).reshape(48, 128)[None]

    def grow(chain, masks, pairs):
        return jnp.concatenate([chain] + [lax.ppermute(chain, both, pairs(m)) for m in masks])

    def pairs_x(mask):
        return [(i * count_y + n, (i ^ mask) * count_y + n) for n in (0, count_y - 1) for i in range(count_x)]

    def pairs_y(mask):
        return [(n * count_y + j, n * count_y + (j ^ mask)) for n in (0, count_x - 1) for j in range(count_y)]

    rb = lax.ppermute(xb, "nx", pairs_b)
    from_low = lax.ppermute(y_high, "ny", up)
    from_high = lax.ppermute(y_low, "ny", down)
    for mx, my in zip(rounds_of(count_x), rounds_of(count_y), strict=True):
        chain_x = grow(chain_x, mx, pairs_x)
        chain_y = grow(chain_y, my, pairs_y)
    masks_x, masks_y = masks_of(count_x), masks_of(count_y)
    chain_x = chain_x.reshape(16 * count_x, 128)
    blocks = nx ^ jnp.array(masks_x, jnp.int32)
    colid = (blocks[:, None] * 16 + jnp.arange(16, dtype=jnp.int32)).reshape(1, -1)
    colid = jnp.broadcast_to(colid, (8, 16 * count_x))

    fill_t = fill_sn.reshape(32, 16).T
    fill_t = jnp.pad(fill_t.reshape(2, 8, 32), ((0, 0), (0, 32), (0, 0))).reshape(80, 32)[:WX]
    colpack = jnp.concatenate(
        [
            jnp.zeros((WX, 64), f32),
            index_sn.astype(f32)[:, None],
            weight_sn[:, None],
            jnp.zeros((WX, 30), f32),
            fill_t,
        ],
        axis=1,
    )

    def corner(start):
        low = lax.dynamic_slice(from_low, (start, 0), (8, WY))
        high = lax.dynamic_slice(from_high, (start, 0), (8, WY))
        own = jnp.pad(lax.dynamic_slice(colpack, (start, 0), (8, 128)), ((0, 0), (256, 0)))
        clear = lax.broadcasted_iota(jnp.int32, (8, WY), 1) < 256 + 64
        return jnp.concatenate([jnp.where(clear, low, own), high])

    ca = lax.ppermute(corner(40 * odd), "nx", pairs_a)
    cb = lax.ppermute(corner(40 - 40 * odd), "nx", pairs_b)

    any_ = pl.BlockSpec(memory_space=pl.ANY)
    return pl.pallas_call(
        functools.partial(main_kernel, count_x, count_y, masks_y),
        out_shape=jax.ShapeDtypeStruct((LV, WX, WY), f32),
        in_specs=[smem, any_, any_] + [vmem] * 13,
        out_specs=vmem,
        scratch_shapes=[
            pltpu.VMEM((LV, NG + 1, 72, 128), f32),
            pltpu.VMEM((LV, NG + 1, 72, 128), f32),
            pltpu.VMEM((NG + 1, 72, 128), f32),
            pltpu.VMEM((LV, NG + 1, 64, 128), f32),
            pltpu.VMEM((LV, NG + 1, 64, 128), f32),
            pltpu.VMEM((LV, NG + 1, 8, 128), f32),
            pltpu.VMEM((2, 64, WY), f32),
            pltpu.VMEM((NG + 1, 48, 128), f32),
            pltpu.VMEM((64, 128), f32),
            pltpu.VMEM((64, 128), f32),
            pltpu.SemaphoreType.DMA((2 * NG,)),
        ],
        compiler_params=pltpu.CompilerParams(vmem_limit_bytes=48 << 20),
        name="steps",
    )(
        place, state, diffuse, vertical, ra, rb, from_low, from_high, ca, cb,
        colpack, interp, chain_y, chain_x, colid, filler,
    )


def solution(mesh):
    return jax.shard_map(
        on_device,
        mesh=mesh,
        in_specs=(
            P(None, "nx", "ny"),
            P(None, "nx", "ny"),
            P("nx", "ny"),
            P(None, None, None, "ny"),
            P(None, None, None, "nx"),
            P(None, None, "ny"),
            P(None, None, "nx"),
            P("ny"),
            P("ny"),
            P("nx"),
            P("nx"),
            P(),
        ),
        out_specs=P(None, "nx", "ny"),
        check_vma=False,
    )
```

time: 663 us -> 125 us (0.19)
  the two profiles are of different devices: /device:TPU:31 before, /device:TPU:1 now
where the time goes in v1:
time: 125 us; the launch traced here: 124 us
  starting transfers between devices  73.3 us (59%)
  local copies, waits for them, and re-layouts  24.1 us (19%)
  Pallas kernels  11.3 us (9%)
  other arithmetic  8.58 us (7%)
  waiting for transfers between devices  6.35 us (5%)
    ppermute x12, starting transfers between devices, grow(): lax.ppermute(chain, both, pairs(m))  53.7 us
    unnamed x36, local copies, waits for them, and re-layouts  12.7 us
    pallas_call x1, Pallas kernels, on_device(): pl.pallas_call(functools.partial(main_kernel, count_x, count_y, masks_y),...  9.51 us
    ppermute x1, starting transfers between devices, on_device(): from_high = lax.ppermute(y_low, 'ny', down)  7.08 us
    ppermute x1, starting transfers between devices, on_device(): rb = lax.ppermute(xb, 'nx', pairs_b)  4.88 us
    ppermute x1, starting transfers between devices, on_device(): from_low = lax.ppermute(y_high, 'ny', up)  4.37 us
    ppermute x12, waiting for transfers between devices, grow(): lax.ppermute(chain, both, pairs(m))  3.75 us
    ppermute x1, waiting for transfers between devices, on_device(): cb = lax.ppermute(corner(40 - 40 * odd), 'nx', pairs_b)  2.58 us
  transfers between devices with their start and end apart: 18, of which 4 were waited for; matrix products, arithmetic and copies ran while one was open for 20% of the time, Pallas kernels for 1%

profile of v1, /device:TPU:1, one launch (start us, length us, event | category | flops | bytes accessed | tf_op | source)
XLA Modules:
  0.0 124.0 jit_solution(4121737221489834589)
XLA Ops:
  0.0 0.8 slice_select_fusion
  1.4 1.2 %collective-permute-start.11 = (f32[1,16,128]{2,1,0:T(8,128)}, f32[1,16,128]{2,1,0:T(8,128)}, u32[]{:S(2)}, u32[]{:S(2)}) collective-permute-start(f32[1,16,128]{2,1,0:T(8,128)} %pad_bitcast_fusion), channel_id=1, source_target_pairs={{0,256},{16,272},{32,288},{48,304},{64,320},{80,336},{96,352},{112... | collective-permute-start | bytes 24584 | tf_op jit(solution)/shard_map/ppermute | solution.py:415
  2.7 1.4 %slice_select_fusion.1 = f32[3,1,16,128]{3,2,1,0:T(8,128)} fusion(f32[3,2,16,128]{3,2,1,0:T(8,128)} %param.16, pred[]{:T(512)S(6)} %eq.8), kind=kLoop, calls=%fused_computation.28 | loop fusion | flops 6144 | bytes 73729 | tf_op jit(solution)/shard_map/jit(_where)/select_n | solution.py:412
  4.1 9.6 %collective-permute-start.6 = (f32[1,48,128]{2,1,0:T(8,128)}, f32[1,48,128]{2,1,0:T(8,128)}, u32[]{:S(2)}, u32[]{:S(2)}) collective-permute-start(f32[1,48,128]{2,1,0:T(8,128)} %bitcast.9), channel_id=1, source_target_pairs={{0,8},{1,9},{2,10},{3,11},{4,12},{5,13},{6,14},{7,15},{8,0},{9,1},... | collective-permute-start | bytes 73736 | tf_op jit(solution)/shard_map/ppermute | solution.py:415
  13.7 0.7 stack.22
  14.4 0.7 convert_element_type.17
  15.1 0.7 pad.23.filler
  15.8 0.7 pad_add_fusion.place
  16.5 1.3 %copy-done = f32[16,48,384]{2,1,0:T(8,128)S(1)} copy-done((f32[16,48,384]{2,1,0:T(8,128)S(1)}, f32[16,48,384]{2,1,0:T(8,128)}, u32[]{:S(2)}) %copy-start) | copy-done | bytes 1179672
  17.8 1.3 %copy-done.2 = f32[16,48,384]{2,1,0:T(8,128)S(1)} copy-done((f32[16,48,384]{2,1,0:T(8,128)S(1)}, f32[16,48,384]{2,1,0:T(8,128)}, u32[]{:S(2)}) %copy-start.2) | copy-done | bytes 1179672
  19.1 0.9 copy-done.4
  20.0 1.8 %pack.1 = (f32[3,184,128]{2,1,0:T(8,128)}, f32[3,184,128]{2,1,0:T(8,128)S(1)}, f32[48,384]{1,0:T(8,128)}, f32[48,384]{1,0:T(8,128)}) custom-call(s32[4]{0:T(128)S(1)} %pad_add_fusion.place, f32[16,48,384]{2,1,0:T(8,128)S(1)} %copy-done, f32[16,48,384]{2,1,0:T(8,128)S(1)} %copy-done.2, f32[48,384]{1,0:T(8,128)S(1)} %copy-done.4, f32[48,128]{1,0:T(8,128)S(1)} %pad.23.filler, ...), custom_call_target="tpu_custom_call" | custom-call | tf_op jit(solution)/shard_map/pack/pallas_call | solution.py:388
  21.7 0.7 copy-done.9
  22.5 4.4 %collective-permute-start.2 = (f32[48,384]{1,0:T(8,128)}, f32[48,384]{1,0:T(8,128)S(1)}, u32[]{:S(2)}, u32[]{:S(2)}) collective-permute-start(f32[48,384]{1,0:T(8,128)} %get-tuple-element.11), channel_id=1, source_target_pairs={{0,1},{1,2},{2,3},{3,4},{4,5},{5,6},{6,7},{7,8},{8,9},{9,10},{10,1... | collective-permute-start | bytes 221192 | tf_op jit(solution)/shard_map/ppermute | solution.py:424
  26.8 7.1 %collective-permute-start.3 = (f32[48,384]{1,0:T(8,128)}, f32[48,384]{1,0:T(8,128)S(1)}, u32[]{:S(2)}, u32[]{:S(2)}) collective-permute-start(f32[48,384]{1,0:T(8,128)} %get-tuple-element.12), channel_id=1, source_target_pairs={{1,0},{2,1},{3,2},{4,3},{5,4},{6,5},{7,6},{8,7},{9,8},{10,9},{11,1... | collective-permute-start | bytes 221192 | tf_op jit(solution)/shard_map/ppermute | solution.py:425
  33.9 0.7 collective-permute-start
  35.2 1.4 %constant_dynamic-update-slice_fusion.4 = (f32[8,48,128]{2,1,0:T(8,128)}, f32[16,48,128]{2,1,0:T(8,128)S(1)}) fusion(f32[1,48,128]{2,1,0:T(8,128)} %bitcast.9), kind=kLoop, calls=%fused_computation.4 | loop fusion | bytes 73728
  37.8 1.3 %iota_add_fusion = s32[32,16]{1,0:T(8,128)} fusion(s32[32]{0:T(128)} %xor_multiply_fusion), kind=kLoop, calls=%fused_computation.30 | loop fusion | flops 512 | bytes 2176 | tf_op jit(solution)/shard_map/add | solution.py:432
  39.0 1.3 %copy.19 = f32[48,1]{1,0:T(8,128)} copy(f32[48,1]{0,1:T(1,128)} %convert_bitcast_fusion) | data formatting | bytes 384 | tf_op jit(solution)/shard_map/broadcast_in_dim | solution.py:440
  40.3 1.3 %copy.20 = f32[48,1]{1,0:T(8,128)} copy(f32[48,1]{0,1:T(1,128)} %bitcast.30) | data formatting | bytes 384 | tf_op jit(solution)/shard_map/broadcast_in_dim | solution.py:441
  43.5 0.9 concatenate.31.colpack
  45.6 1.4 %add.53 = s32[512]{0:T(512)} reshape(s32[32,16]{1,0:T(8,128)} %iota_add_fusion) | data formatting | bytes 4096 | tf_op jit(solution)/shard_map/add | solution.py:432
  47.0 0.7 pad_maximum_fusion.3
  47.7 0.7 collective-permute-start.12
  48.3 1.3 %constant_dynamic-update-slice_fusion.14 = (f32[8,16,128]{2,1,0:T(8,128)}, f32[32,16,128]{2,1,0:T(8,128)S(1)}) fusion(f32[8,16,128]{2,1,0:T(8,128)} %get-tuple-element.37, f32[1,16,128]{2,1,0:T(8,128)} %collective-permute-done.11, f32[32,16,128]{2,1,0:T(8,128)S(1)} %get-tuple-element.38), kind=kLoop, calls=%fused_computation.14 | loop fusion | bytes 24576
  49.6 0.7 collective-permute-start.13
  50.9 0.7 collective-permute-start.14
  52.2 4.9 %collective-permute-start.1 = (f32[3,184,128]{2,1,0:T(8,128)}, f32[3,184,128]{2,1,0:T(8,128)S(1)}, u32[]{:S(2)}, u32[]{:S(2)}) collective-permute-start(f32[3,184,128]{2,1,0:T(8,128)} %copy-done.9), channel_id=1, source_target_pairs={{0,16},{32,48},{64,80},{96,112},{128,144},{160,176},{192,208},{224... | collective-permute-start | bytes 847880 | tf_op jit(solution)/shard_map/ppermute | solution.py:423
  57.7 0.8 pad_maximum_fusion
  58.4 1.9 %collective-permute-start.7 = (f32[2,48,128]{2,1,0:T(8,128)S(1)}, f32[2,48,128]{2,1,0:T(8,128)S(1)}, u32[]{:S(2)}, u32[]{:S(2)}) collective-permute-start(f32[2,48,128]{2,1,0:T(8,128)S(1)} %pad_maximum_fusion), channel_id=1, source_target_pairs={{0,2},{1,3},{2,0},{3,1},{4,6},{5,7},{6,4},{7,5},{8,10},{9,11},{10,... | collective-permute-start | bytes 147464 | tf_op jit(solution)/shard_map/ppermute | solution.py:415
  60.3 1.3 %constant_dynamic-update-slice_fusion.3 = (f32[8,48,128]{2,1,0:T(8,128)}, f32[16,48,128]{2,1,0:T(8,128)S(1)}) fusion(f32[8,48,128]{2,1,0:T(8,128)} %get-tuple-element.25, f32[1,48,128]{2,1,0:T(8,128)} %collective-permute-done.6, f32[16,48,128]{2,1,0:T(8,128)S(1)} %get-tuple-element.26), kind=kLoop, calls=%fused_computation.3 | loop fusion | bytes 73728
  61.7 2.1 %collective-permute-done.7 = f32[2,48,128]{2,1,0:T(8,128)S(1)} collective-permute-done((f32[2,48,128]{2,1,0:T(8,128)S(1)}, f32[2,48,128]{2,1,0:T(8,128)S(1)}, u32[]{:S(2)}, u32[]{:S(2)}) %collective-permute-start.7) | collective-permute-done | bytes 49184 | tf_op jit(solution)/shard_map/ppermute | solution.py:415
  63.7 4.5 %collective-permute-start.8 = (f32[2,48,128]{2,1,0:T(8,128)S(1)}, f32[2,48,128]{2,1,0:T(8,128)S(1)}, u32[]{:S(2)}, u32[]{:S(2)}) collective-permute-start(f32[2,48,128]{2,1,0:T(8,128)S(1)} %pad_maximum_fusion), channel_id=1, source_target_pairs={{0,4},{1,5},{2,6},{3,7},{4,0},{5,1},{6,2},{7,3},{8,12},{9,13},{10,... | collective-permute-start | bytes 147464 | tf_op jit(solution)/shard_map/ppermute | solution.py:415
  68.9 0.8 collective-permute-done.8
  69.7 0.7 collective-permute-start.17
  71.0 0.7 collective-permute-start.16
  71.7 6.0 %collective-permute-start.9 = (f32[2,48,128]{2,1,0:T(8,128)S(1)}, f32[2,48,128]{2,1,0:T(8,128)S(1)}, u32[]{:S(2)}, u32[]{:S(2)}) collective-permute-start(f32[2,48,128]{2,1,0:T(8,128)S(1)} %pad_maximum_fusion), channel_id=1, source_target_pairs={{0,6},{1,7},{2,4},{3,5},{4,2},{5,3},{6,0},{7,1},{8,14},{9,15},{10,... | collective-permute-start | bytes 147464 | tf_op jit(solution)/shard_map/ppermute | solution.py:415
  77.7 0.7 pad_select_fusion
  78.4 0.8 collective-permute-done.9
  79.3 0.7 collective-permute-start.15
  80.6 26.5 %collective-permute-start.10 = (f32[8,48,128]{2,1,0:T(8,128)}, f32[8,48,128]{2,1,0:T(8,128)S(1)}, u32[]{:S(2)}, u32[]{:S(2)}) collective-permute-start(f32[8,48,128]{2,1,0:T(8,128)} %get-tuple-element.17), channel_id=1, source_target_pairs={{0,1},{1,0},{2,3},{3,2},{4,5},{5,4},{6,7},{7,6},{8,9},{9,8},{10,11... | collective-permute-start | bytes 589832 | tf_op jit(solution)/shard_map/ppermute | solution.py:415
  107.1 0.7 collective-permute-start.4
  107.8 1.9 %collective-permute-start.5 = (f32[16,384]{1,0:T(8,128)S(1)}, f32[16,384]{1,0:T(8,128)S(1)}, u32[]{:S(2)}, u32[]{:S(2)}) collective-permute-start(f32[16,384]{1,0:T(8,128)S(1)} %pad_maximum_fusion.2), channel_id=1, source_target_pairs={{0,16},{32,48},{64,80},{96,112},{128,144},{160,176},{192,208},{224... | collective-permute-start | bytes 73736 | tf_op jit(solution)/shard_map/ppermute | solution.py:456
  109.8 2.6 %collective-permute-done.5.cb = f32[16,384]{1,0:T(8,128)S(1)} collective-permute-done((f32[16,384]{1,0:T(8,128)S(1)}, f32[16,384]{1,0:T(8,128)S(1)}, u32[]{:S(2)}, u32[]{:S(2)}) %collective-permute-start.5) | collective-permute-done | bytes 24608 | tf_op jit(solution)/shard_map/ppermute | solution.py:456
  112.4 0.7 broadcast_in_dim.27.colid
  113.1 0.7 copy-done.6
  113.8 0.7 copy-done.8
  114.4 9.5 %steps.1 = f32[16,48,384]{2,1,0:T(8,128)} custom-call(s32[4]{0:T(128)S(1)} %copy-done.8, f32[16,48,384]{2,1,0:T(8,128)S(1)} %copy-done.1, f32[16,48,384]{2,1,0:T(8,128)S(1)} %copy-done.3, f32[48,384]{1,0:T(8,128)S(1)} %copy-done.5, f32[3,184,128]{2,1,0:T(8,128)S(1)} %collective-permute-done.ra, f32[3,184,128]{2,1,0:T(8,128)S(1)} %collective-permute-done.1.rb, ...), custom_call_target="tpu_custom_call" | custom-call | tf_op jit(solution)/shard_map/steps/pallas_call | solution.py:459
  (61 shorter events, 9.2 us)
Async XLA Ops:
  1.4 45.5 %collective-permute-start.11 = (f32[1,16,128]{2,1,0:T(8,128)}, f32[1,16,128]{2,1,0:T(8,128)}, u32[]{:S(2)}, u32[]{:S(2)}) collective-permute-start(f32[1,16,128]{2,1,0:T(8,128)} %pad_bitcast_fusion), channel_id=1, source_target_pairs={{0,256},{16,272},{32,288},{48,304},{64,320},{80,336},{96,352},{112... | collective-permute-start | bytes 24584 | tf_op jit(solution)/shard_map/ppermute | solution.py:415
  4.1 53.6 %collective-permute-start.6 = (f32[1,48,128]{2,1,0:T(8,128)}, f32[1,48,128]{2,1,0:T(8,128)}, u32[]{:S(2)}, u32[]{:S(2)}) collective-permute-start(f32[1,48,128]{2,1,0:T(8,128)} %bitcast.9), channel_id=1, source_target_pairs={{0,8},{1,9},{2,10},{3,11},{4,12},{5,13},{6,14},{7,15},{8,0},{9,1},... | collective-permute-start | bytes 73736 | tf_op jit(solution)/shard_map/ppermute | solution.py:415
  16.5 1.3 %copy-start = (f32[16,48,384]{2,1,0:T(8,128)S(1)}, f32[16,48,384]{2,1,0:T(8,128)}, u32[]{:S(2)}) copy-start(f32[16,48,384]{2,1,0:T(8,128)} %state.3) | copy-start | bytes 3538948
  17.8 1.3 %copy-start.2 = (f32[16,48,384]{2,1,0:T(8,128)S(1)}, f32[16,48,384]{2,1,0:T(8,128)}, u32[]{:S(2)}) copy-start(f32[16,48,384]{2,1,0:T(8,128)} %diffuse.3) | copy-start | bytes 3538948
  19.1 0.9 copy-start.4
  20.0 1.8 %copy-start.7 = (s32[4]{0:T(128)}, s32[4]{0:T(128)S(1)}, u32[]{:S(2)}) copy-start(s32[4]{0:T(128)S(1)} %pad_add_fusion.place) | copy-start | bytes 52
  20.0 16.7 %copy-start.12 = (s32[32]{0:T(128)S(1)}, s32[32]{0:T(128)}, u32[]{:S(2)}) copy-start(s32[32]{0:T(128)} %constant.39.clone) | copy-start | bytes 388
  20.0 17.2 %copy-start.11 = (s32[48]{0:T(128)S(1)}, s32[48]{0:T(128)}, u32[]{:S(2)}) copy-start(s32[48]{0:T(128)} %param.22) | copy-start | bytes 580
  20.0 17.7 %copy-start.10 = (f32[2,16,16]{2,1,0:T(8,128)S(1)}, f32[2,16,16]{2,1,0:T(8,128)}, u32[]{:S(2)}) copy-start(f32[2,16,16]{2,1,0:T(8,128)} %param.19) | copy-start | bytes 6148
  21.7 0.7 copy-start.9
  22.5 49.3 %collective-permute-start.2 = (f32[48,384]{1,0:T(8,128)}, f32[48,384]{1,0:T(8,128)S(1)}, u32[]{:S(2)}, u32[]{:S(2)}) collective-permute-start(f32[48,384]{1,0:T(8,128)} %get-tuple-element.11), channel_id=1, source_target_pairs={{0,1},{1,2},{2,3},{3,4},{4,5},{5,6},{6,7},{7,8},{8,9},{9,10},{10,1... | collective-permute-start | bytes 221192 | tf_op jit(solution)/shard_map/ppermute | solution.py:424
  26.8 44.2 %collective-permute-start.3 = (f32[48,384]{1,0:T(8,128)}, f32[48,384]{1,0:T(8,128)S(1)}, u32[]{:S(2)}, u32[]{:S(2)}) collective-permute-start(f32[48,384]{1,0:T(8,128)} %get-tuple-element.12), channel_id=1, source_target_pairs={{1,0},{2,1},{3,2},{4,3},{5,4},{6,5},{7,6},{8,7},{9,8},{10,9},{11,1... | collective-permute-start | bytes 221192 | tf_op jit(solution)/shard_map/ppermute | solution.py:425
  33.9 78.4 %collective-permute-start = (f32[3,184,128]{2,1,0:T(8,128)}, f32[3,184,128]{2,1,0:T(8,128)S(1)}, u32[]{:S(2)}, u32[]{:S(2)}) collective-permute-start(f32[3,184,128]{2,1,0:T(8,128)} %get-tuple-element.9), channel_id=1, source_target_pairs={{16,32},{48,64},{80,96},{112,128},{144,160},{176,192},{208,224},{2... | collective-permute-start | bytes 847880 | tf_op jit(solution)/shard_map/ppermute | solution.py:408
  34.6 78.4 %copy-start.5 = (f32[48,384]{1,0:T(8,128)S(1)}, f32[48,384]{1,0:T(8,128)}, u32[]{:S(2)}) copy-start(f32[48,384]{1,0:T(8,128)} %vertical.3) | copy-start | bytes 221188
  35.2 77.8 %copy-start.3 = (f32[16,48,384]{2,1,0:T(8,128)S(1)}, f32[16,48,384]{2,1,0:T(8,128)}, u32[]{:S(2)}) copy-start(f32[16,48,384]{2,1,0:T(8,128)} %diffuse.3) | copy-start | bytes 3538948
  36.7 76.4 %copy-start.1 = (f32[16,48,384]{2,1,0:T(8,128)S(1)}, f32[16,48,384]{2,1,0:T(8,128)}, u32[]{:S(2)}) copy-start(f32[16,48,384]{2,1,0:T(8,128)} %state.3) | copy-start | bytes 3538948
  47.7 2.0 %collective-permute-start.12 = (f32[2,16,128]{2,1,0:T(8,128)S(1)}, f32[2,16,128]{2,1,0:T(8,128)S(1)}, u32[]{:S(2)}, u32[]{:S(2)}) collective-permute-start(f32[2,16,128]{2,1,0:T(8,128)S(1)} %pad_maximum_fusion.3), channel_id=1, source_target_pairs={{0,64},{16,80},{32,96},{48,112},{64,0},{80,16},{96,32},{112,48},{1... | collective-permute-start | bytes 49160 | tf_op jit(solution)/shard_map/ppermute | solution.py:415
  49.6 1.3 %collective-permute-start.13 = (f32[2,16,128]{2,1,0:T(8,128)S(1)}, f32[2,16,128]{2,1,0:T(8,128)S(1)}, u32[]{:S(2)}, u32[]{:S(2)}) collective-permute-start(f32[2,16,128]{2,1,0:T(8,128)S(1)} %pad_maximum_fusion.3), channel_id=1, source_target_pairs={{0,128},{16,144},{32,160},{48,176},{64,192},{80,208},{96,224},{112... | collective-permute-start | bytes 49160 | tf_op jit(solution)/shard_map/ppermute | solution.py:415
  50.9 1.3 %collective-permute-start.14 = (f32[2,16,128]{2,1,0:T(8,128)S(1)}, f32[2,16,128]{2,1,0:T(8,128)S(1)}, u32[]{:S(2)}, u32[]{:S(2)}) collective-permute-start(f32[2,16,128]{2,1,0:T(8,128)S(1)} %pad_maximum_fusion.3), channel_id=1, source_target_pairs={{0,192},{16,208},{32,224},{48,240},{64,128},{80,144},{96,160},{112... | collective-permute-start | bytes 49160 | tf_op jit(solution)/shard_map/ppermute | solution.py:415
  52.2 60.2 %collective-permute-start.1 = (f32[3,184,128]{2,1,0:T(8,128)}, f32[3,184,128]{2,1,0:T(8,128)S(1)}, u32[]{:S(2)}, u32[]{:S(2)}) collective-permute-start(f32[3,184,128]{2,1,0:T(8,128)} %copy-done.9), channel_id=1, source_target_pairs={{0,16},{32,48},{64,80},{96,112},{128,144},{160,176},{192,208},{224... | collective-permute-start | bytes 847880 | tf_op jit(solution)/shard_map/ppermute | solution.py:423
  58.4 5.3 %collective-permute-start.7 = (f32[2,48,128]{2,1,0:T(8,128)S(1)}, f32[2,48,128]{2,1,0:T(8,128)S(1)}, u32[]{:S(2)}, u32[]{:S(2)}) collective-permute-start(f32[2,48,128]{2,1,0:T(8,128)S(1)} %pad_maximum_fusion), channel_id=1, source_target_pairs={{0,2},{1,3},{2,0},{3,1},{4,6},{5,7},{6,4},{7,5},{8,10},{9,11},{10,... | collective-permute-start | bytes 147464 | tf_op jit(solution)/shard_map/ppermute | solution.py:415
  63.7 6.0 %collective-permute-start.8 = (f32[2,48,128]{2,1,0:T(8,128)S(1)}, f32[2,48,128]{2,1,0:T(8,128)S(1)}, u32[]{:S(2)}, u32[]{:S(2)}) collective-permute-start(f32[2,48,128]{2,1,0:T(8,128)S(1)} %pad_maximum_fusion), channel_id=1, source_target_pairs={{0,4},{1,5},{2,6},{3,7},{4,0},{5,1},{6,2},{7,3},{8,12},{9,13},{10,... | collective-permute-start | bytes 147464 | tf_op jit(solution)/shard_map/ppermute | solution.py:415
  69.7 38.0 %collective-permute-start.17 = (f32[8,16,128]{2,1,0:T(8,128)}, f32[8,16,128]{2,1,0:T(8,128)S(1)}, u32[]{:S(2)}, u32[]{:S(2)}) collective-permute-start(f32[8,16,128]{2,1,0:T(8,128)} %get-tuple-element.29), channel_id=1, source_target_pairs={{0,48},{16,32},{32,16},{48,0},{64,112},{80,96},{96,80},{112,64},{1... | collective-permute-start | bytes 196616 | tf_op jit(solution)/shard_map/ppermute | solution.py:415
  71.0 36.1 %collective-permute-start.16 = (f32[8,16,128]{2,1,0:T(8,128)}, f32[8,16,128]{2,1,0:T(8,128)S(1)}, u32[]{:S(2)}, u32[]{:S(2)}) collective-permute-start(f32[8,16,128]{2,1,0:T(8,128)} %get-tuple-element.29), channel_id=1, source_target_pairs={{0,32},{16,48},{32,0},{48,16},{64,96},{80,112},{96,64},{112,80},{1... | collective-permute-start | bytes 196616 | tf_op jit(solution)/shard_map/ppermute | solution.py:415
  71.7 7.5 %collective-permute-start.9 = (f32[2,48,128]{2,1,0:T(8,128)S(1)}, f32[2,48,128]{2,1,0:T(8,128)S(1)}, u32[]{:S(2)}, u32[]{:S(2)}) collective-permute-start(f32[2,48,128]{2,1,0:T(8,128)S(1)} %pad_maximum_fusion), channel_id=1, source_target_pairs={{0,6},{1,7},{2,4},{3,5},{4,2},{5,3},{6,0},{7,1},{8,14},{9,15},{10,... | collective-permute-start | bytes 147464 | tf_op jit(solution)/shard_map/ppermute | solution.py:415
  79.3 1.3 %collective-permute-start.15 = (f32[8,16,128]{2,1,0:T(8,128)}, f32[8,16,128]{2,1,0:T(8,128)S(1)}, u32[]{:S(2)}, u32[]{:S(2)}) collective-permute-start(f32[8,16,128]{2,1,0:T(8,128)} %get-tuple-element.29), channel_id=1, source_target_pairs={{0,16},{16,0},{32,48},{48,32},{64,80},{80,64},{96,112},{112,96},{1... | collective-permute-start | bytes 196616 | tf_op jit(solution)/shard_map/ppermute | solution.py:415
  80.6 29.2 %collective-permute-start.10 = (f32[8,48,128]{2,1,0:T(8,128)}, f32[8,48,128]{2,1,0:T(8,128)S(1)}, u32[]{:S(2)}, u32[]{:S(2)}) collective-permute-start(f32[8,48,128]{2,1,0:T(8,128)} %get-tuple-element.17), channel_id=1, source_target_pairs={{0,1},{1,0},{2,3},{3,2},{4,5},{5,4},{6,7},{7,6},{8,9},{9,8},{10,11... | collective-permute-start | bytes 589832 | tf_op jit(solution)/shard_map/ppermute | solution.py:415
  107.1 2.7 %collective-permute-start.4 = (f32[16,384]{1,0:T(8,128)S(1)}, f32[16,384]{1,0:T(8,128)S(1)}, u32[]{:S(2)}, u32[]{:S(2)}) collective-permute-start(f32[16,384]{1,0:T(8,128)S(1)} %pad_maximum_fusion.1), channel_id=1, source_target_pairs={{16,32},{48,64},{80,96},{112,128},{144,160},{176,192},{208,224},{2... | collective-permute-start | bytes 73736 | tf_op jit(solution)/shard_map/ppermute | solution.py:455
  107.8 4.6 %collective-permute-start.5 = (f32[16,384]{1,0:T(8,128)S(1)}, f32[16,384]{1,0:T(8,128)S(1)}, u32[]{:S(2)}, u32[]{:S(2)}) collective-permute-start(f32[16,384]{1,0:T(8,128)S(1)} %pad_maximum_fusion.2), channel_id=1, source_target_pairs={{0,16},{32,48},{64,80},{96,112},{128,144},{160,176},{192,208},{224... | collective-permute-start | bytes 73736 | tf_op jit(solution)/shard_map/ppermute | solution.py:456
  113.1 0.7 copy-start.6
  113.8 0.7 copy-start.8

commit v2 on v1

--- a/solution.py
+++ b/solution.py
@@ -24,21 +24,52 @@
         return [[16], [4, 8, 12], [1, 2, 3]]
     if count == 16:
         return [[8], [2, 4, 6], [1]]
-    masks, bit = [], count // 2
-    while bit:
-        masks.append([bit])
-        bit //= 2
-    return masks
-
-
-def masks_of(count):
+    return [[2], [1], []]
+
+
+def masks_of(rounds):
     have = [0]
-    for masks in rounds_of(count):
+    for masks in rounds:
         have = [m ^ h for m in [0] + masks for h in have]
     return have
 
 
-def pack_kernel(place, state, diffuse, vertical, filler, interp, xa, xb, y_low, y_high):
+def pack_kernel(
+    state_hbm, diffuse_hbm, vertical, rows_we, rows_sn, fill_we, fill_sn, index_we, weight_we, index_sn, weight_sn,
+    xa, xb, y_low, y_high, chain_x, chain_y, colpack, interp, state, diffuse, square, sem,
+):
+    copies = [
+        pltpu.make_async_copy(state_hbm, state, sem.at[0]),
+        pltpu.make_async_copy(diffuse_hbm, diffuse, sem.at[1]),
+    ]
+    for copy in copies:
+        copy.start()
+    nx, ny = lax.axis_index("nx"), lax.axis_index("ny")
+    odd = nx % 2 == 1
+
+    side_x = jnp.where(ny == 0, 0, 1)
+    side_y = jnp.where(nx == 0, 0, 1)
+    lane = lax.broadcasted_iota(jnp.int32, (128, 128), 1)
+    square[...] = jnp.zeros((128, 128), jnp.float32)
+    for step in range(3):
+        chain_y[0, 16 * step : 16 * step + 16, :] = rows_we[step, side_y]
+        square[16 * step : 16 * step + 16, 0:16] = rows_sn[step, side_x]
+    chain_x[0] = square[...].T[0:16]
+    square[0:48, :] = jnp.zeros((48, 128), jnp.float32)
+    square[96:112, 0:16] = fill_sn[0]
+    square[112:128, 0:16] = fill_sn[1]
+    square[64:65, 0:WX] = index_sn[...].astype(jnp.float32).reshape(1, WX)
+    square[65:66, 0:WX] = weight_sn[...].reshape(1, WX)
+    whole = square[...]
+    row = lax.broadcasted_iota(jnp.int32, (128, 128), 0)
+    whole = jnp.where((lane < 8) | (row < 96), whole, pltpu.roll(whole, 32, 1))
+    colpack[...] = whole.T[0:WX]
+    interp[...] = jnp.zeros((8, WY), jnp.float32)
+    interp[0:1, :] = index_we[...].astype(jnp.float32).reshape(1, WY)
+    interp[1:2, :] = weight_we[...].reshape(1, WY)
+    square[0:16, :] = fill_we[0]
+    square[16:32, :] = fill_we[1]
+
     def rows(ref, high):
         at = WX - STATE_ROWS if high else 0
         bt = WX - COEF_ROWS if high else 0
@@ -52,7 +83,8 @@
             ref[l, VERT_AT : VERT_AT + COEF_ROWS, :] = vertical[bt : bt + COEF_ROWS, lanes]
             ref[l, VERT_AT + COEF_ROWS :, :] = jnp.zeros((XROWS - VERT_AT - COEF_ROWS, 128), jnp.float32)
 
-    odd = place[2] % 2 == 1
+    for copy in copies:
+        copy.wait()
 
     @pl.when(odd)
     def _():
@@ -75,9 +107,8 @@
                 total = jnp.where((lane >= 8 * k) & (lane < 8 * k + 8), part, total)
             ref[:, 128 * which : 128 * which + 128] = total
         last = jnp.where(lane < 8, pltpu.roll(vertical[:, lanes], (-first) % 128, 1), 0.0)
-        src = filler[:, 0:128]
         last = jnp.where(
-            (lane >= 8) & (lane < 16), pltpu.roll(src, (8 - first) % 128, 1), last
+            (lane >= 8) & (lane < 16), pltpu.roll(square[0:WX, :], (8 - first) % 128, 1), last
         )
         pair = jnp.where(row == 0, interp[0:1, lanes], interp[1:2, lanes])
         last = jnp.where(
@@ -86,11 +117,44 @@
         ref[:, 256:384] = last
 
 
+def corner_kernel(from_low, from_high, colpack, ca, cb):
+    odd = lax.axis_index("nx") % 2 == 1
+    clear = lax.broadcasted_iota(jnp.int32, (8, 128), 1) < 64
+
+    def rows(ref, at):
+        ref[0:8, 0:256] = from_low[at : at + 8, 0:256]
+        ref[0:8, 256:384] = jnp.where(clear, from_low[at : at + 8, 256:384], colpack[at : at + 8, :])
+        ref[8:16, :] = from_high[at : at + 8, :]
+
+    @pl.when(odd)
+    def _():
+        rows(ca, 40)
+        rows(cb, 0)
+
+    @pl.when(jnp.logical_not(odd))
+    def _():
+        rows(ca, 0)
+        rows(cb, 40)
+
+
+def join_kernel(count_x, count_y, after, *refs):
+    ins, (out_x, out_y) = refs[:-2], refs[-2:]
+    for out, parts in ((out_x, ins[:count_x]), (out_y, ins[count_x : count_x + count_y])):
+        at = 0
+        for part in parts:
+            out[at : at + part.shape[0]] = part[...]
+            at += part.shape[0]
+
+
 def main_kernel(
-    count_x, count_y, masks_y, place, state, diffuse, vertical, ra, rb, from_low, from_high, ca, cb,
-    colpack, interp, chain_y, chain_x, colid, filler, out, es, ed, ev, mv, gv, fac, strip, ey, ex, pack, sem,
+    count_x, count_y, plan_x, plan_y, jump, state, diffuse, vertical, ra, rb, from_low, from_high, ca, cb,
+    colpack, interp, fill_we, *refs,
 ):
-    dx, dy, nx, ny = place[0], place[1], place[2], place[3]
+    chain_x, refs = refs[: len(plan_x)], refs[len(plan_x) :]
+    chain_y, refs = refs[: len(plan_y)], refs[len(plan_y) :]
+    out, es, ed, ev, mv, gv, fac, strip, ey, ex, pack, sem = refs
+    dx, dy = jump[0], jump[1]
+    nx, ny = lax.axis_index("nx"), lax.axis_index("ny")
     copies = []
     for which, (src, dst) in enumerate(((state, es), (diffuse, ed))):
         for l in range(NG):
@@ -166,9 +230,10 @@
                 at = index + offset
                 block, inside = at >> 7, at & 127
                 total = jnp.zeros((48, 128), jnp.float32)
-                for piece, mask in enumerate(masks_y):
-                    value = jnp.take_along_axis(chain_y[piece], inside, axis=1, mode="promise_in_bounds")
-                    total = jnp.where(block == (ny ^ mask), value, total)
+                for ref, masks in zip(chain_y, plan_y, strict=True):
+                    for piece, mask in enumerate(masks):
+                        value = jnp.take_along_axis(ref[piece], inside, axis=1, mode="promise_in_bounds")
+                        total = jnp.where(block == (ny ^ mask), value, total)
                 ends.append(total)
             ey[l] = (1.0 - got[1]) * ends[0] + got[1] * ends[1]
 
@@ -176,11 +241,21 @@
     def _():
         index = pack[:, 64:65].astype(jnp.int32)
         weight = pack[:, 65:66]
-        ids = colid[0:1, :]
-        spread = jnp.where(ids == index, 1.0 - weight, 0.0) + jnp.where(ids == index + 1, weight, 0.0)
-        ex[0:64, :] = jnp.dot(
-            spread, chain_x[...], preferred_element_type=jnp.float32, precision=lax.Precision.HIGHEST
-        )
+        total = jnp.zeros((64, 128), jnp.float32)
+        for ref, masks in zip(chain_x, plan_x, strict=True):
+            size = 16 * len(masks)
+            at = lax.broadcasted_iota(jnp.int32, (1, size), 1)
+            ids = at & 15
+            for piece, mask in enumerate(masks):
+                ids = jnp.where(at >> 4 == piece, ids + 16 * (nx ^ mask), ids)
+            spread = jnp.where(ids == index, 1.0 - weight, 0.0) + jnp.where(ids == index + 1, weight, 0.0)
+            total += jnp.dot(
+                spread,
+                ref[...].reshape(size, 128),
+                preferred_element_type=jnp.float32,
+                precision=lax.Precision.HIGHEST,
+            )
+        ex[0:64, :] = total
 
     def ghosts(field, step, row_low, row_high, shift):
         @pl.when(west)
@@ -302,8 +377,7 @@
 
             @pl.when(is_side)
             def _():
-                rows = slice(16 * side, 16 * side + 16)
-                own = filler[rows, :]
+                own = fill_we[side]
                 ring = jnp.where(
                     lane16 < 64,
                     pltpu.roll(strip[1, HX + 16 * side : HX + 16 * side + 16, 256:384], 120, 1),
@@ -375,29 +449,37 @@
 ):
     f32 = jnp.float32
     count_x, count_y = lax.axis_size("nx"), lax.axis_size("ny")
-    nx, ny = lax.axis_index("nx"), lax.axis_index("ny")
     both = ("nx", "ny")
-    place = jnp.stack([jump[0], jump[1], nx, ny]).astype(jnp.int32)
-    odd = nx % 2
-
-    filler = fill_we.reshape(32, 128)
-    interp = jnp.stack([index_we.astype(f32), weight_we])
-    interp = jnp.pad(interp, ((0, 6), (0, 0)))
     vmem = pl.BlockSpec(memory_space=pltpu.VMEM)
     smem = pl.BlockSpec(memory_space=pltpu.SMEM)
-    xa, xb, y_low, y_high = pl.pallas_call(
+    hbm = pl.BlockSpec(memory_space=pl.ANY)
+
+    def shape(*dims):
+        return jax.ShapeDtypeStruct(dims, f32)
+
+    xa, xb, y_low, y_high, chain_x, chain_y, colpack, interp = pl.pallas_call(
         pack_kernel,
         out_shape=(
-            jax.ShapeDtypeStruct((NG, XROWS, 128), f32),
-            jax.ShapeDtypeStruct((NG, XROWS, 128), f32),
-            jax.ShapeDtypeStruct((WX, WY), f32),
-            jax.ShapeDtypeStruct((WX, WY), f32),
+            shape(NG, XROWS, 128),
+            shape(NG, XROWS, 128),
+            shape(WX, WY),
+            shape(WX, WY),
+            shape(1, 16, 128),
+            shape(1, 48, 128),
+            shape(WX, 128),
+            shape(8, WY),
         ),
-        in_specs=[smem] + [vmem] * 5,
-        out_specs=(vmem,) * 4,
+        in_specs=[hbm] * 2 + [vmem] * 9,
+        out_specs=(vmem,) * 8,
+        scratch_shapes=[
+            pltpu.VMEM((LV, WX, WY), f32),
+            pltpu.VMEM((LV, WX, WY), f32),
+            pltpu.VMEM((128, 128), f32),
+            pltpu.SemaphoreType.DMA((2,)),
+        ],
         compiler_params=pltpu.CompilerParams(vmem_limit_bytes=40 << 20),
         name="pack",
-    )(place, state, diffuse, vertical, jnp.pad(filler, ((0, 16), (0, 0))), interp)
+    )(state, diffuse, vertical, rows_we, rows_sn, fill_we, fill_sn, index_we, weight_we, index_sn, weight_sn)
 
     pairs_a = [(i, i + 1) for i in range(1, count_x - 1, 2)]
     pairs_a += [(b, a) for a, b in pairs_a]
@@ -405,61 +487,69 @@
     pairs_b += [(b, a) for a, b in pairs_b]
     up = [(i, i + 1) for i in range(count_y - 1)]
     down = [(b, a) for a, b in up]
+    rounds_x, rounds_y = rounds_of(count_x), rounds_of(count_y)
+
+    def along_x(chain, masks):
+        return [
+            lax.ppermute(
+                chain,
+                both,
+                [(i * count_y + n, (i ^ m) * count_y + n) for n in (0, count_y - 1) for i in range(count_x)],
+            )
+            for m in masks
+        ]
+
+    def along_y(chain, masks):
+        return [
+            lax.ppermute(
+                chain,
+                both,
+                [(n * count_y + j, n * count_y + (j ^ m)) for n in (0, count_x - 1) for j in range(count_y)],
+            )
+            for m in masks
+        ]
+
+    def join(after, parts_x, parts_y, name):
+        return pl.pallas_call(
+            functools.partial(join_kernel, len(parts_x), len(parts_y)),
+            out_shape=(
+                shape(sum(p.shape[0] for p in parts_x), 16, 128),
+                shape(sum(p.shape[0] for p in parts_y), 48, 128),
+            ),
+            in_specs=[hbm] + [vmem] * (len(parts_x) + len(parts_y)),
+            out_specs=(vmem, vmem),
+            name=name,
+        )(after, *parts_x, *parts_y)
+
+    parts_x = [chain_x] + along_x(chain_x, rounds_x[0])
     ra = lax.ppermute(xa, "nx", pairs_a)
-
-    chain_x = jnp.where(ny == 0, rows_sn[:, 0], rows_sn[:, 1]).reshape(48, 16)
-    chain_x = jnp.pad(chain_x.T, ((0, 0), (0, 80)))[None]
-    chain_y = jnp.where(nx == 0, rows_we[:, 0], rows_we[:, 1]).reshape(48, 128)[None]
-
-    def grow(chain, masks, pairs):
-        return jnp.concatenate([chain] + [lax.ppermute(chain, both, pairs(m)) for m in masks])
-
-    def pairs_x(mask):
-        return [(i * count_y + n, (i ^ mask) * count_y + n) for n in (0, count_y - 1) for i in range(count_x)]
-
-    def pairs_y(mask):
-        return [(n * count_y + j, n * count_y + (j ^ mask)) for n in (0, count_x - 1) for j in range(count_y)]
-
-    rb = lax.ppermute(xb, "nx", pairs_b)
+    parts_y = [chain_y] + along_y(chain_y, rounds_y[0])
     from_low = lax.ppermute(y_high, "ny", up)
     from_high = lax.ppermute(y_low, "ny", down)
-    for mx, my in zip(rounds_of(count_x), rounds_of(count_y), strict=True):
-        chain_x = grow(chain_x, mx, pairs_x)
-        chain_y = grow(chain_y, my, pairs_y)
-    masks_x, masks_y = masks_of(count_x), masks_of(count_y)
-    chain_x = chain_x.reshape(16 * count_x, 128)
-    blocks = nx ^ jnp.array(masks_x, jnp.int32)
-    colid = (blocks[:, None] * 16 + jnp.arange(16, dtype=jnp.int32)).reshape(1, -1)
-    colid = jnp.broadcast_to(colid, (8, 16 * count_x))
-
-    fill_t = fill_sn.reshape(32, 16).T
-    fill_t = jnp.pad(fill_t.reshape(2, 8, 32), ((0, 0), (0, 32), (0, 0))).reshape(80, 32)[:WX]
-    colpack = jnp.concatenate(
-        [
-            jnp.zeros((WX, 64), f32),
-            index_sn.astype(f32)[:, None],
-            weight_sn[:, None],
-            jnp.zeros((WX, 30), f32),
-            fill_t,
-        ],
-        axis=1,
-    )
-
-    def corner(start):
-        low = lax.dynamic_slice(from_low, (start, 0), (8, WY))
-        high = lax.dynamic_slice(from_high, (start, 0), (8, WY))
-        own = jnp.pad(lax.dynamic_slice(colpack, (start, 0), (8, 128)), ((0, 0), (256, 0)))
-        clear = lax.broadcasted_iota(jnp.int32, (8, WY), 1) < 256 + 64
-        return jnp.concatenate([jnp.where(clear, low, own), high])
-
-    ca = lax.ppermute(corner(40 * odd), "nx", pairs_a)
-    cb = lax.ppermute(corner(40 - 40 * odd), "nx", pairs_b)
-
-    any_ = pl.BlockSpec(memory_space=pl.ANY)
+    rb = lax.ppermute(xb, "nx", pairs_b)
+    ca, cb = pl.pallas_call(
+        corner_kernel,
+        out_shape=(shape(16, WY), shape(16, WY)),
+        in_specs=[vmem] * 3,
+        out_specs=(vmem, vmem),
+        name="corner",
+    )(from_low, from_high, colpack)
+    chain_x, chain_y = join(ca, parts_x, parts_y, "join_first")
+    parts_x = [chain_x] + along_x(chain_x, rounds_x[1])
+    parts_y = [chain_y] + along_y(chain_y, rounds_y[1])
+    ra2 = lax.ppermute(ca, "nx", pairs_a)
+    rb2 = lax.ppermute(cb, "nx", pairs_b)
+    chain_x, chain_y = join(ca, parts_x, parts_y, "join_second")
+    parts_x = [chain_x] + along_x(chain_x, rounds_x[2])
+    parts_y = [chain_y] + along_y(chain_y, rounds_y[2])
+    have_x, have_y = masks_of(rounds_x[:2]), masks_of(rounds_y[:2])
+    plan_x = [[m ^ h for h in have_x] for m in [0] + rounds_x[2]]
+    plan_y = [[m ^ h for h in have_y] for m in [0] + rounds_y[2]]
+
     return pl.pallas_call(
-        functools.partial(main_kernel, count_x, count_y, masks_y),
-        out_shape=jax.ShapeDtypeStruct((LV, WX, WY), f32),
-        in_specs=[smem, any_, any_] + [vmem] * 13,
+        functools.partial(main_kernel, count_x, count_y, plan_x, plan_y),
+        out_shape=shape(LV, WX, WY),
+        in_specs=[smem, hbm, hbm] + [vmem] * (10 + len(parts_x) + len(parts_y)),
         out_specs=vmem,
         scratch_shapes=[
             pltpu.VMEM((LV, NG + 1, 72, 128), f32),
@@ -477,8 +567,8 @@
         compiler_params=pltpu.CompilerParams(vmem_limit_bytes=48 << 20),
         name="steps",
     )(
-        place, state, diffuse, vertical, ra, rb, from_low, from_high, ca, cb,
-        colpack, interp, chain_y, chain_x, colid, filler,
+        jump, state, diffuse, vertical, ra, rb, from_low, from_high, ra2, rb2,
+        colpack, interp, fill_we, *parts_x, *parts_y,
     )
 
 

time: 125 us -> 117 us (0.936)
  the two profiles are of different devices: /device:TPU:1 before, /device:TPU:26 now
where the time goes in v2:
time: 117 us; the launch traced here: 116 us
  starting transfers between devices  69.2 us (59%)
  local copies, waits for them, and re-layouts  16.4 us (14%)
  Pallas kernels  16.2 us (14%)
  waiting for transfers between devices  13.8 us (12%)
    ppermute x7, starting transfers between devices, along_x(): lax.ppermute(chain, both, [(i * count_y + n, (i ^ m) * count_y + n) for n...  51.2 us
    unnamed x68, local copies, waits for them, and re-layouts  16.4 us
    pallas_call x1, Pallas kernels, on_device(): pl.pallas_call(functools.partial(main_kernel, count_x, count_y, plan_x, p...  9.75 us
    ppermute x7, waiting for transfers between devices, along_x(): lax.ppermute(chain, both, [(i * count_y + n, (i ^ m) * count_y + n) for n...  6.41 us
    ppermute x1, waiting for transfers between devices, on_device(): ra2 = lax.ppermute(ca, 'nx', pairs_a)  4 us
    ppermute x1, starting transfers between devices, on_device(): rb = lax.ppermute(xb, 'nx', pairs_b)  3.89 us
    ppermute x1, starting transfers between devices, on_device(): ra = lax.ppermute(xa, 'nx', pairs_a)  3.4 us
    ppermute x1, waiting for transfers between devices, on_device(): rb2 = lax.ppermute(cb, 'nx', pairs_b)  3.4 us
  transfers between devices with their start and end apart: 18, of which 5 were waited for; matrix products, arithmetic and copies ran while one was open for 0% of the time, Pallas kernels for 4%

profile of v2, /device:TPU:26, one launch (start us, length us, event | category | flops | bytes accessed | tf_op | source)
XLA Modules:
  0.0 116.1 jit_solution(11448114319418665038)
XLA Ops:
  0.0 1.3 %copy-done = f32[16,48,384]{2,1,0:T(8,128)S(1)} copy-done((f32[16,48,384]{2,1,0:T(8,128)S(1)}, f32[16,48,384]{2,1,0:T(8,128)}, u32[]{:S(2)}) %copy-start) | copy-done | bytes 1179672
  1.3 1.3 %copy-done.2 = f32[16,48,384]{2,1,0:T(8,128)S(1)} copy-done((f32[16,48,384]{2,1,0:T(8,128)S(1)}, f32[16,48,384]{2,1,0:T(8,128)}, u32[]{:S(2)}) %copy-start.2) | copy-done | bytes 1179672
  2.5 0.9 copy-done.4
  3.4 0.7 copy-done.14
  4.1 0.8 copy-done.16
  4.9 0.8 copy-done.17
  5.7 0.7 copy-done.19
  6.5 0.7 copy-done.21
  7.1 0.7 copy-done.22
  7.8 0.7 copy-done.23
  8.5 0.7 copy-done.24
  9.2 1.9 %pack.1 = (f32[3,184,128]{2,1,0:T(8,128)}, f32[3,184,128]{2,1,0:T(8,128)S(1)}, f32[48,384]{1,0:T(8,128)S(1)}, f32[48,384]{1,0:T(8,128)S(1)}, f32[1,16,128]{2,1,0...) custom-call(f32[16,48,384]{2,1,0:T(8,128)S(1)} %copy-done, ...), custom_call_target="tpu_custom_call" | custom-call | tf_op jit(solution)/shard_map/pack/pallas_call | solution.py:460
  11.0 0.6 copy-done.11
  11.6 1.7 %collective-permute-start.2 = (f32[48,384]{1,0:T(8,128)S(1)}, f32[48,384]{1,0:T(8,128)S(1)}, u32[]{:S(2)}, u32[]{:S(2)}) collective-permute-start(f32[48,384]{1,0:T(8,128)S(1)} %get-tuple-element.21), channel_id=1, source_target_pairs={{0,1},{1,2},{2,3},{3,4},{4,5},{5,6},{6,7},{7,8},{8,9},{9,10},{10,1... | collective-permute-start | bytes 221192 | tf_op jit(solution)/shard_map/ppermute | solution.py:527
  13.4 1.3 %collective-permute-start.3 = (f32[48,384]{1,0:T(8,128)S(1)}, f32[48,384]{1,0:T(8,128)S(1)}, u32[]{:S(2)}, u32[]{:S(2)}) collective-permute-start(f32[48,384]{1,0:T(8,128)S(1)} %get-tuple-element.22), channel_id=1, source_target_pairs={{1,0},{2,1},{3,2},{4,3},{5,4},{6,5},{7,6},{8,7},{9,8},{10,9},{11,1... | collective-permute-start | bytes 221192 | tf_op jit(solution)/shard_map/ppermute | solution.py:528
  14.7 0.7 collective-permute-start.7
  15.3 3.4 %collective-permute-start = (f32[3,184,128]{2,1,0:T(8,128)}, f32[3,184,128]{2,1,0:T(8,128)S(1)}, u32[]{:S(2)}, u32[]{:S(2)}) collective-permute-start(f32[3,184,128]{2,1,0:T(8,128)} %get-tuple-element.19), channel_id=1, source_target_pairs={{16,32},{48,64},{80,96},{112,128},{144,160},{176,192},{208,224},{2... | collective-permute-start | bytes 847880 | tf_op jit(solution)/shard_map/ppermute | solution.py:525
  18.8 3.9 %collective-permute-start.1 = (f32[3,184,128]{2,1,0:T(8,128)S(1)}, f32[3,184,128]{2,1,0:T(8,128)S(1)}, u32[]{:S(2)}, u32[]{:S(2)}) collective-permute-start(f32[3,184,128]{2,1,0:T(8,128)S(1)} %get-tuple-element.20), channel_id=1, source_target_pairs={{0,16},{32,48},{64,80},{96,112},{128,144},{160,176},{192,208},{224... | collective-permute-start | bytes 847880 | tf_op jit(solution)/shard_map/ppermute | solution.py:529
  22.7 15.7 %collective-permute-start.6 = (f32[1,16,128]{2,1,0:T(8,128)S(1)}, f32[1,16,128]{2,1,0:T(8,128)S(1)}, u32[]{:S(2)}, u32[]{:S(2)}) collective-permute-start(f32[1,16,128]{2,1,0:T(8,128)S(1)} %get-tuple-element.27.refs_0_), channel_id=1, source_target_pairs={{0,256},{16,272},{32,288},{48,304},{64,320},{80,336},{96,352},{112... | collective-permute-start | bytes 24584 | tf_op jit(solution)/shard_map/ppermute | solution.py:494
  38.4 0.6 copy-done.8
  39.0 1.5 %corner.1 = (f32[16,384]{1,0:T(8,128)}, f32[16,384]{1,0:T(8,128)}) custom-call(f32[48,384]{1,0:T(8,128)} %copy-done.6, f32[48,384]{1,0:T(8,128)} %copy-done.8, f32[48,128]{1,0:T(8,128)} %copy-done.11), custom_call_target="tpu_custom_call" | custom-call | tf_op jit(solution)/shard_map/corner/pallas_call | solution.py:530
  40.6 0.6 copy-done.33
  41.2 1.4 %join_first.1 = (f32[2,16,128]{2,1,0:T(8,128)}, f32[2,48,128]{2,1,0:T(8,128)}) custom-call(f32[16,384]{1,0:T(8,128)} %get-tuple-element.24.after, f32[1,16,128]{2,1,0:T(8,128)} %copy-done.20, f32[1,16,128]{2,1,0:T(8,128)} %copy-done.33, f32[1,48,128]{2,1,0:T(8,128)} %copy-done.18, f32[1,48,128]{2,1,0:T(8,128)} %copy-done.29), custom_call_target="tpu_custom_call" | custom-call | tf_op jit(solution)/shard_map/join_first/pallas_call | solution.py:513
  42.6 6.5 %collective-permute-start.10 = (f32[2,16,128]{2,1,0:T(8,128)}, f32[2,16,128]{2,1,0:T(8,128)S(1)}, u32[]{:S(2)}, u32[]{:S(2)}) collective-permute-start(f32[2,16,128]{2,1,0:T(8,128)} %get-tuple-element.29.refs_0_), channel_id=1, source_target_pairs={{0,192},{16,208},{32,224},{48,240},{64,128},{80,144},{96,160},{112... | collective-permute-start | bytes 49160 | tf_op jit(solution)/shard_map/ppermute | solution.py:494
  49.1 1.9 %collective-permute-start.9 = (f32[2,16,128]{2,1,0:T(8,128)}, f32[2,16,128]{2,1,0:T(8,128)S(1)}, u32[]{:S(2)}, u32[]{:S(2)}) collective-permute-start(f32[2,16,128]{2,1,0:T(8,128)} %get-tuple-element.29.refs_0_), channel_id=1, source_target_pairs={{0,128},{16,144},{32,160},{48,176},{64,192},{80,208},{96,224},{112... | collective-permute-start | bytes 49160 | tf_op jit(solution)/shard_map/ppermute | solution.py:494
  51.0 2.8 %collective-permute-start.8 = (f32[2,16,128]{2,1,0:T(8,128)}, f32[2,16,128]{2,1,0:T(8,128)S(1)}, u32[]{:S(2)}, u32[]{:S(2)}) collective-permute-start(f32[2,16,128]{2,1,0:T(8,128)} %get-tuple-element.29.refs_0_), channel_id=1, source_target_pairs={{0,64},{16,80},{32,96},{48,112},{64,0},{80,16},{96,32},{112,48},{1... | collective-permute-start | bytes 49160 | tf_op jit(solution)/shard_map/ppermute | solution.py:494
  53.8 0.7 collective-permute-start.13
  54.5 2.0 %collective-permute-done.9.refs_2_ = f32[2,16,128]{2,1,0:T(8,128)S(1)} collective-permute-done((f32[2,16,128]{2,1,0:T(8,128)}, f32[2,16,128]{2,1,0:T(8,128)S(1)}, u32[]{:S(2)}, u32[]{:S(2)}) %collective-permute-start.9) | collective-permute-done | bytes 16416 | tf_op jit(solution)/shard_map/ppermute | solution.py:494
  56.5 0.7 collective-permute-start.12
  57.1 0.7 collective-permute-start.11
  57.9 0.5 copy-done.26
  58.5 0.6 copy-done.28
  59.1 1.6 %join_second.1 = (f32[8,16,128]{2,1,0:T(8,128)}, f32[8,48,128]{2,1,0:T(8,128)}) custom-call(f32[16,384]{1,0:T(8,128)} %get-tuple-element.24.after, f32[2,16,128]{2,1,0:T(8,128)} %get-tuple-element.29.refs_0_, f32[2,16,128]{2,1,0:T(8,128)} %copy-done.32, f32[2,16,128]{2,1,0:T(8,128)} %copy-done.31, f32[2,16,128]{2,1,0:T(8,128)} %copy-done.30, ...), custom_call_target="tpu_custom_call" | custom-call | tf_op jit(solution)/shard_map/join_second/pallas_call | solution.py:513
  60.7 0.7 collective-permute-start.17
  61.4 8.1 %collective-permute-start.16 = (f32[8,16,128]{2,1,0:T(8,128)}, f32[8,16,128]{2,1,0:T(8,128)S(1)}, u32[]{:S(2)}, u32[]{:S(2)}) collective-permute-start(f32[8,16,128]{2,1,0:T(8,128)} %get-tuple-element.31.refs_0_), channel_id=1, source_target_pairs={{0,48},{16,32},{32,16},{48,0},{64,112},{80,96},{96,80},{112,64},{1... | collective-permute-start | bytes 196616 | tf_op jit(solution)/shard_map/ppermute | solution.py:494
  69.5 2.5 %collective-permute-start.5 = (f32[16,384]{1,0:T(8,128)}, f32[16,384]{1,0:T(8,128)S(1)}, u32[]{:S(2)}, u32[]{:S(2)}) collective-permute-start(f32[16,384]{1,0:T(8,128)} %get-tuple-element.25), channel_id=1, source_target_pairs={{0,16},{32,48},{64,80},{96,112},{128,144},{160,176},{192,208},{224... | collective-permute-start | bytes 73736 | tf_op jit(solution)/shard_map/ppermute | solution.py:541
  72.0 3.4 %collective-permute-done.5.cb = f32[16,384]{1,0:T(8,128)S(1)} collective-permute-done((f32[16,384]{1,0:T(8,128)}, f32[16,384]{1,0:T(8,128)S(1)}, u32[]{:S(2)}, u32[]{:S(2)}) %collective-permute-start.5) | collective-permute-done | bytes 24608 | tf_op jit(solution)/shard_map/ppermute | solution.py:541
  75.4 1.9 %collective-permute-start.4 = (f32[16,384]{1,0:T(8,128)}, f32[16,384]{1,0:T(8,128)S(1)}, u32[]{:S(2)}, u32[]{:S(2)}) collective-permute-start(f32[16,384]{1,0:T(8,128)} %get-tuple-element.24.after), channel_id=1, source_target_pairs={{16,32},{48,64},{80,96},{112,128},{144,160},{176,192},{208,224},{2... | collective-permute-start | bytes 73736 | tf_op jit(solution)/shard_map/ppermute | solution.py:540
  77.3 4.0 %collective-permute-done.4.ca = f32[16,384]{1,0:T(8,128)S(1)} collective-permute-done((f32[16,384]{1,0:T(8,128)}, f32[16,384]{1,0:T(8,128)S(1)}, u32[]{:S(2)}, u32[]{:S(2)}) %collective-permute-start.4) | collective-permute-done | bytes 24608 | tf_op jit(solution)/shard_map/ppermute | solution.py:540
  81.3 14.3 %collective-permute-start.15 = (f32[8,16,128]{2,1,0:T(8,128)}, f32[8,16,128]{2,1,0:T(8,128)S(1)}, u32[]{:S(2)}, u32[]{:S(2)}) collective-permute-start(f32[8,16,128]{2,1,0:T(8,128)} %get-tuple-element.31.refs_0_), channel_id=1, source_target_pairs={{0,32},{16,48},{32,0},{48,16},{64,96},{80,112},{96,64},{112,80},{1... | collective-permute-start | bytes 196616 | tf_op jit(solution)/shard_map/ppermute | solution.py:494
  95.6 1.9 %collective-permute-start.14 = (f32[8,16,128]{2,1,0:T(8,128)}, f32[8,16,128]{2,1,0:T(8,128)S(1)}, u32[]{:S(2)}, u32[]{:S(2)}) collective-permute-start(f32[8,16,128]{2,1,0:T(8,128)} %get-tuple-element.31.refs_0_), channel_id=1, source_target_pairs={{0,16},{16,0},{32,48},{48,32},{64,80},{80,64},{96,112},{112,96},{1... | collective-permute-start | bytes 196616 | tf_op jit(solution)/shard_map/ppermute | solution.py:494
  98.1 3.9 %collective-permute-done.14.refs_1_ = f32[8,16,128]{2,1,0:T(8,128)S(1)} collective-permute-done((f32[8,16,128]{2,1,0:T(8,128)}, f32[8,16,128]{2,1,0:T(8,128)S(1)}, u32[]{:S(2)}, u32[]{:S(2)}) %collective-permute-start.14) | collective-permute-done | bytes 65568 | tf_op jit(solution)/shard_map/ppermute | solution.py:494
  102.1 0.9 copy-done.7
  103.0 0.9 copy-done.9
  103.8 0.9 copy-done.10
  104.8 0.7 copy-done.12
  105.5 0.8 copy-done.13
  106.3 9.8 %steps.1 = f32[16,48,384]{2,1,0:T(8,128)} custom-call(s32[2]{0:T(128)S(1)} %copy-done.25, f32[16,48,384]{2,1,0:T(8,128)S(1)} %copy-done.1, f32[16,48,384]{2,1,0:T(8,128)S(1)} %copy-done.3, f32[48,384]{1,0:T(8,128)S(1)} %copy-done.5, f32[3,184,128]{2,1,0:T(8,128)S(1)} %collective-permute-done.ra, f32[3,184,128]{2,1,0:T(8,128)S(1)} %collective-permute-done.1.rb, ...), custom_call_target="tpu_custom_call" | custom-call | tf_op jit(solution)/shard_map/steps/pallas_call | solution.py:549
  (61 shorter events, 0.7 us)
Async XLA Ops:
  0.0 1.3 %copy-start = (f32[16,48,384]{2,1,0:T(8,128)S(1)}, f32[16,48,384]{2,1,0:T(8,128)}, u32[]{:S(2)}) copy-start(f32[16,48,384]{2,1,0:T(8,128)} %state.1) | copy-start | bytes 3538948
  1.3 1.3 %copy-start.2 = (f32[16,48,384]{2,1,0:T(8,128)S(1)}, f32[16,48,384]{2,1,0:T(8,128)}, u32[]{:S(2)}) copy-start(f32[16,48,384]{2,1,0:T(8,128)} %diffuse.1) | copy-start | bytes 3538948
  2.5 0.9 copy-start.4
  3.4 0.7 copy-start.14
  4.1 0.8 copy-start.16
  4.9 0.8 copy-start.17
  5.7 0.7 copy-start.19
  6.5 0.7 copy-start.21
  7.1 0.7 copy-start.22
  7.8 0.7 copy-start.23
  8.5 0.7 copy-start.24
  9.1 92.9 %copy-start.1 = (f32[16,48,384]{2,1,0:T(8,128)S(1)}, f32[16,48,384]{2,1,0:T(8,128)}, u32[]{:S(2)}) copy-start(f32[16,48,384]{2,1,0:T(8,128)} %state.1) | copy-start | bytes 3538948
  9.1 92.9 %copy-start.3 = (f32[16,48,384]{2,1,0:T(8,128)S(1)}, f32[16,48,384]{2,1,0:T(8,128)}, u32[]{:S(2)}) copy-start(f32[16,48,384]{2,1,0:T(8,128)} %diffuse.1) | copy-start | bytes 3538948
  9.1 92.9 %copy-start.5 = (f32[48,384]{1,0:T(8,128)S(1)}, f32[48,384]{1,0:T(8,128)}, u32[]{:S(2)}) copy-start(f32[48,384]{1,0:T(8,128)} %vertical.3) | copy-start | bytes 221188
  9.1 92.9 %copy-start.15 = (f32[2,16,128]{2,1,0:T(8,128)S(1)}, f32[2,16,128]{2,1,0:T(8,128)}, u32[]{:S(2)}) copy-start(f32[2,16,128]{2,1,0:T(8,128)} %fill_we.3) | copy-start | bytes 49156
  9.1 92.9 %copy-start.25 = (s32[2]{0:T(128)S(1)}, s32[2]{0:T(128)}, u32[]{:S(2)}) copy-start(s32[2]{0:T(128)} %jump.1) | copy-start | bytes 28
  11.6 29.0 %copy-start.18 = (f32[1,48,128]{2,1,0:T(8,128)}, f32[1,48,128]{2,1,0:T(8,128)S(1)}, u32[]{:S(2)}) copy-start(f32[1,48,128]{2,1,0:T(8,128)S(1)} %get-tuple-element.28.refs_2_) | copy-start | bytes 73732
  11.6 29.0 %copy-start.20 = (f32[1,16,128]{2,1,0:T(8,128)}, f32[1,16,128]{2,1,0:T(8,128)S(1)}, u32[]{:S(2)}) copy-start(f32[1,16,128]{2,1,0:T(8,128)S(1)} %get-tuple-element.27.refs_0_) | copy-start | bytes 24580
  11.6 11.0 %collective-permute-start.2 = (f32[48,384]{1,0:T(8,128)S(1)}, f32[48,384]{1,0:T(8,128)S(1)}, u32[]{:S(2)}, u32[]{:S(2)}) collective-permute-start(f32[48,384]{1,0:T(8,128)S(1)} %get-tuple-element.21), channel_id=1, source_target_pairs={{0,1},{1,2},{2,3},{3,4},{4,5},{5,6},{6,7},{7,8},{8,9},{9,10},{10,1... | collective-permute-start | bytes 221192 | tf_op jit(solution)/shard_map/ppermute | solution.py:527
  13.4 25.0 %collective-permute-start.3 = (f32[48,384]{1,0:T(8,128)S(1)}, f32[48,384]{1,0:T(8,128)S(1)}, u32[]{:S(2)}, u32[]{:S(2)}) collective-permute-start(f32[48,384]{1,0:T(8,128)S(1)} %get-tuple-element.22), channel_id=1, source_target_pairs={{1,0},{2,1},{3,2},{4,3},{5,4},{6,5},{7,6},{8,7},{9,8},{10,9},{11,1... | collective-permute-start | bytes 221192 | tf_op jit(solution)/shard_map/ppermute | solution.py:528
  14.7 25.9 %collective-permute-start.7 = (f32[1,48,128]{2,1,0:T(8,128)S(1)}, f32[1,48,128]{2,1,0:T(8,128)S(1)}, u32[]{:S(2)}, u32[]{:S(2)}) collective-permute-start(f32[1,48,128]{2,1,0:T(8,128)S(1)} %get-tuple-element.28.refs_2_), channel_id=1, source_target_pairs={{0,8},{1,9},{2,10},{3,11},{4,12},{5,13},{6,14},{7,15},{8,0},{9,1},... | collective-permute-start | bytes 73736 | tf_op jit(solution)/shard_map/ppermute | solution.py:504
  15.3 86.7 %collective-permute-start = (f32[3,184,128]{2,1,0:T(8,128)}, f32[3,184,128]{2,1,0:T(8,128)S(1)}, u32[]{:S(2)}, u32[]{:S(2)}) collective-permute-start(f32[3,184,128]{2,1,0:T(8,128)} %get-tuple-element.19), channel_id=1, source_target_pairs={{16,32},{48,64},{80,96},{112,128},{144,160},{176,192},{208,224},{2... | collective-permute-start | bytes 847880 | tf_op jit(solution)/shard_map/ppermute | solution.py:525
  18.8 83.2 %collective-permute-start.1 = (f32[3,184,128]{2,1,0:T(8,128)S(1)}, f32[3,184,128]{2,1,0:T(8,128)S(1)}, u32[]{:S(2)}, u32[]{:S(2)}) collective-permute-start(f32[3,184,128]{2,1,0:T(8,128)S(1)} %get-tuple-element.20), channel_id=1, source_target_pairs={{0,16},{32,48},{64,80},{96,112},{128,144},{160,176},{192,208},{224... | collective-permute-start | bytes 847880 | tf_op jit(solution)/shard_map/ppermute | solution.py:529
  22.7 15.8 %copy-start.6 = (f32[48,384]{1,0:T(8,128)}, f32[48,384]{1,0:T(8,128)S(1)}, u32[]{:S(2)}) copy-start(f32[48,384]{1,0:T(8,128)S(1)} %collective-permute-done.2.from_low) | copy-start | bytes 221188
  22.7 17.9 %collective-permute-start.6 = (f32[1,16,128]{2,1,0:T(8,128)S(1)}, f32[1,16,128]{2,1,0:T(8,128)S(1)}, u32[]{:S(2)}, u32[]{:S(2)}) collective-permute-start(f32[1,16,128]{2,1,0:T(8,128)S(1)} %get-tuple-element.27.refs_0_), channel_id=1, source_target_pairs={{0,256},{16,272},{32,288},{48,304},{64,320},{80,336},{96,352},{112... | collective-permute-start | bytes 24584 | tf_op jit(solution)/shard_map/ppermute | solution.py:494
  38.4 0.6 copy-start.8
  42.6 11.2 %collective-permute-start.10 = (f32[2,16,128]{2,1,0:T(8,128)}, f32[2,16,128]{2,1,0:T(8,128)S(1)}, u32[]{:S(2)}, u32[]{:S(2)}) collective-permute-start(f32[2,16,128]{2,1,0:T(8,128)} %get-tuple-element.29.refs_0_), channel_id=1, source_target_pairs={{0,192},{16,208},{32,224},{48,240},{64,128},{80,144},{96,160},{112... | collective-permute-start | bytes 49160 | tf_op jit(solution)/shard_map/ppermute | solution.py:494
  49.1 7.3 %collective-permute-start.9 = (f32[2,16,128]{2,1,0:T(8,128)}, f32[2,16,128]{2,1,0:T(8,128)S(1)}, u32[]{:S(2)}, u32[]{:S(2)}) collective-permute-start(f32[2,16,128]{2,1,0:T(8,128)} %get-tuple-element.29.refs_0_), channel_id=1, source_target_pairs={{0,128},{16,144},{32,160},{48,176},{64,192},{80,208},{96,224},{112... | collective-permute-start | bytes 49160 | tf_op jit(solution)/shard_map/ppermute | solution.py:494
  51.0 6.1 %collective-permute-start.8 = (f32[2,16,128]{2,1,0:T(8,128)}, f32[2,16,128]{2,1,0:T(8,128)S(1)}, u32[]{:S(2)}, u32[]{:S(2)}) collective-permute-start(f32[2,16,128]{2,1,0:T(8,128)} %get-tuple-element.29.refs_0_), channel_id=1, source_target_pairs={{0,64},{16,80},{32,96},{48,112},{64,0},{80,16},{96,32},{112,48},{1... | collective-permute-start | bytes 49160 | tf_op jit(solution)/shard_map/ppermute | solution.py:494
  53.8 4.0 %copy-start.30 = (f32[2,16,128]{2,1,0:T(8,128)}, f32[2,16,128]{2,1,0:T(8,128)S(1)}, u32[]{:S(2)}) copy-start(f32[2,16,128]{2,1,0:T(8,128)S(1)} %collective-permute-done.10.refs_3_) | copy-start | bytes 49156
  53.8 4.0 %collective-permute-start.13 = (f32[2,48,128]{2,1,0:T(8,128)}, f32[2,48,128]{2,1,0:T(8,128)S(1)}, u32[]{:S(2)}, u32[]{:S(2)}) collective-permute-start(f32[2,48,128]{2,1,0:T(8,128)} %get-tuple-element.30.refs_4_), channel_id=1, source_target_pairs={{0,6},{1,7},{2,4},{3,5},{4,2},{5,3},{6,0},{7,1},{8,14},{9,15},{10,... | collective-permute-start | bytes 147464 | tf_op jit(solution)/shard_map/ppermute | solution.py:504
  56.5 1.4 %copy-start.31 = (f32[2,16,128]{2,1,0:T(8,128)}, f32[2,16,128]{2,1,0:T(8,128)S(1)}, u32[]{:S(2)}) copy-start(f32[2,16,128]{2,1,0:T(8,128)S(1)} %collective-permute-done.9.refs_2_) | copy-start | bytes 49156
  56.5 1.4 %collective-permute-start.12 = (f32[2,48,128]{2,1,0:T(8,128)}, f32[2,48,128]{2,1,0:T(8,128)S(1)}, u32[]{:S(2)}, u32[]{:S(2)}) collective-permute-start(f32[2,48,128]{2,1,0:T(8,128)} %get-tuple-element.30.refs_4_), channel_id=1, source_target_pairs={{0,4},{1,5},{2,6},{3,7},{4,0},{5,1},{6,2},{7,3},{8,12},{9,13},{10,... | collective-permute-start | bytes 147464 | tf_op jit(solution)/shard_map/ppermute | solution.py:504
  57.1 0.8 copy-start.32
  57.1 0.7 collective-permute-start.11
  57.8 0.6 copy-start.26
  57.8 0.6 copy-start.27
  60.7 41.3 %collective-permute-start.17 = (f32[8,48,128]{2,1,0:T(8,128)}, f32[8,48,128]{2,1,0:T(8,128)S(1)}, u32[]{:S(2)}, u32[]{:S(2)}) collective-permute-start(f32[8,48,128]{2,1,0:T(8,128)} %get-tuple-element.32.refs_4_), channel_id=1, source_target_pairs={{0,1},{1,0},{2,3},{3,2},{4,5},{5,4},{6,7},{7,6},{8,9},{9,8},{10,11... | collective-permute-start | bytes 589832 | tf_op jit(solution)/shard_map/ppermute | solution.py:504
  61.4 34.2 %collective-permute-start.16 = (f32[8,16,128]{2,1,0:T(8,128)}, f32[8,16,128]{2,1,0:T(8,128)S(1)}, u32[]{:S(2)}, u32[]{:S(2)}) collective-permute-start(f32[8,16,128]{2,1,0:T(8,128)} %get-tuple-element.31.refs_0_), channel_id=1, source_target_pairs={{0,48},{16,32},{32,16},{48,0},{64,112},{80,96},{96,80},{112,64},{1... | collective-permute-start | bytes 196616 | tf_op jit(solution)/shard_map/ppermute | solution.py:494
  69.5 5.9 %collective-permute-start.5 = (f32[16,384]{1,0:T(8,128)}, f32[16,384]{1,0:T(8,128)S(1)}, u32[]{:S(2)}, u32[]{:S(2)}) collective-permute-start(f32[16,384]{1,0:T(8,128)} %get-tuple-element.25), channel_id=1, source_target_pairs={{0,16},{32,48},{64,80},{96,112},{128,144},{160,176},{192,208},{224... | collective-permute-start | bytes 73736 | tf_op jit(solution)/shard_map/ppermute | solution.py:541
  75.4 5.9 %collective-permute-start.4 = (f32[16,384]{1,0:T(8,128)}, f32[16,384]{1,0:T(8,128)S(1)}, u32[]{:S(2)}, u32[]{:S(2)}) collective-permute-start(f32[16,384]{1,0:T(8,128)} %get-tuple-element.24.after), channel_id=1, source_target_pairs={{16,32},{48,64},{80,96},{112,128},{144,160},{176,192},{208,224},{2... | collective-permute-start | bytes 73736 | tf_op jit(solution)/shard_map/ppermute | solution.py:540
  81.3 16.7 %collective-permute-start.15 = (f32[8,16,128]{2,1,0:T(8,128)}, f32[8,16,128]{2,1,0:T(8,128)S(1)}, u32[]{:S(2)}, u32[]{:S(2)}) collective-permute-start(f32[8,16,128]{2,1,0:T(8,128)} %get-tuple-element.31.refs_0_), channel_id=1, source_target_pairs={{0,32},{16,48},{32,0},{48,16},{64,96},{80,112},{96,64},{112,80},{1... | collective-permute-start | bytes 196616 | tf_op jit(solution)/shard_map/ppermute | solution.py:494
  95.6 6.4 %collective-permute-start.14 = (f32[8,16,128]{2,1,0:T(8,128)}, f32[8,16,128]{2,1,0:T(8,128)S(1)}, u32[]{:S(2)}, u32[]{:S(2)}) collective-permute-start(f32[8,16,128]{2,1,0:T(8,128)} %get-tuple-element.31.refs_0_), channel_id=1, source_target_pairs={{0,16},{16,0},{32,48},{48,32},{64,80},{80,64},{96,112},{112,96},{1... | collective-permute-start | bytes 196616 | tf_op jit(solution)/shard_map/ppermute | solution.py:494
  102.1 0.9 copy-start.7
  102.9 0.9 copy-start.9
  103.8 0.9 copy-start.10
  104.8 0.7 copy-start.12
  105.5 0.8 copy-start.13
  (4 other events, 2.4 us)

commit v3 on v2

--- a/solution.py
+++ b/solution.py
@@ -17,6 +17,8 @@
 COEF_AT = LV * STATE_ROWS
 VERT_AT = COEF_AT + LV * COEF_ROWS
 XROWS = 184
+CORNER_AT = NG * XROWS
+SENT = CORNER_AT + 16 * NG
 
 
 def rounds_of(count):
@@ -35,25 +37,40 @@
 
 
 def pack_kernel(
-    state_hbm, diffuse_hbm, vertical, rows_we, rows_sn, fill_we, fill_sn, index_we, weight_we, index_sn, weight_sn,
-    xa, xb, y_low, y_high, chain_x, chain_y, colpack, interp, state, diffuse, square, sem,
+    state_hbm, diffuse_hbm, vertical_hbm, rows_we_hbm, rows_sn_hbm, fill_we_hbm, fill_sn_hbm,
+    index_we_hbm, weight_we_hbm, index_sn_hbm, weight_sn_hbm,
+    y_low, y_high, chain_x, chain_y, colpack, interp,
+    state, diffuse, vertical, rows_we, rows_sn, fill_we, fill_sn, index_we, weight_we, index_sn, weight_sn,
+    square, sem,
 ):
-    copies = [
-        pltpu.make_async_copy(state_hbm, state, sem.at[0]),
-        pltpu.make_async_copy(diffuse_hbm, diffuse, sem.at[1]),
+    nx, ny = lax.axis_index("nx"), lax.axis_index("ny")
+    side_x = jnp.where(ny == 0, 0, 1)
+    side_y = jnp.where(nx == 0, 0, 1)
+    pairs = [
+        (rows_we_hbm.at[:, side_y], rows_we),
+        (rows_sn_hbm.at[:, side_x], rows_sn),
+        (fill_we_hbm, fill_we),
+        (fill_sn_hbm, fill_sn),
+        (index_we_hbm, index_we),
+        (weight_we_hbm, weight_we),
+        (index_sn_hbm, index_sn),
+        (weight_sn_hbm, weight_sn),
+        (vertical_hbm, vertical),
     ]
+    for src, dst in ((state_hbm, state), (diffuse_hbm, diffuse)):
+        for at, group in enumerate((0, NG - 1)):
+            pairs.append((src.at[:, :, pl.ds(128 * group, 128)], dst.at[at]))
+    copies = [pltpu.make_async_copy(src, dst, sem.at[n]) for n, (src, dst) in enumerate(pairs)]
     for copy in copies:
         copy.start()
-    nx, ny = lax.axis_index("nx"), lax.axis_index("ny")
-    odd = nx % 2 == 1
-
-    side_x = jnp.where(ny == 0, 0, 1)
-    side_y = jnp.where(nx == 0, 0, 1)
     lane = lax.broadcasted_iota(jnp.int32, (128, 128), 1)
     square[...] = jnp.zeros((128, 128), jnp.float32)
+    interp[...] = jnp.zeros((8, WY), jnp.float32)
+    for copy in copies[:8]:
+        copy.wait()
     for step in range(3):
-        chain_y[0, 16 * step : 16 * step + 16, :] = rows_we[step, side_y]
-        square[16 * step : 16 * step + 16, 0:16] = rows_sn[step, side_x]
+        chain_y[0, 16 * step : 16 * step + 16, :] = rows_we[step]
+        square[16 * step : 16 * step + 16, 0:16] = rows_sn[step]
     chain_x[0] = square[...].T[0:16]
     square[0:48, :] = jnp.zeros((48, 128), jnp.float32)
     square[96:112, 0:16] = fill_sn[0]
@@ -64,46 +81,21 @@
     row = lax.broadcasted_iota(jnp.int32, (128, 128), 0)
     whole = jnp.where((lane < 8) | (row < 96), whole, pltpu.roll(whole, 32, 1))
     colpack[...] = whole.T[0:WX]
-    interp[...] = jnp.zeros((8, WY), jnp.float32)
     interp[0:1, :] = index_we[...].astype(jnp.float32).reshape(1, WY)
     interp[1:2, :] = weight_we[...].reshape(1, WY)
     square[0:16, :] = fill_we[0]
     square[16:32, :] = fill_we[1]
-
-    def rows(ref, high):
-        at = WX - STATE_ROWS if high else 0
-        bt = WX - COEF_ROWS if high else 0
-        for l in range(NG):
-            lanes = slice(128 * l, 128 * l + 128)
-            for k in range(LV):
-                ref[l, k * STATE_ROWS : (k + 1) * STATE_ROWS, :] = state[k, at : at + STATE_ROWS, lanes]
-                ref[l, COEF_AT + k * COEF_ROWS : COEF_AT + (k + 1) * COEF_ROWS, :] = diffuse[
-                    k, bt : bt + COEF_ROWS, lanes
-                ]
-            ref[l, VERT_AT : VERT_AT + COEF_ROWS, :] = vertical[bt : bt + COEF_ROWS, lanes]
-            ref[l, VERT_AT + COEF_ROWS :, :] = jnp.zeros((XROWS - VERT_AT - COEF_ROWS, 128), jnp.float32)
-
-    for copy in copies:
+    for copy in copies[8:]:
         copy.wait()
-
-    @pl.when(odd)
-    def _():
-        rows(xa, True)
-        rows(xb, False)
-
-    @pl.when(jnp.logical_not(odd))
-    def _():
-        rows(xa, False)
-        rows(xb, True)
 
     lane = lax.broadcasted_iota(jnp.int32, (WX, 128), 1)
     row = lax.broadcasted_iota(jnp.int32, (WX, 128), 0)
-    for ref, group, first in ((y_low, 0, 0), (y_high, NG - 1, 120)):
+    for at, (ref, group, first) in enumerate(((y_low, 0, 0), (y_high, NG - 1, 120))):
         lanes = slice(128 * group, 128 * group + 128)
         for which, field in enumerate((state, diffuse)):
             total = jnp.zeros((WX, 128), jnp.float32)
             for k in range(LV):
-                part = pltpu.roll(field[k, :, lanes], (8 * k - first) % 128, 1)
+                part = pltpu.roll(field[at, k], (8 * k - first) % 128, 1)
                 total = jnp.where((lane >= 8 * k) & (lane < 8 * k + 8), part, total)
             ref[:, 128 * which : 128 * which + 128] = total
         last = jnp.where(lane < 8, pltpu.roll(vertical[:, lanes], (-first) % 128, 1), 0.0)
@@ -117,24 +109,53 @@
         ref[:, 256:384] = last
 
 
-def corner_kernel(from_low, from_high, colpack, ca, cb):
+def border_kernel(
+    state_hbm, diffuse_hbm, vertical_hbm, from_low, from_high, colpack, xa, xb, state, diffuse, vertical, sem
+):
+    copies = [pltpu.make_async_copy(vertical_hbm, vertical, sem.at[4])]
+    for n, (src, dst) in enumerate(((state_hbm, state), (diffuse_hbm, diffuse))):
+        for side in range(2):
+            copies.append(
+                pltpu.make_async_copy(src.at[:, pl.ds(40 * side, 8), :], dst.at[side], sem.at[2 * n + side])
+            )
+    for copy in copies:
+        copy.start()
     odd = lax.axis_index("nx") % 2 == 1
     clear = lax.broadcasted_iota(jnp.int32, (8, 128), 1) < 64
-
-    def rows(ref, at):
-        ref[0:8, 0:256] = from_low[at : at + 8, 0:256]
-        ref[0:8, 256:384] = jnp.where(clear, from_low[at : at + 8, 256:384], colpack[at : at + 8, :])
-        ref[8:16, :] = from_high[at : at + 8, :]
+    for copy in copies:
+        copy.wait()
+
+    def rows(ref, side):
+        at = 8 - STATE_ROWS if side else 0
+        bt = 8 - COEF_ROWS if side else 0
+        for l in range(NG):
+            lanes = slice(128 * l, 128 * l + 128)
+            base = XROWS * l
+            for k in range(LV):
+                n = base + k * STATE_ROWS
+                ref[n : n + STATE_ROWS, :] = state[side, k, at : at + STATE_ROWS, lanes]
+                n = base + COEF_AT + k * COEF_ROWS
+                ref[n : n + COEF_ROWS, :] = diffuse[side, k, bt : bt + COEF_ROWS, lanes]
+            n = base + VERT_AT
+            ref[n : n + COEF_ROWS, :] = vertical[40 * side + bt : 40 * side + bt + COEF_ROWS, lanes]
+            ref[n + COEF_ROWS : base + XROWS, :] = jnp.zeros((XROWS - VERT_AT - COEF_ROWS, 128), jnp.float32)
+        for which, strips in enumerate((from_low, from_high)):
+            for l in range(NG):
+                part = strips[40 * side : 40 * side + 8, 128 * l : 128 * l + 128]
+                if which == 0 and l == NG - 1:
+                    part = jnp.where(clear, part, colpack[40 * side : 40 * side + 8, :])
+                n = CORNER_AT + 8 * (NG * which + l)
+                ref[n : n + 8, :] = part
 
     @pl.when(odd)
     def _():
-        rows(ca, 40)
-        rows(cb, 0)
+        rows(xa, 1)
+        rows(xb, 0)
 
     @pl.when(jnp.logical_not(odd))
     def _():
-        rows(ca, 0)
-        rows(cb, 40)
+        rows(xa, 0)
+        rows(xb, 1)
 
 
 def join_kernel(count_x, count_y, after, *refs):
@@ -147,12 +168,12 @@
 
 
 def main_kernel(
-    count_x, count_y, plan_x, plan_y, jump, state, diffuse, vertical, ra, rb, from_low, from_high, ca, cb,
-    colpack, interp, fill_we, *refs,
+    count_x, count_y, plan_x, plan_y, jump, state, diffuse, vertical_hbm, fill_we_hbm, ra, rb, from_low, from_high,
+    colpack, interp, *refs,
 ):
     chain_x, refs = refs[: len(plan_x)], refs[len(plan_x) :]
     chain_y, refs = refs[: len(plan_y)], refs[len(plan_y) :]
-    out, es, ed, ev, mv, gv, fac, strip, ey, ex, pack, sem = refs
+    out, es, ed, ev, mv, gv, fac, strip, ey, ex, pack, vertical, fill_we, sem = refs
     dx, dy = jump[0], jump[1]
     nx, ny = lax.axis_index("nx"), lax.axis_index("ny")
     copies = []
@@ -163,14 +184,22 @@
             )
             copy.start()
             copies.append(copy)
+    first_copies = [
+        pltpu.make_async_copy(vertical_hbm, vertical, sem.at[2 * NG]),
+        pltpu.make_async_copy(fill_we_hbm, fill_we, sem.at[2 * NG + 1]),
+    ]
+    for copy in first_copies:
+        copy.start()
     odd = nx % 2 == 1
     lane = lax.broadcasted_iota(jnp.int32, (8, 128), 1)
     lane64 = lax.broadcasted_iota(jnp.int32, (64, 128), 1)
 
     def beyond(at, size, l):
-        a, b = ra[l, at : at + size, :], rb[l, at : at + size, :]
+        a, b = ra[XROWS * l + at : XROWS * l + at + size, :], rb[XROWS * l + at : XROWS * l + at + size, :]
         return jnp.where(odd, b, a), jnp.where(odd, a, b)
 
+    for copy in first_copies:
+        copy.wait()
     for l in range(NG):
         for k in range(LV):
             low, high = beyond(k * STATE_ROWS, STATE_ROWS, l)
@@ -184,15 +213,21 @@
         ev[l, HX + WX : HX + WX + COEF_ROWS, :] = high
         ev[l, HX : HX + WX, :] = vertical[:, 128 * l : 128 * l + 128]
 
-    low = jnp.where(odd, cb[...], ca[...])
-    high = jnp.where(odd, ca[...], cb[...])
+    def corner(side, l):
+        n = CORNER_AT + 8 * (NG * side + l)
+        a, b = ra[n : n + 8, :], rb[n : n + 8, :]
+        return jnp.where(odd, b, a), jnp.where(odd, a, b)
+
     for side, ref in enumerate((from_low, from_high)):
-        strip[side, 0:HX, :] = low[8 * side : 8 * side + 8]
         strip[side, HX : HX + WX, :] = ref[...]
-        strip[side, HX + WX : 64, :] = high[8 * side : 8 * side + 8]
-    pack[0:HX, :] = low[0:8, 256:384]
+        for l in range(NG):
+            low, high = corner(side, l)
+            strip[side, 0:HX, 128 * l : 128 * l + 128] = low
+            strip[side, HX + WX : 64, 128 * l : 128 * l + 128] = high
+    low, high = corner(0, NG - 1)
+    pack[0:HX, :] = low
     pack[HX : HX + WX, :] = colpack[...]
-    pack[HX + WX : 64, :] = high[0:8, 256:384]
+    pack[HX + WX : 64, :] = high
     for which, dst in enumerate((es, ed)):
         lanes = slice(128 * which, 128 * which + 128)
         for k in range(LV):
@@ -452,16 +487,15 @@
     both = ("nx", "ny")
     vmem = pl.BlockSpec(memory_space=pltpu.VMEM)
     smem = pl.BlockSpec(memory_space=pltpu.SMEM)
-    hbm = pl.BlockSpec(memory_space=pl.ANY)
+    hbm = pl.BlockSpec(memory_space=pltpu.HBM)
+    any_ = pl.BlockSpec(memory_space=pl.ANY)
 
     def shape(*dims):
         return jax.ShapeDtypeStruct(dims, f32)
 
-    xa, xb, y_low, y_high, chain_x, chain_y, colpack, interp = pl.pallas_call(
+    y_low, y_high, chain_x, chain_y, colpack, interp = pl.pallas_call(
         pack_kernel,
         out_shape=(
-            shape(NG, XROWS, 128),
-            shape(NG, XROWS, 128),
             shape(WX, WY),
             shape(WX, WY),
             shape(1, 16, 128),
@@ -469,13 +503,22 @@
             shape(WX, 128),
             shape(8, WY),
         ),
-        in_specs=[hbm] * 2 + [vmem] * 9,
-        out_specs=(vmem,) * 8,
+        in_specs=[hbm] * 11,
+        out_specs=(vmem,) * 6,
         scratch_shapes=[
-            pltpu.VMEM((LV, WX, WY), f32),
-            pltpu.VMEM((LV, WX, WY), f32),
+            pltpu.VMEM((2, LV, WX, 128), f32),
+            pltpu.VMEM((2, LV, WX, 128), f32),
+            pltpu.VMEM((WX, WY), f32),
+            pltpu.VMEM((3, 16, 128), f32),
+            pltpu.VMEM((3, 16, 16), f32),
+            pltpu.VMEM((2, 16, 128), f32),
+            pltpu.VMEM((2, 16, 16), f32),
+            pltpu.VMEM((WY,), jnp.int32),
+            pltpu.VMEM((WY,), f32),
+            pltpu.VMEM((WX,), jnp.int32),
+            pltpu.VMEM((WX,), f32),
             pltpu.VMEM((128, 128), f32),
-            pltpu.SemaphoreType.DMA((2,)),
+            pltpu.SemaphoreType.DMA((13,)),
         ],
         compiler_params=pltpu.CompilerParams(vmem_limit_bytes=40 << 20),
         name="pack",
@@ -516,30 +559,34 @@
                 shape(sum(p.shape[0] for p in parts_x), 16, 128),
                 shape(sum(p.shape[0] for p in parts_y), 48, 128),
             ),
-            in_specs=[hbm] + [vmem] * (len(parts_x) + len(parts_y)),
+            in_specs=[any_] + [vmem] * (len(parts_x) + len(parts_y)),
             out_specs=(vmem, vmem),
             name=name,
         )(after, *parts_x, *parts_y)
 
     parts_x = [chain_x] + along_x(chain_x, rounds_x[0])
-    ra = lax.ppermute(xa, "nx", pairs_a)
     parts_y = [chain_y] + along_y(chain_y, rounds_y[0])
     from_low = lax.ppermute(y_high, "ny", up)
     from_high = lax.ppermute(y_low, "ny", down)
+    xa, xb = pl.pallas_call(
+        border_kernel,
+        out_shape=(shape(SENT, 128), shape(SENT, 128)),
+        in_specs=[hbm] * 3 + [vmem] * 3,
+        out_specs=(vmem, vmem),
+        scratch_shapes=[
+            pltpu.VMEM((2, LV, 8, WY), f32),
+            pltpu.VMEM((2, LV, 8, WY), f32),
+            pltpu.VMEM((WX, WY), f32),
+            pltpu.SemaphoreType.DMA((5,)),
+        ],
+        name="border",
+    )(state, diffuse, vertical, from_low, from_high, colpack)
+    ra = lax.ppermute(xa, "nx", pairs_a)
     rb = lax.ppermute(xb, "nx", pairs_b)
-    ca, cb = pl.pallas_call(
-        corner_kernel,
-        out_shape=(shape(16, WY), shape(16, WY)),
-        in_specs=[vmem] * 3,
-        out_specs=(vmem, vmem),
-        name="corner",
-    )(from_low, from_high, colpack)
-    chain_x, chain_y = join(ca, parts_x, parts_y, "join_first")
+    chain_x, chain_y = join(xa, parts_x, parts_y, "join_first")
     parts_x = [chain_x] + along_x(chain_x, rounds_x[1])
     parts_y = [chain_y] + along_y(chain_y, rounds_y[1])
-    ra2 = lax.ppermute(ca, "nx", pairs_a)
-    rb2 = lax.ppermute(cb, "nx", pairs_b)
-    chain_x, chain_y = join(ca, parts_x, parts_y, "join_second")
+    chain_x, chain_y = join(xa, parts_x, parts_y, "join_second")
     parts_x = [chain_x] + along_x(chain_x, rounds_x[2])
     parts_y = [chain_y] + along_y(chain_y, rounds_y[2])
     have_x, have_y = masks_of(rounds_x[:2]), masks_of(rounds_y[:2])
@@ -549,7 +596,7 @@
     return pl.pallas_call(
         functools.partial(main_kernel, count_x, count_y, plan_x, plan_y),
         out_shape=shape(LV, WX, WY),
-        in_specs=[smem, hbm, hbm] + [vmem] * (10 + len(parts_x) + len(parts_y)),
+        in_specs=[smem] + [hbm] * 4 + [vmem] * (6 + len(parts_x) + len(parts_y)),
         out_specs=vmem,
         scratch_shapes=[
             pltpu.VMEM((LV, NG + 1, 72, 128), f32),
@@ -562,13 +609,15 @@
             pltpu.VMEM((NG + 1, 48, 128), f32),
             pltpu.VMEM((64, 128), f32),
             pltpu.VMEM((64, 128), f32),
-            pltpu.SemaphoreType.DMA((2 * NG,)),
+            pltpu.VMEM((WX, WY), f32),
+            pltpu.VMEM((2, 16, 128), f32),
+            pltpu.SemaphoreType.DMA((2 * NG + 2,)),
         ],
         compiler_params=pltpu.CompilerParams(vmem_limit_bytes=48 << 20),
         name="steps",
     )(
-        jump, state, diffuse, vertical, ra, rb, from_low, from_high, ra2, rb2,
-        colpack, interp, fill_we, *parts_x, *parts_y,
+        jump, state, diffuse, vertical, fill_we, ra, rb, from_low, from_high,
+        colpack, interp, *parts_x, *parts_y,
     )
 
 

time: 117 us -> 108 us (0.923)
  the two profiles are of different devices: /device:TPU:26 before, /device:TPU:2 now
where the time goes in v3:
time: 108 us; the launch traced here: 107 us
  starting transfers between devices  62.6 us (58%)
  Pallas kernels  17.2 us (16%)
  local copies, waits for them, and re-layouts  16.3 us (15%)
  waiting for transfers between devices  10.1 us (9%)
    ppermute x7, starting transfers between devices, along_x(): lax.ppermute(chain, both, [(i * count_y + n, (i ^ m) * count_y + n) for n...  48.7 us
    unnamed x68, local copies, waits for them, and re-layouts  16.3 us
    pallas_call x1, Pallas kernels, on_device(): pl.pallas_call(functools.partial(main_kernel, count_x, count_y, plan_x, p...  9.91 us
    ppermute x7, waiting for transfers between devices, along_x(): lax.ppermute(chain, both, [(i * count_y + n, (i ^ m) * count_y + n) for n...  6.53 us
    ppermute x1, starting transfers between devices, on_device(): rb = lax.ppermute(xb, 'nx', pairs_b)  5.67 us
    ppermute x1, waiting for transfers between devices, on_device(): from_high = lax.ppermute(y_low, 'ny', down)  3.54 us
    ppermute x5, starting transfers between devices, along_y(): lax.ppermute(chain, both, [(n * count_y + j, n * count_y + (j ^ m)) for n...  3.29 us
    pallas_call x1, Pallas kernels, on_device(): pl.pallas_call(border_kernel, out_shape=(shape(SENT, 128), shape(SENT, 12...  3.26 us
  transfers between devices with their start and end apart: 16, of which 5 were waited for; matrix products, arithmetic and copies ran while one was open for 0% of the time, Pallas kernels for 3%

profile of v3, /device:TPU:2, one launch (start us, length us, event | category | flops | bytes accessed | tf_op | source)
XLA Modules:
  0.0 106.6 jit_solution(5611402158401620670)
XLA Ops:
  0.0 1.3 %copy-done = f32[16,48,384]{2,1,0:T(8,128)S(1)} copy-done((f32[16,48,384]{2,1,0:T(8,128)S(1)}, f32[16,48,384]{2,1,0:T(8,128)}, u32[]{:S(2)}) %copy-start) | copy-done | bytes 1179672
  1.3 1.3 %copy-done.2 = f32[16,48,384]{2,1,0:T(8,128)S(1)} copy-done((f32[16,48,384]{2,1,0:T(8,128)S(1)}, f32[16,48,384]{2,1,0:T(8,128)}, u32[]{:S(2)}) %copy-start.2) | copy-done | bytes 1179672
  2.5 0.9 copy-done.4
  3.4 0.7 copy-done.14
  4.1 0.8 copy-done.16
  4.9 0.8 copy-done.17
  5.7 0.7 copy-done.19
  6.5 0.7 copy-done.21
  7.1 0.7 copy-done.22
  7.8 0.7 copy-done.23
  8.5 0.7 copy-done.24
  9.1 1.0 pack.1
  10.1 0.6 copy-done.11
  10.8 1.7 %collective-permute-start = (f32[48,384]{1,0:T(8,128)S(1)}, f32[48,384]{1,0:T(8,128)S(1)}, u32[]{:S(2)}, u32[]{:S(2)}) collective-permute-start(f32[48,384]{1,0:T(8,128)S(1)} %get-tuple-element.17), channel_id=1, source_target_pairs={{0,1},{1,2},{2,3},{3,4},{4,5},{5,6},{6,7},{7,8},{8,9},{9,10},{10,1... | collective-permute-start | bytes 221192 | tf_op jit(solution)/shard_map/ppermute | solution.py:569
  12.5 1.3 %collective-permute-start.1 = (f32[48,384]{1,0:T(8,128)S(1)}, f32[48,384]{1,0:T(8,128)S(1)}, u32[]{:S(2)}, u32[]{:S(2)}) collective-permute-start(f32[48,384]{1,0:T(8,128)S(1)} %get-tuple-element.18), channel_id=1, source_target_pairs={{1,0},{2,1},{3,2},{4,3},{5,4},{6,5},{7,6},{8,7},{9,8},{10,9},{11,1... | collective-permute-start | bytes 221192 | tf_op jit(solution)/shard_map/ppermute | solution.py:570
  13.8 3.5 %collective-permute-done.1.from_high = f32[48,384]{1,0:T(8,128)S(1)} collective-permute-done((f32[48,384]{1,0:T(8,128)S(1)}, f32[48,384]{1,0:T(8,128)S(1)}, u32[]{:S(2)}, u32[]{:S(2)}) %collective-permute-start.1) | collective-permute-done | bytes 73760 | tf_op jit(solution)/shard_map/ppermute | solution.py:570
  17.4 0.6 copy-done.8
  18.0 3.3 %border.1 = (f32[600,128]{1,0:T(8,128)}, f32[600,128]{1,0:T(8,128)}) custom-call(f32[16,48,384]{2,1,0:T(8,128)} %state.1, f32[16,48,384]{2,1,0:T(8,128)} %diffuse.1, f32[48,384]{1,0:T(8,128)} %vertical_hbm.5, f32[48,384]{1,0:T(8,128)} %copy-done.6, f32[48,384]{1,0:T(8,128)} %copy-done.8, f32[48,128]{1,0:T(8,128)} %copy-done.11), custom_call_target="tpu_custom_call" | custom-call | tf_op jit(solution)/shard_map/border/pallas_call | solution.py:571
  21.3 5.7 %collective-permute-start.3 = (f32[600,128]{1,0:T(8,128)}, f32[600,128]{1,0:T(8,128)S(1)}, u32[]{:S(2)}, u32[]{:S(2)}) collective-permute-start(f32[600,128]{1,0:T(8,128)} %get-tuple-element.21), channel_id=1, source_target_pairs={{0,16},{32,48},{64,80},{96,112},{128,144},{160,176},{192,208},{224... | collective-permute-start | bytes 921608 | tf_op jit(solution)/shard_map/ppermute | solution.py:585
  27.0 1.9 %collective-permute-start.2 = (f32[600,128]{1,0:T(8,128)}, f32[600,128]{1,0:T(8,128)S(1)}, u32[]{:S(2)}, u32[]{:S(2)}) collective-permute-start(f32[600,128]{1,0:T(8,128)} %get-tuple-element.20.after), channel_id=1, source_target_pairs={{16,32},{48,64},{80,96},{112,128},{144,160},{176,192},{208,224},{2... | collective-permute-start | bytes 921608 | tf_op jit(solution)/shard_map/ppermute | solution.py:584
  28.9 0.7 collective-permute-start.5
  29.6 13.7 %collective-permute-start.4 = (f32[1,16,128]{2,1,0:T(8,128)S(1)}, f32[1,16,128]{2,1,0:T(8,128)S(1)}, u32[]{:S(2)}, u32[]{:S(2)}) collective-permute-start(f32[1,16,128]{2,1,0:T(8,128)S(1)} %get-tuple-element.23.refs_0_), channel_id=1, source_target_pairs={{0,256},{16,272},{32,288},{48,304},{64,320},{80,336},{96,352},{112... | collective-permute-start | bytes 24584 | tf_op jit(solution)/shard_map/ppermute | solution.py:537
  43.3 1.6 %collective-permute-done.4.refs_1_ = f32[1,16,128]{2,1,0:T(8,128)S(1)} collective-permute-done((f32[1,16,128]{2,1,0:T(8,128)S(1)}, f32[1,16,128]{2,1,0:T(8,128)S(1)}, u32[]{:S(2)}, u32[]{:S(2)}) %collective-permute-start.4) | collective-permute-done | bytes 8224 | tf_op jit(solution)/shard_map/ppermute | solution.py:537
  45.0 0.6 copy-done.33
  45.5 0.6 copy-done.29
  46.1 1.4 %join_first.1 = (f32[2,16,128]{2,1,0:T(8,128)}, f32[2,48,128]{2,1,0:T(8,128)}) custom-call(f32[600,128]{1,0:T(8,128)} %get-tuple-element.20.after, f32[1,16,128]{2,1,0:T(8,128)} %copy-done.20, f32[1,16,128]{2,1,0:T(8,128)} %copy-done.33, f32[1,48,128]{2,1,0:T(8,128)} %copy-done.18, f32[1,48,128]{2,1,0:T(8,128)} %copy-done.29), custom_call_target="tpu_custom_call" | custom-call | tf_op jit(solution)/shard_map/join_first/pallas_call | solution.py:556
  47.5 4.9 %collective-permute-start.8 = (f32[2,16,128]{2,1,0:T(8,128)}, f32[2,16,128]{2,1,0:T(8,128)S(1)}, u32[]{:S(2)}, u32[]{:S(2)}) collective-permute-start(f32[2,16,128]{2,1,0:T(8,128)} %get-tuple-element.25.refs_0_), channel_id=1, source_target_pairs={{0,192},{16,208},{32,224},{48,240},{64,128},{80,144},{96,160},{112... | collective-permute-start | bytes 49160 | tf_op jit(solution)/shard_map/ppermute | solution.py:537
  52.5 2.5 %collective-permute-start.7 = (f32[2,16,128]{2,1,0:T(8,128)}, f32[2,16,128]{2,1,0:T(8,128)S(1)}, u32[]{:S(2)}, u32[]{:S(2)}) collective-permute-start(f32[2,16,128]{2,1,0:T(8,128)} %get-tuple-element.25.refs_0_), channel_id=1, source_target_pairs={{0,128},{16,144},{32,160},{48,176},{64,192},{80,208},{96,224},{112... | collective-permute-start | bytes 49160 | tf_op jit(solution)/shard_map/ppermute | solution.py:537
  55.0 2.4 %collective-permute-start.6 = (f32[2,16,128]{2,1,0:T(8,128)}, f32[2,16,128]{2,1,0:T(8,128)S(1)}, u32[]{:S(2)}, u32[]{:S(2)}) collective-permute-start(f32[2,16,128]{2,1,0:T(8,128)} %get-tuple-element.25.refs_0_), channel_id=1, source_target_pairs={{0,64},{16,80},{32,96},{48,112},{64,0},{80,16},{96,32},{112,48},{1... | collective-permute-start | bytes 49160 | tf_op jit(solution)/shard_map/ppermute | solution.py:537
  57.4 0.7 collective-permute-start.11
  58.1 1.7 %collective-permute-done.7.refs_2_ = f32[2,16,128]{2,1,0:T(8,128)S(1)} collective-permute-done((f32[2,16,128]{2,1,0:T(8,128)}, f32[2,16,128]{2,1,0:T(8,128)S(1)}, u32[]{:S(2)}, u32[]{:S(2)}) %collective-permute-start.7) | collective-permute-done | bytes 16416 | tf_op jit(solution)/shard_map/ppermute | solution.py:537
  59.8 0.7 collective-permute-start.10
  60.5 0.4 collective-permute-done.6.refs_1_
  60.8 0.7 collective-permute-start.9
  61.6 0.5 copy-done.26
  62.1 0.0 copy-done.27
  62.2 0.6 copy-done.28
  62.8 1.6 %join_second.1 = (f32[8,16,128]{2,1,0:T(8,128)}, f32[8,48,128]{2,1,0:T(8,128)}) custom-call(f32[600,128]{1,0:T(8,128)} %get-tuple-element.20.after, f32[2,16,128]{2,1,0:T(8,128)} %get-tuple-element.25.refs_0_, f32[2,16,128]{2,1,0:T(8,128)} %copy-done.32, f32[2,16,128]{2,1,0:T(8,128)} %copy-done.31, f32[2,16,128]{2,1,0:T(8,128)} %copy-done.30, ...), custom_call_target="tpu_custom_call" | custom-call | tf_op jit(solution)/shard_map/join_second/pallas_call | solution.py:556
  64.4 0.7 collective-permute-start.15
  65.1 1.9 %collective-permute-start.14 = (f32[8,16,128]{2,1,0:T(8,128)}, f32[8,16,128]{2,1,0:T(8,128)S(1)}, u32[]{:S(2)}, u32[]{:S(2)}) collective-permute-start(f32[8,16,128]{2,1,0:T(8,128)} %get-tuple-element.27.refs_0_), channel_id=1, source_target_pairs={{0,48},{16,32},{32,16},{48,0},{64,112},{80,96},{96,80},{112,64},{1... | collective-permute-start | bytes 196616 | tf_op jit(solution)/shard_map/ppermute | solution.py:537
  67.0 19.7 %collective-permute-start.13 = (f32[8,16,128]{2,1,0:T(8,128)}, f32[8,16,128]{2,1,0:T(8,128)S(1)}, u32[]{:S(2)}, u32[]{:S(2)}) collective-permute-start(f32[8,16,128]{2,1,0:T(8,128)} %get-tuple-element.27.refs_0_), channel_id=1, source_target_pairs={{0,32},{16,48},{32,0},{48,16},{64,96},{80,112},{96,64},{112,80},{1... | collective-permute-start | bytes 196616 | tf_op jit(solution)/shard_map/ppermute | solution.py:537
  86.7 3.6 %collective-permute-start.12 = (f32[8,16,128]{2,1,0:T(8,128)}, f32[8,16,128]{2,1,0:T(8,128)S(1)}, u32[]{:S(2)}, u32[]{:S(2)}) collective-permute-start(f32[8,16,128]{2,1,0:T(8,128)} %get-tuple-element.27.refs_0_), channel_id=1, source_target_pairs={{0,16},{16,0},{32,48},{48,32},{64,80},{80,64},{96,112},{112,96},{1... | collective-permute-start | bytes 196616 | tf_op jit(solution)/shard_map/ppermute | solution.py:537
  90.3 2.8 %collective-permute-done.12.refs_1_ = f32[8,16,128]{2,1,0:T(8,128)S(1)} collective-permute-done((f32[8,16,128]{2,1,0:T(8,128)}, f32[8,16,128]{2,1,0:T(8,128)S(1)}, u32[]{:S(2)}, u32[]{:S(2)}) %collective-permute-start.12) | collective-permute-done | bytes 65568 | tf_op jit(solution)/shard_map/ppermute | solution.py:537
  93.2 0.9 copy-done.7
  94.1 0.9 copy-done.9
  95.0 0.9 copy-done.10
  95.9 0.8 copy-done.13
  96.7 9.9 %steps.1 = f32[16,48,384]{2,1,0:T(8,128)} custom-call(s32[2]{0:T(128)S(1)} %copy-done.25, f32[16,48,384]{2,1,0:T(8,128)S(1)} %copy-done.1, f32[16,48,384]{2,1,0:T(8,128)S(1)} %copy-done.3, f32[48,384]{1,0:T(8,128)S(1)} %copy-done.5, f32[2,16,128]{2,1,0:T(8,128)S(1)} %copy-done.15, f32[600,128]{1,0:T(8,128)S(1)} %collective-permute-done.2.ra, ...), custom_call_target="tpu_custom_call" | custom-call | tf_op jit(solution)/shard_map/steps/pallas_call | solution.py:596
  (57 shorter events, 0.1 us)
Async XLA Ops:
  0.0 1.3 %copy-start = (f32[16,48,384]{2,1,0:T(8,128)S(1)}, f32[16,48,384]{2,1,0:T(8,128)}, u32[]{:S(2)}) copy-start(f32[16,48,384]{2,1,0:T(8,128)} %state.1) | copy-start | bytes 3538948
  1.3 1.3 %copy-start.2 = (f32[16,48,384]{2,1,0:T(8,128)S(1)}, f32[16,48,384]{2,1,0:T(8,128)}, u32[]{:S(2)}) copy-start(f32[16,48,384]{2,1,0:T(8,128)} %diffuse.1) | copy-start | bytes 3538948
  2.5 0.9 copy-start.4
  3.4 0.7 copy-start.14
  4.1 0.8 copy-start.16
  4.9 0.8 copy-start.17
  5.7 0.7 copy-start.19
  6.5 0.7 copy-start.21
  7.1 0.7 copy-start.22
  7.8 0.7 copy-start.23
  8.5 0.7 copy-start.24
  10.1 0.6 copy-start.11
  10.8 34.2 %copy-start.18 = (f32[1,48,128]{2,1,0:T(8,128)}, f32[1,48,128]{2,1,0:T(8,128)S(1)}, u32[]{:S(2)}) copy-start(f32[1,48,128]{2,1,0:T(8,128)S(1)} %get-tuple-element.24.refs_2_) | copy-start | bytes 73732
  10.8 34.2 %copy-start.20 = (f32[1,16,128]{2,1,0:T(8,128)}, f32[1,16,128]{2,1,0:T(8,128)S(1)}, u32[]{:S(2)}) copy-start(f32[1,16,128]{2,1,0:T(8,128)S(1)} %get-tuple-element.23.refs_0_) | copy-start | bytes 24580
  10.8 3.0 %collective-permute-start = (f32[48,384]{1,0:T(8,128)S(1)}, f32[48,384]{1,0:T(8,128)S(1)}, u32[]{:S(2)}, u32[]{:S(2)}) collective-permute-start(f32[48,384]{1,0:T(8,128)S(1)} %get-tuple-element.17), channel_id=1, source_target_pairs={{0,1},{1,2},{2,3},{3,4},{4,5},{5,6},{6,7},{7,8},{8,9},{9,10},{10,1... | collective-permute-start | bytes 221192 | tf_op jit(solution)/shard_map/ppermute | solution.py:569
  12.5 4.9 %collective-permute-start.1 = (f32[48,384]{1,0:T(8,128)S(1)}, f32[48,384]{1,0:T(8,128)S(1)}, u32[]{:S(2)}, u32[]{:S(2)}) collective-permute-start(f32[48,384]{1,0:T(8,128)S(1)} %get-tuple-element.18), channel_id=1, source_target_pairs={{1,0},{2,1},{3,2},{4,3},{5,4},{6,5},{7,6},{8,7},{9,8},{10,9},{11,1... | collective-permute-start | bytes 221192 | tf_op jit(solution)/shard_map/ppermute | solution.py:570
  13.8 3.6 %copy-start.6 = (f32[48,384]{1,0:T(8,128)}, f32[48,384]{1,0:T(8,128)S(1)}, u32[]{:S(2)}) copy-start(f32[48,384]{1,0:T(8,128)S(1)} %collective-permute-done.from_low) | copy-start | bytes 221188
  17.4 0.6 copy-start.8
  18.0 75.1 %copy-start.1 = (f32[16,48,384]{2,1,0:T(8,128)S(1)}, f32[16,48,384]{2,1,0:T(8,128)}, u32[]{:S(2)}) copy-start(f32[16,48,384]{2,1,0:T(8,128)} %state.1) | copy-start | bytes 3538948
  18.0 75.1 %copy-start.3 = (f32[16,48,384]{2,1,0:T(8,128)S(1)}, f32[16,48,384]{2,1,0:T(8,128)}, u32[]{:S(2)}) copy-start(f32[16,48,384]{2,1,0:T(8,128)} %diffuse.1) | copy-start | bytes 3538948
  18.0 75.1 %copy-start.5 = (f32[48,384]{1,0:T(8,128)S(1)}, f32[48,384]{1,0:T(8,128)}, u32[]{:S(2)}) copy-start(f32[48,384]{1,0:T(8,128)} %vertical_hbm.5) | copy-start | bytes 221188
  18.0 75.2 %copy-start.12 = (f32[48,128]{1,0:T(8,128)S(1)}, f32[48,128]{1,0:T(8,128)}, u32[]{:S(2)}) copy-start(f32[48,128]{1,0:T(8,128)} %copy-done.11) | copy-start | bytes 73732
  18.0 75.2 %copy-start.15 = (f32[2,16,128]{2,1,0:T(8,128)S(1)}, f32[2,16,128]{2,1,0:T(8,128)}, u32[]{:S(2)}) copy-start(f32[2,16,128]{2,1,0:T(8,128)} %fill_we_hbm.3) | copy-start | bytes 49156
  18.0 75.2 %copy-start.25 = (s32[2]{0:T(128)S(1)}, s32[2]{0:T(128)}, u32[]{:S(2)}) copy-start(s32[2]{0:T(128)} %jump.1) | copy-start | bytes 28
  21.3 71.8 %collective-permute-start.3 = (f32[600,128]{1,0:T(8,128)}, f32[600,128]{1,0:T(8,128)S(1)}, u32[]{:S(2)}, u32[]{:S(2)}) collective-permute-start(f32[600,128]{1,0:T(8,128)} %get-tuple-element.21), channel_id=1, source_target_pairs={{0,16},{32,48},{64,80},{96,112},{128,144},{160,176},{192,208},{224... | collective-permute-start | bytes 921608 | tf_op jit(solution)/shard_map/ppermute | solution.py:585
  27.0 66.1 %collective-permute-start.2 = (f32[600,128]{1,0:T(8,128)}, f32[600,128]{1,0:T(8,128)S(1)}, u32[]{:S(2)}, u32[]{:S(2)}) collective-permute-start(f32[600,128]{1,0:T(8,128)} %get-tuple-element.20.after), channel_id=1, source_target_pairs={{16,32},{48,64},{80,96},{112,128},{144,160},{176,192},{208,224},{2... | collective-permute-start | bytes 921608 | tf_op jit(solution)/shard_map/ppermute | solution.py:584
  28.9 16.0 %collective-permute-start.5 = (f32[1,48,128]{2,1,0:T(8,128)S(1)}, f32[1,48,128]{2,1,0:T(8,128)S(1)}, u32[]{:S(2)}, u32[]{:S(2)}) collective-permute-start(f32[1,48,128]{2,1,0:T(8,128)S(1)} %get-tuple-element.24.refs_2_), channel_id=1, source_target_pairs={{0,8},{1,9},{2,10},{3,11},{4,12},{5,13},{6,14},{7,15},{8,0},{9,1},... | collective-permute-start | bytes 73736 | tf_op jit(solution)/shard_map/ppermute | solution.py:547
  29.6 15.4 %collective-permute-start.4 = (f32[1,16,128]{2,1,0:T(8,128)S(1)}, f32[1,16,128]{2,1,0:T(8,128)S(1)}, u32[]{:S(2)}, u32[]{:S(2)}) collective-permute-start(f32[1,16,128]{2,1,0:T(8,128)S(1)} %get-tuple-element.23.refs_0_), channel_id=1, source_target_pairs={{0,256},{16,272},{32,288},{48,304},{64,320},{80,336},{96,352},{112... | collective-permute-start | bytes 24584 | tf_op jit(solution)/shard_map/ppermute | solution.py:537
  47.5 9.8 %collective-permute-start.8 = (f32[2,16,128]{2,1,0:T(8,128)}, f32[2,16,128]{2,1,0:T(8,128)S(1)}, u32[]{:S(2)}, u32[]{:S(2)}) collective-permute-start(f32[2,16,128]{2,1,0:T(8,128)} %get-tuple-element.25.refs_0_), channel_id=1, source_target_pairs={{0,192},{16,208},{32,224},{48,240},{64,128},{80,144},{96,160},{112... | collective-permute-start | bytes 49160 | tf_op jit(solution)/shard_map/ppermute | solution.py:537
  52.5 7.3 %collective-permute-start.7 = (f32[2,16,128]{2,1,0:T(8,128)}, f32[2,16,128]{2,1,0:T(8,128)S(1)}, u32[]{:S(2)}, u32[]{:S(2)}) collective-permute-start(f32[2,16,128]{2,1,0:T(8,128)} %get-tuple-element.25.refs_0_), channel_id=1, source_target_pairs={{0,128},{16,144},{32,160},{48,176},{64,192},{80,208},{96,224},{112... | collective-permute-start | bytes 49160 | tf_op jit(solution)/shard_map/ppermute | solution.py:537
  55.0 5.8 %collective-permute-start.6 = (f32[2,16,128]{2,1,0:T(8,128)}, f32[2,16,128]{2,1,0:T(8,128)S(1)}, u32[]{:S(2)}, u32[]{:S(2)}) collective-permute-start(f32[2,16,128]{2,1,0:T(8,128)} %get-tuple-element.25.refs_0_), channel_id=1, source_target_pairs={{0,64},{16,80},{32,96},{48,112},{64,0},{80,16},{96,32},{112,48},{1... | collective-permute-start | bytes 49160 | tf_op jit(solution)/shard_map/ppermute | solution.py:537
  57.4 4.2 %copy-start.30 = (f32[2,16,128]{2,1,0:T(8,128)}, f32[2,16,128]{2,1,0:T(8,128)S(1)}, u32[]{:S(2)}) copy-start(f32[2,16,128]{2,1,0:T(8,128)S(1)} %collective-permute-done.8.refs_3_) | copy-start | bytes 49156
  57.4 4.1 %collective-permute-start.11 = (f32[2,48,128]{2,1,0:T(8,128)}, f32[2,48,128]{2,1,0:T(8,128)S(1)}, u32[]{:S(2)}, u32[]{:S(2)}) collective-permute-start(f32[2,48,128]{2,1,0:T(8,128)} %get-tuple-element.26.refs_4_), channel_id=1, source_target_pairs={{0,6},{1,7},{2,4},{3,5},{4,2},{5,3},{6,0},{7,1},{8,14},{9,15},{10,... | collective-permute-start | bytes 147464 | tf_op jit(solution)/shard_map/ppermute | solution.py:547
  59.8 1.8 %copy-start.31 = (f32[2,16,128]{2,1,0:T(8,128)}, f32[2,16,128]{2,1,0:T(8,128)S(1)}, u32[]{:S(2)}) copy-start(f32[2,16,128]{2,1,0:T(8,128)S(1)} %collective-permute-done.7.refs_2_) | copy-start | bytes 49156
  59.8 1.7 %collective-permute-start.10 = (f32[2,48,128]{2,1,0:T(8,128)}, f32[2,48,128]{2,1,0:T(8,128)S(1)}, u32[]{:S(2)}, u32[]{:S(2)}) collective-permute-start(f32[2,48,128]{2,1,0:T(8,128)} %get-tuple-element.26.refs_4_), channel_id=1, source_target_pairs={{0,4},{1,5},{2,6},{3,7},{4,0},{5,1},{6,2},{7,3},{8,12},{9,13},{10,... | collective-permute-start | bytes 147464 | tf_op jit(solution)/shard_map/ppermute | solution.py:547
  60.8 0.7 copy-start.32
  60.8 0.7 collective-permute-start.9
  61.5 0.6 copy-start.26
  61.5 0.6 copy-start.27
  62.2 0.6 copy-start.28
  64.4 28.7 %collective-permute-start.15 = (f32[8,48,128]{2,1,0:T(8,128)}, f32[8,48,128]{2,1,0:T(8,128)S(1)}, u32[]{:S(2)}, u32[]{:S(2)}) collective-permute-start(f32[8,48,128]{2,1,0:T(8,128)} %get-tuple-element.28.refs_4_), channel_id=1, source_target_pairs={{0,1},{1,0},{2,3},{3,2},{4,5},{5,4},{6,7},{7,6},{8,9},{9,8},{10,11... | collective-permute-start | bytes 589832 | tf_op jit(solution)/shard_map/ppermute | solution.py:547
  65.1 21.6 %collective-permute-start.14 = (f32[8,16,128]{2,1,0:T(8,128)}, f32[8,16,128]{2,1,0:T(8,128)S(1)}, u32[]{:S(2)}, u32[]{:S(2)}) collective-permute-start(f32[8,16,128]{2,1,0:T(8,128)} %get-tuple-element.27.refs_0_), channel_id=1, source_target_pairs={{0,48},{16,32},{32,16},{48,0},{64,112},{80,96},{96,80},{112,64},{1... | collective-permute-start | bytes 196616 | tf_op jit(solution)/shard_map/ppermute | solution.py:537
  67.0 23.3 %collective-permute-start.13 = (f32[8,16,128]{2,1,0:T(8,128)}, f32[8,16,128]{2,1,0:T(8,128)S(1)}, u32[]{:S(2)}, u32[]{:S(2)}) collective-permute-start(f32[8,16,128]{2,1,0:T(8,128)} %get-tuple-element.27.refs_0_), channel_id=1, source_target_pairs={{0,32},{16,48},{32,0},{48,16},{64,96},{80,112},{96,64},{112,80},{1... | collective-permute-start | bytes 196616 | tf_op jit(solution)/shard_map/ppermute | solution.py:537
  86.7 6.4 %collective-permute-start.12 = (f32[8,16,128]{2,1,0:T(8,128)}, f32[8,16,128]{2,1,0:T(8,128)S(1)}, u32[]{:S(2)}, u32[]{:S(2)}) collective-permute-start(f32[8,16,128]{2,1,0:T(8,128)} %get-tuple-element.27.refs_0_), channel_id=1, source_target_pairs={{0,16},{16,0},{32,48},{48,32},{64,80},{80,64},{96,112},{112,96},{1... | collective-permute-start | bytes 196616 | tf_op jit(solution)/shard_map/ppermute | solution.py:537
  93.2 0.9 copy-start.7
  94.1 0.9 copy-start.9
  95.0 0.9 copy-start.10
  95.9 0.8 copy-start.13
  (2 other events, 1.2 us)

commit v4 on v3

--- a/solution.py
+++ b/solution.py
@@ -44,8 +44,8 @@
     square, sem,
 ):
     nx, ny = lax.axis_index("nx"), lax.axis_index("ny")
-    side_x = jnp.where(ny == 0, 0, 1)
-    side_y = jnp.where(nx == 0, 0, 1)
+    side_x = jnp.where(ny < lax.axis_size("ny") // 2, 0, 1)
+    side_y = jnp.where(nx < lax.axis_size("nx") // 2, 0, 1)
     pairs = [
         (rows_we_hbm.at[:, side_y], rows_we),
         (rows_sn_hbm.at[:, side_x], rows_sn),
@@ -110,7 +110,8 @@
 
 
 def border_kernel(
-    state_hbm, diffuse_hbm, vertical_hbm, from_low, from_high, colpack, xa, xb, state, diffuse, vertical, sem
+    after_x, after_y, state_hbm, diffuse_hbm, vertical_hbm, from_low, from_high, colpack,
+    xa, xb, state, diffuse, vertical, sem,
 ):
     copies = [pltpu.make_async_copy(vertical_hbm, vertical, sem.at[4])]
     for n, (src, dst) in enumerate(((state_hbm, state), (diffuse_hbm, diffuse))):
@@ -158,7 +159,7 @@
         rows(xb, 1)
 
 
-def join_kernel(count_x, count_y, after, *refs):
+def join_kernel(count_x, count_y, *refs):
     ins, (out_x, out_y) = refs[:-2], refs[-2:]
     for out, parts in ((out_x, ins[:count_x]), (out_y, ins[count_x : count_x + count_y])):
         at = 0
@@ -167,13 +168,77 @@
             at += part.shape[0]
 
 
-def main_kernel(
-    count_x, count_y, plan_x, plan_y, jump, state, diffuse, vertical_hbm, fill_we_hbm, ra, rb, from_low, from_high,
-    colpack, interp, *refs,
-):
+def edge_kernel(count_x, count_y, plan_x, plan_y, ra, rb, from_low, from_high, colpack, interp, *refs):
     chain_x, refs = refs[: len(plan_x)], refs[len(plan_x) :]
     chain_y, refs = refs[: len(plan_y)], refs[len(plan_y) :]
-    out, es, ed, ev, mv, gv, fac, strip, ey, ex, pack, vertical, fill_we, sem = refs
+    edges, pack = refs
+    nx, ny = lax.axis_index("nx"), lax.axis_index("ny")
+    odd = nx % 2 == 1
+    border_x = (nx == 0) | (nx == count_x - 1)
+    border_y = (ny == 0) | (ny == count_y - 1)
+    inner_x = (nx == 1) | (nx == count_x - 2)
+    inner_y = (ny == 1) | (ny == count_y - 2)
+
+    @pl.when((border_x & jnp.logical_not(inner_y)) | (inner_x & inner_y))
+    def _():
+        lane1 = lax.broadcasted_iota(jnp.int32, (1, 128), 1)
+        for l in range(NG + 1):
+            got = []
+            for item in range(2):
+                if l < NG:
+                    got.append(interp[item : item + 1, 128 * l : 128 * l + 128])
+                else:
+                    got.append(
+                        jnp.where(
+                            lane1 < 64,
+                            pltpu.roll(from_high[0:8, 256:384], 112, 1)[item : item + 1],
+                            pltpu.roll(from_low[0:8, 256:384], 104, 1)[item : item + 1],
+                        )
+                    )
+            index = jnp.broadcast_to(got[0], (48, 128)).astype(jnp.int32)
+            ends = []
+            for offset in range(2):
+                at = index + offset
+                block, inside = at >> 7, at & 127
+                total = jnp.zeros((48, 128), jnp.float32)
+                for ref, masks in zip(chain_y, plan_y, strict=True):
+                    for piece, mask in enumerate(masks):
+                        value = jnp.take_along_axis(ref[piece], inside, axis=1, mode="promise_in_bounds")
+                        total = jnp.where(block == (ny ^ mask), value, total)
+                ends.append(total)
+            edges[64 + 48 * l : 112 + 48 * l, :] = (1.0 - got[1]) * ends[0] + got[1] * ends[1]
+
+    @pl.when((border_y & jnp.logical_not(border_x)) | (border_x & inner_y))
+    def _():
+        n = CORNER_AT + 8 * (NG - 1)
+        a, b = ra[n : n + 8, :], rb[n : n + 8, :]
+        pack[0:HX, :] = jnp.where(odd, b, a)
+        pack[HX : HX + WX, :] = colpack[...]
+        pack[HX + WX : 64, :] = jnp.where(odd, a, b)
+        index = pack[:, 64:65].astype(jnp.int32)
+        weight = pack[:, 65:66]
+        total = jnp.zeros((64, 128), jnp.float32)
+        for ref, masks in zip(chain_x, plan_x, strict=True):
+            size = 16 * len(masks)
+            at = lax.broadcasted_iota(jnp.int32, (1, size), 1)
+            ids = at & 15
+            for piece, mask in enumerate(masks):
+                ids = jnp.where(at >> 4 == piece, ids + 16 * (nx ^ mask), ids)
+            spread = jnp.where(ids == index, 1.0 - weight, 0.0) + jnp.where(ids == index + 1, weight, 0.0)
+            total += jnp.dot(
+                spread,
+                ref[...].reshape(size, 128),
+                preferred_element_type=jnp.float32,
+                precision=lax.Precision.HIGHEST,
+            )
+        edges[0:64, :] = total
+
+
+def main_kernel(
+    count_x, count_y, jump, state, diffuse, vertical_hbm, fill_we_hbm, ra, rb, from_low, from_high,
+    colpack, edges, brought_ref,
+    out, es, ed, ev, mv, gv, fac, strip, ey, ex, pack, vertical, fill_we, sem,
+):
     dx, dy = jump[0], jump[1]
     nx, ny = lax.axis_index("nx"), lax.axis_index("ny")
     copies = []
@@ -245,52 +310,14 @@
 
     @pl.when(west | east)
     def _():
-        lane1 = lax.broadcasted_iota(jnp.int32, (1, 128), 1)
+        brought = (ny == 1) | (ny == count_y - 2)
         for l in range(NG + 1):
-            got = []
-            for item in range(2):
-                if l < NG:
-                    got.append(interp[item : item + 1, 128 * l : 128 * l + 128])
-                else:
-                    got.append(
-                        jnp.where(
-                            lane1 < 64,
-                            pltpu.roll(strip[1, HX : HX + 8, 256:384], 112, 1)[item : item + 1],
-                            pltpu.roll(strip[0, HX : HX + 8, 256:384], 104, 1)[item : item + 1],
-                        )
-                    )
-            index = jnp.broadcast_to(got[0], (48, 128)).astype(jnp.int32)
-            ends = []
-            for offset in range(2):
-                at = index + offset
-                block, inside = at >> 7, at & 127
-                total = jnp.zeros((48, 128), jnp.float32)
-                for ref, masks in zip(chain_y, plan_y, strict=True):
-                    for piece, mask in enumerate(masks):
-                        value = jnp.take_along_axis(ref[piece], inside, axis=1, mode="promise_in_bounds")
-                        total = jnp.where(block == (ny ^ mask), value, total)
-                ends.append(total)
-            ey[l] = (1.0 - got[1]) * ends[0] + got[1] * ends[1]
+            rows = slice(64 + 48 * l, 112 + 48 * l)
+            ey[l] = jnp.where(brought, brought_ref[rows, :], edges[rows, :])
 
     @pl.when(south | north)
     def _():
-        index = pack[:, 64:65].astype(jnp.int32)
-        weight = pack[:, 65:66]
-        total = jnp.zeros((64, 128), jnp.float32)
-        for ref, masks in zip(chain_x, plan_x, strict=True):
-            size = 16 * len(masks)
-            at = lax.broadcasted_iota(jnp.int32, (1, size), 1)
-            ids = at & 15
-            for piece, mask in enumerate(masks):
-                ids = jnp.where(at >> 4 == piece, ids + 16 * (nx ^ mask), ids)
-            spread = jnp.where(ids == index, 1.0 - weight, 0.0) + jnp.where(ids == index + 1, weight, 0.0)
-            total += jnp.dot(
-                spread,
-                ref[...].reshape(size, 128),
-                preferred_element_type=jnp.float32,
-                precision=lax.Precision.HIGHEST,
-            )
-        ex[0:64, :] = total
+        ex[...] = jnp.where(west | east, brought_ref[0:64, :], edges[0:64, :])
 
     def ghosts(field, step, row_low, row_high, shift):
         @pl.when(west)
@@ -493,6 +520,12 @@
     def shape(*dims):
         return jax.ShapeDtypeStruct(dims, f32)
 
+    state, diffuse, vertical, rows_we, rows_sn, fill_we, fill_sn, index_we, weight_we, index_sn, weight_sn = (
+        pltpu.with_memory_space_constraint(x, pltpu.HBM)
+        for x in (
+            state, diffuse, vertical, rows_we, rows_sn, fill_we, fill_sn, index_we, weight_we, index_sn, weight_sn
+        )
+    )
     y_low, y_high, chain_x, chain_y, colpack, interp = pl.pallas_call(
         pack_kernel,
         out_shape=(
@@ -520,7 +553,7 @@
             pltpu.VMEM((128, 128), f32),
             pltpu.SemaphoreType.DMA((13,)),
         ],
-        compiler_params=pltpu.CompilerParams(vmem_limit_bytes=40 << 20),
+        compiler_params=pltpu.CompilerParams(vmem_limit_bytes=16 << 20),
         name="pack",
     )(state, diffuse, vertical, rows_we, rows_sn, fill_we, fill_sn, index_we, weight_we, index_sn, weight_sn)
 
@@ -532,37 +565,45 @@
     down = [(b, a) for a, b in up]
     rounds_x, rounds_y = rounds_of(count_x), rounds_of(count_y)
 
-    def along_x(chain, masks):
+    def place(i, j):
+        return i * count_y + j
+
+    last_x, last_y = count_x - 1, count_y - 1
+    set_x = [
+        [place(i, (1 if i in (0, last_x) else 0) if side == 0 else (last_y - 1 if i in (0, last_x) else last_y))
+         for i in range(count_x)]
+        for side in range(2)
+    ]
+    set_y = [
+        [place((1 if j in (1, last_y - 1) else 0) if side == 0 else (last_x - 1 if j in (1, last_y - 1) else last_x), j)
+         for j in range(count_y)]
+        for side in range(2)
+    ]
+    bring = []
+    for i, step in ((0, 1), (last_x, -1)):
+        for j, other in ((0, 1), (last_y, last_y - 1)):
+            bring.append((place(i, other), place(i, j)))
+            bring.append((place(i + step, other), place(i, other)))
+
+    def along(sets, chain, masks):
         return [
-            lax.ppermute(
-                chain,
-                both,
-                [(i * count_y + n, (i ^ m) * count_y + n) for n in (0, count_y - 1) for i in range(count_x)],
-            )
-            for m in masks
+            lax.ppermute(chain, both, [(own[n], own[n ^ m]) for own in sets for n in range(len(own))]) for m in masks
         ]
 
-    def along_y(chain, masks):
-        return [
-            lax.ppermute(
-                chain,
-                both,
-                [(n * count_y + j, n * count_y + (j ^ m)) for n in (0, count_x - 1) for j in range(count_y)],
-            )
-            for m in masks
-        ]
-
-    def join(after, parts_x, parts_y, name):
+    along_x, along_y = functools.partial(along, set_x), functools.partial(along, set_y)
+
+    def join(parts_x, parts_y, name):
         return pl.pallas_call(
             functools.partial(join_kernel, len(parts_x), len(parts_y)),
             out_shape=(
                 shape(sum(p.shape[0] for p in parts_x), 16, 128),
                 shape(sum(p.shape[0] for p in parts_y), 48, 128),
             ),
-            in_specs=[any_] + [vmem] * (len(parts_x) + len(parts_y)),
+            in_specs=[vmem] * (len(parts_x) + len(parts_y)),
             out_specs=(vmem, vmem),
+            compiler_params=pltpu.CompilerParams(vmem_limit_bytes=8 << 20),
             name=name,
-        )(after, *parts_x, *parts_y)
+        )(*parts_x, *parts_y)
 
     parts_x = [chain_x] + along_x(chain_x, rounds_x[0])
     parts_y = [chain_y] + along_y(chain_y, rounds_y[0])
@@ -571,7 +612,7 @@
     xa, xb = pl.pallas_call(
         border_kernel,
         out_shape=(shape(SENT, 128), shape(SENT, 128)),
-        in_specs=[hbm] * 3 + [vmem] * 3,
+        in_specs=[any_] * 2 + [hbm] * 3 + [vmem] * 3,
         out_specs=(vmem, vmem),
         scratch_shapes=[
             pltpu.VMEM((2, LV, 8, WY), f32),
@@ -579,24 +620,36 @@
             pltpu.VMEM((WX, WY), f32),
             pltpu.SemaphoreType.DMA((5,)),
         ],
+        compiler_params=pltpu.CompilerParams(vmem_limit_bytes=8 << 20),
         name="border",
-    )(state, diffuse, vertical, from_low, from_high, colpack)
+    )(parts_x[-1], parts_y[-1], state, diffuse, vertical, from_low, from_high, colpack)
     ra = lax.ppermute(xa, "nx", pairs_a)
     rb = lax.ppermute(xb, "nx", pairs_b)
-    chain_x, chain_y = join(xa, parts_x, parts_y, "join_first")
+    chain_x, chain_y = join(parts_x, parts_y, "join_first")
     parts_x = [chain_x] + along_x(chain_x, rounds_x[1])
     parts_y = [chain_y] + along_y(chain_y, rounds_y[1])
-    chain_x, chain_y = join(xa, parts_x, parts_y, "join_second")
+    chain_x, chain_y = join(parts_x, parts_y, "join_second")
     parts_x = [chain_x] + along_x(chain_x, rounds_x[2])
     parts_y = [chain_y] + along_y(chain_y, rounds_y[2])
     have_x, have_y = masks_of(rounds_x[:2]), masks_of(rounds_y[:2])
     plan_x = [[m ^ h for h in have_x] for m in [0] + rounds_x[2]]
     plan_y = [[m ^ h for h in have_y] for m in [0] + rounds_y[2]]
 
+    edges = pl.pallas_call(
+        functools.partial(edge_kernel, count_x, count_y, plan_x, plan_y),
+        out_shape=shape(256, 128),
+        in_specs=[vmem] * (6 + len(parts_x) + len(parts_y)),
+        out_specs=vmem,
+        scratch_shapes=[pltpu.VMEM((64, 128), f32)],
+        compiler_params=pltpu.CompilerParams(vmem_limit_bytes=8 << 20),
+        name="edges",
+    )(ra, rb, from_low, from_high, colpack, interp, *parts_x, *parts_y)
+    brought = lax.ppermute(edges, both, bring)
+
     return pl.pallas_call(
-        functools.partial(main_kernel, count_x, count_y, plan_x, plan_y),
+        functools.partial(main_kernel, count_x, count_y),
         out_shape=shape(LV, WX, WY),
-        in_specs=[smem] + [hbm] * 4 + [vmem] * (6 + len(parts_x) + len(parts_y)),
+        in_specs=[smem] + [hbm] * 4 + [vmem] * 7,
         out_specs=vmem,
         scratch_shapes=[
             pltpu.VMEM((LV, NG + 1, 72, 128), f32),
@@ -613,11 +666,11 @@
             pltpu.VMEM((2, 16, 128), f32),
             pltpu.SemaphoreType.DMA((2 * NG + 2,)),
         ],
-        compiler_params=pltpu.CompilerParams(vmem_limit_bytes=48 << 20),
+        compiler_params=pltpu.CompilerParams(vmem_limit_bytes=22 << 20),
         name="steps",
     )(
         jump, state, diffuse, vertical, fill_we, ra, rb, from_low, from_high,
-        colpack, interp, *parts_x, *parts_y,
+        colpack, edges, brought,
     )
 
 

time: 108 us -> 83.8 us (0.78)
  the two profiles are of different devices: /device:TPU:2 before, /device:TPU:1 now
where the time goes in v4:
time: 83.8 us; the launch traced here: 83.3 us
  starting transfers between devices  56.4 us (67%)
  Pallas kernels  14 us (17%)
  waiting for transfers between devices  12.7 us (15%)
    ppermute x12, starting transfers between devices, along(): lax.ppermute(chain, both, [(own[n], own[n ^ m]) for own in sets for n in...  41.8 us
    pallas_call x1, Pallas kernels, on_device(): pl.pallas_call(functools.partial(main_kernel, count_x, count_y), out_shap...  10 us
    ppermute x12, waiting for transfers between devices, along(): lax.ppermute(chain, both, [(own[n], own[n ^ m]) for own in sets for n in...  8.89 us
    ppermute x1, starting transfers between devices, on_device(): from_high = lax.ppermute(y_low, 'ny', down)  5.14 us
    ppermute x1, starting transfers between devices, on_device(): from_low = lax.ppermute(y_high, 'ny', up)  4.94 us
    ppermute x1, waiting for transfers between devices, on_device(): brought = lax.ppermute(edges, both, bring)  3.78 us
    pallas_call x1, Pallas kernels, on_device(): pl.pallas_call(pack_kernel, out_shape=(shape(WX, WY), shape(WX, WY), shap...  2.13 us
    ppermute x1, starting transfers between devices, on_device(): brought = lax.ppermute(edges, both, bring)  1.92 us
  transfers between devices with their start and end apart: 17, of which 6 were waited for; matrix products, arithmetic and copies ran while one was open for 0% of the time, Pallas kernels for 0%

profile of v4, /device:TPU:1, one launch (start us, length us, event | category | flops | bytes accessed | tf_op | source)
XLA Modules:
  0.0 83.3 jit_solution(8839508790500898515)
XLA Ops:
  0.0 2.1 %pack.1 = (f32[48,384]{1,0:T(8,128)S(1)}, f32[48,384]{1,0:T(8,128)S(1)}, f32[1,16,128]{2,1,0:T(8,128)S(1)}, f32[1,48,128]{2,1,0:T(8,128)S(1)}, f32[48,128]{1,0:T(8,128)S(1)}, /*index=5*/f32[8,384]{1,0:T(8,128)S(1)}) custom-call(f32[16,48,384]{2,1,0:T(8,128)} %state.1, f32[16,48,384]{2,1,0:T(8,128)} %diffuse.1, f32[48,384]{1,0:T(8,128)} %vertical_hbm.5, ...), custom_call_target="tpu_custom_call" | custom-call | tf_op jit(solution)/shard_map/pack/pallas_call | solution.py:529
  2.1 4.9 %collective-permute-start.2 = (f32[48,384]{1,0:T(8,128)S(1)}, f32[48,384]{1,0:T(8,128)S(1)}, u32[]{:S(2)}, u32[]{:S(2)}) collective-permute-start(f32[48,384]{1,0:T(8,128)S(1)} %get-tuple-element.19), channel_id=1, source_target_pairs={{0,1},{1,2},{2,3},{3,4},{4,5},{5,6},{6,7},{7,8},{8,9},{9,10},{10,1... | collective-permute-start | bytes 221192 | tf_op jit(solution)/shard_map/ppermute | solution.py:610
  7.1 5.1 %collective-permute-start.3 = (f32[48,384]{1,0:T(8,128)S(1)}, f32[48,384]{1,0:T(8,128)S(1)}, u32[]{:S(2)}, u32[]{:S(2)}) collective-permute-start(f32[48,384]{1,0:T(8,128)S(1)} %get-tuple-element.20), channel_id=1, source_target_pairs={{1,0},{2,1},{3,2},{4,3},{5,4},{6,5},{7,6},{8,7},{9,8},{10,9},{11,1... | collective-permute-start | bytes 221192 | tf_op jit(solution)/shard_map/ppermute | solution.py:611
  12.2 0.7 collective-permute-start.1
  12.9 9.8 %collective-permute-start = (f32[1,16,128]{2,1,0:T(8,128)S(1)}, f32[1,16,128]{2,1,0:T(8,128)S(1)}, u32[]{:S(2)}, u32[]{:S(2)}) collective-permute-start(f32[1,16,128]{2,1,0:T(8,128)S(1)} %get-tuple-element.17.refs_0_), channel_id=1, source_target_pairs={{1,256},{16,272},{32,288},{48,304},{64,320},{80,336},{96,352},{112... | collective-permute-start | bytes 24584 | tf_op jit(solution)/shard_map/ppermute | solution.py:590
  22.7 3.9 %collective-permute-done.after_x.refs_1_ = f32[1,16,128]{2,1,0:T(8,128)S(1)} collective-permute-done((f32[1,16,128]{2,1,0:T(8,128)S(1)}, f32[1,16,128]{2,1,0:T(8,128)S(1)}, u32[]{:S(2)}, u32[]{:S(2)}) %collective-permute-start) | collective-permute-done | bytes 8224 | tf_op jit(solution)/shard_map/ppermute | solution.py:590
  26.6 0.0 collective-permute-done.1.after_y.refs_3_
  26.6 0.0 collective-permute-done.2.from_low
  26.6 0.0 collective-permute-done.3.from_high
  26.6 1.4 %border.1 = (f32[600,128]{1,0:T(8,128)S(1)}, f32[600,128]{1,0:T(8,128)S(1)}) custom-call(f32[1,16,128]{2,1,0:T(8,128)S(1)} %collective-permute-done.after_x.refs_1_, f32[1,48,128]{2,1,0:T(8,128)S(1)} %collective-permute-done.1.after_y.refs_3_, f32[16,48,384]{2,1,0:T(8,128)} %state.1, f32[16,48,384]{2,1,0:T(8,128)} %diffuse.1, f32[48,384]{1,0:T(8,128)} %vertical_hbm.5, ...), custom_call_target="tpu_custom_call" | custom-call | tf_op jit(solution)/shard_map/border/pallas_call | solution.py:612
  28.0 0.0 copy-start
  28.0 0.7 collective-permute-start.4
  28.7 1.9 %collective-permute-start.5 = (f32[600,128]{1,0:T(8,128)S(1)}, f32[600,128]{1,0:T(8,128)S(1)}, u32[]{:S(2)}, u32[]{:S(2)}) collective-permute-start(f32[600,128]{1,0:T(8,128)S(1)} %get-tuple-element.23), channel_id=1, source_target_pairs={{0,16},{32,48},{64,80},{96,112},{128,144},{160,176},{192,208},{224... | collective-permute-start | bytes 921608 | tf_op jit(solution)/shard_map/ppermute | solution.py:627
  30.6 6.9 %collective-permute-start.8 = (f32[2,16,128]{2,1,0:T(8,128)S(1)}, f32[2,16,128]{2,1,0:T(8,128)S(1)}, u32[]{:S(2)}, u32[]{:S(2)}) collective-permute-start(f32[2,16,128]{2,1,0:T(8,128)S(1)} %get-tuple-element.25.refs_0_), channel_id=1, source_target_pairs={{1,192},{16,208},{32,224},{48,240},{64,128},{80,144},{96,160},{112... | collective-permute-start | bytes 49160 | tf_op jit(solution)/shard_map/ppermute | solution.py:590
  37.5 2.5 %collective-permute-start.7 = (f32[2,16,128]{2,1,0:T(8,128)S(1)}, f32[2,16,128]{2,1,0:T(8,128)S(1)}, u32[]{:S(2)}, u32[]{:S(2)}) collective-permute-start(f32[2,16,128]{2,1,0:T(8,128)S(1)} %get-tuple-element.25.refs_0_), channel_id=1, source_target_pairs={{1,128},{16,144},{32,160},{48,176},{64,192},{80,208},{96,224},{112... | collective-permute-start | bytes 49160 | tf_op jit(solution)/shard_map/ppermute | solution.py:590
  40.0 2.1 %collective-permute-start.6 = (f32[2,16,128]{2,1,0:T(8,128)S(1)}, f32[2,16,128]{2,1,0:T(8,128)S(1)}, u32[]{:S(2)}, u32[]{:S(2)}) collective-permute-start(f32[2,16,128]{2,1,0:T(8,128)S(1)} %get-tuple-element.25.refs_0_), channel_id=1, source_target_pairs={{1,64},{16,80},{32,96},{48,112},{64,1},{80,16},{96,32},{112,48},{1... | collective-permute-start | bytes 49160 | tf_op jit(solution)/shard_map/ppermute | solution.py:590
  42.2 0.0 collective-permute-done.8.refs_3_
  42.2 0.7 collective-permute-start.11
  42.9 1.2 %collective-permute-done.7.refs_2_ = f32[2,16,128]{2,1,0:T(8,128)S(1)} collective-permute-done((f32[2,16,128]{2,1,0:T(8,128)S(1)}, f32[2,16,128]{2,1,0:T(8,128)S(1)}, u32[]{:S(2)}, u32[]{:S(2)}) %collective-permute-start.7) | collective-permute-done | bytes 16416 | tf_op jit(solution)/shard_map/ppermute | solution.py:590
  44.0 0.7 collective-permute-start.10
  44.7 0.4 collective-permute-done.6.refs_1_
  45.1 0.7 collective-permute-start.9
  45.7 0.0 collective-permute-done.11.refs_7_
  45.8 0.0 collective-permute-done.10.refs_6_
  45.8 0.0 collective-permute-done.9.refs_5_
  45.8 0.7 collective-permute-start.15
  46.5 11.6 %collective-permute-start.14 = (f32[8,16,128]{2,1,0:T(8,128)S(1)}, f32[8,16,128]{2,1,0:T(8,128)S(1)}, u32[]{:S(2)}, u32[]{:S(2)}) collective-permute-start(f32[8,16,128]{2,1,0:T(8,128)S(1)} %get-tuple-element.27.refs_0_), channel_id=1, source_target_pairs={{1,48},{16,32},{32,16},{48,1},{64,112},{80,96},{96,80},{112,64},{1... | collective-permute-start | bytes 196616 | tf_op jit(solution)/shard_map/ppermute | solution.py:590
  58.1 3.4 %collective-permute-start.13 = (f32[8,16,128]{2,1,0:T(8,128)S(1)}, f32[8,16,128]{2,1,0:T(8,128)S(1)}, u32[]{:S(2)}, u32[]{:S(2)}) collective-permute-start(f32[8,16,128]{2,1,0:T(8,128)S(1)} %get-tuple-element.27.refs_0_), channel_id=1, source_target_pairs={{1,32},{16,48},{32,1},{48,16},{64,96},{80,112},{96,64},{112,80},{1... | collective-permute-start | bytes 196616 | tf_op jit(solution)/shard_map/ppermute | solution.py:590
  61.5 0.0 collective-permute-done.14.refs_3_
  61.5 2.1 %collective-permute-start.12 = (f32[8,16,128]{2,1,0:T(8,128)S(1)}, f32[8,16,128]{2,1,0:T(8,128)S(1)}, u32[]{:S(2)}, u32[]{:S(2)}) collective-permute-start(f32[8,16,128]{2,1,0:T(8,128)S(1)} %get-tuple-element.27.refs_0_), channel_id=1, source_target_pairs={{1,16},{16,1},{32,48},{48,32},{64,80},{80,64},{96,112},{112,96},{1... | collective-permute-start | bytes 196616 | tf_op jit(solution)/shard_map/ppermute | solution.py:590
  63.7 1.5 %collective-permute-done.13.refs_2_ = f32[8,16,128]{2,1,0:T(8,128)S(1)} collective-permute-done((f32[8,16,128]{2,1,0:T(8,128)S(1)}, f32[8,16,128]{2,1,0:T(8,128)S(1)}, u32[]{:S(2)}, u32[]{:S(2)}) %collective-permute-start.13) | collective-permute-done | bytes 65568 | tf_op jit(solution)/shard_map/ppermute | solution.py:590
  65.2 1.9 %collective-permute-done.12.refs_1_ = f32[8,16,128]{2,1,0:T(8,128)S(1)} collective-permute-done((f32[8,16,128]{2,1,0:T(8,128)S(1)}, f32[8,16,128]{2,1,0:T(8,128)S(1)}, u32[]{:S(2)}, u32[]{:S(2)}) %collective-permute-start.12) | collective-permute-done | bytes 65568 | tf_op jit(solution)/shard_map/ppermute | solution.py:590
  67.1 0.0 collective-permute-done.15.refs_5_
  67.1 0.0 collective-permute-done.4.ra
  67.1 0.0 collective-permute-done.5.rb
  67.1 0.4 edges.1
  67.6 1.9 %collective-permute-start.16 = (f32[256,128]{1,0:T(8,128)S(1)}, f32[256,128]{1,0:T(8,128)S(1)}, u32[]{:S(2)}, u32[]{:S(2)}) collective-permute-start(f32[256,128]{1,0:T(8,128)S(1)} %edges.1), channel_id=1, source_target_pairs={{1,0},{17,1},{14,15},{30,14},{497,496},{481,497},{510,511},{494,510}} | collective-permute-start | bytes 393224 | tf_op jit(solution)/shard_map/ppermute | solution.py:647
  69.5 3.8 %collective-permute-done.16.brought_ref = f32[256,128]{1,0:T(8,128)S(1)} collective-permute-done((f32[256,128]{1,0:T(8,128)S(1)}, f32[256,128]{1,0:T(8,128)S(1)}, u32[]{:S(2)}, u32[]{:S(2)}) %collective-permute-start.16) | collective-permute-done | bytes 131104 | tf_op jit(solution)/shard_map/ppermute | solution.py:647
  73.3 0.0 copy-done
  73.3 10.0 %steps.1 = f32[16,48,384]{2,1,0:T(8,128)} custom-call(s32[2]{0:T(128)S(1)} %copy-done, f32[16,48,384]{2,1,0:T(8,128)} %state.1, f32[16,48,384]{2,1,0:T(8,128)} %diffuse.1, f32[48,384]{1,0:T(8,128)} %vertical_hbm.5, f32[2,16,128]{2,1,0:T(8,128)} %fill_we_hbm.3, f32[600,128]{1,0:T(8,128)S(1)} %collective-permute-done.4.ra, ...), custom_call_target="tpu_custom_call" | custom-call | tf_op jit(solution)/shard_map/steps/pallas_call | solution.py:649
  (2 shorter events, 0.0 us)
Async XLA Ops:
  2.1 24.5 %collective-permute-start.2 = (f32[48,384]{1,0:T(8,128)S(1)}, f32[48,384]{1,0:T(8,128)S(1)}, u32[]{:S(2)}, u32[]{:S(2)}) collective-permute-start(f32[48,384]{1,0:T(8,128)S(1)} %get-tuple-element.19), channel_id=1, source_target_pairs={{0,1},{1,2},{2,3},{3,4},{4,5},{5,6},{6,7},{7,8},{8,9},{9,10},{10,1... | collective-permute-start | bytes 221192 | tf_op jit(solution)/shard_map/ppermute | solution.py:610
  7.1 19.5 %collective-permute-start.3 = (f32[48,384]{1,0:T(8,128)S(1)}, f32[48,384]{1,0:T(8,128)S(1)}, u32[]{:S(2)}, u32[]{:S(2)}) collective-permute-start(f32[48,384]{1,0:T(8,128)S(1)} %get-tuple-element.20), channel_id=1, source_target_pairs={{1,0},{2,1},{3,2},{4,3},{5,4},{6,5},{7,6},{8,7},{9,8},{10,9},{11,1... | collective-permute-start | bytes 221192 | tf_op jit(solution)/shard_map/ppermute | solution.py:611
  12.2 14.4 %collective-permute-start.1 = (f32[1,48,128]{2,1,0:T(8,128)S(1)}, f32[1,48,128]{2,1,0:T(8,128)S(1)}, u32[]{:S(2)}, u32[]{:S(2)}) collective-permute-start(f32[1,48,128]{2,1,0:T(8,128)S(1)} %get-tuple-element.18.refs_2_), channel_id=1, source_target_pairs={{0,8},{17,9},{2,10},{3,11},{4,12},{5,13},{6,30},{7,15},{8,0},{9,17... | collective-permute-start | bytes 73736 | tf_op jit(solution)/shard_map/ppermute | solution.py:590
  12.9 13.7 %collective-permute-start = (f32[1,16,128]{2,1,0:T(8,128)S(1)}, f32[1,16,128]{2,1,0:T(8,128)S(1)}, u32[]{:S(2)}, u32[]{:S(2)}) collective-permute-start(f32[1,16,128]{2,1,0:T(8,128)S(1)} %get-tuple-element.17.refs_0_), channel_id=1, source_target_pairs={{1,256},{16,272},{32,288},{48,304},{64,320},{80,336},{96,352},{112... | collective-permute-start | bytes 24584 | tf_op jit(solution)/shard_map/ppermute | solution.py:590
  28.0 45.3 %copy-start = (s32[2]{0:T(128)S(1)}, s32[2]{0:T(128)}, u32[]{:S(2)}) copy-start(s32[2]{0:T(128)} %jump.1) | copy-start | bytes 28
  28.0 39.1 %collective-permute-start.4 = (f32[600,128]{1,0:T(8,128)S(1)}, f32[600,128]{1,0:T(8,128)S(1)}, u32[]{:S(2)}, u32[]{:S(2)}) collective-permute-start(f32[600,128]{1,0:T(8,128)S(1)} %get-tuple-element.22), channel_id=1, source_target_pairs={{16,32},{48,64},{80,96},{112,128},{144,160},{176,192},{208,224},{2... | collective-permute-start | bytes 921608 | tf_op jit(solution)/shard_map/ppermute | solution.py:626
  28.7 38.4 %collective-permute-start.5 = (f32[600,128]{1,0:T(8,128)S(1)}, f32[600,128]{1,0:T(8,128)S(1)}, u32[]{:S(2)}, u32[]{:S(2)}) collective-permute-start(f32[600,128]{1,0:T(8,128)S(1)} %get-tuple-element.23), channel_id=1, source_target_pairs={{0,16},{32,48},{64,80},{96,112},{128,144},{160,176},{192,208},{224... | collective-permute-start | bytes 921608 | tf_op jit(solution)/shard_map/ppermute | solution.py:627
  30.6 11.6 %collective-permute-start.8 = (f32[2,16,128]{2,1,0:T(8,128)S(1)}, f32[2,16,128]{2,1,0:T(8,128)S(1)}, u32[]{:S(2)}, u32[]{:S(2)}) collective-permute-start(f32[2,16,128]{2,1,0:T(8,128)S(1)} %get-tuple-element.25.refs_0_), channel_id=1, source_target_pairs={{1,192},{16,208},{32,224},{48,240},{64,128},{80,144},{96,160},{112... | collective-permute-start | bytes 49160 | tf_op jit(solution)/shard_map/ppermute | solution.py:590
  37.5 6.6 %collective-permute-start.7 = (f32[2,16,128]{2,1,0:T(8,128)S(1)}, f32[2,16,128]{2,1,0:T(8,128)S(1)}, u32[]{:S(2)}, u32[]{:S(2)}) collective-permute-start(f32[2,16,128]{2,1,0:T(8,128)S(1)} %get-tuple-element.25.refs_0_), channel_id=1, source_target_pairs={{1,128},{16,144},{32,160},{48,176},{64,192},{80,208},{96,224},{112... | collective-permute-start | bytes 49160 | tf_op jit(solution)/shard_map/ppermute | solution.py:590
  40.0 5.1 %collective-permute-start.6 = (f32[2,16,128]{2,1,0:T(8,128)S(1)}, f32[2,16,128]{2,1,0:T(8,128)S(1)}, u32[]{:S(2)}, u32[]{:S(2)}) collective-permute-start(f32[2,16,128]{2,1,0:T(8,128)S(1)} %get-tuple-element.25.refs_0_), channel_id=1, source_target_pairs={{1,64},{16,80},{32,96},{48,112},{64,1},{80,16},{96,32},{112,48},{1... | collective-permute-start | bytes 49160 | tf_op jit(solution)/shard_map/ppermute | solution.py:590
  42.2 3.6 %collective-permute-start.11 = (f32[2,48,128]{2,1,0:T(8,128)S(1)}, f32[2,48,128]{2,1,0:T(8,128)S(1)}, u32[]{:S(2)}, u32[]{:S(2)}) collective-permute-start(f32[2,48,128]{2,1,0:T(8,128)S(1)} %get-tuple-element.26.refs_4_), channel_id=1, source_target_pairs={{0,6},{17,7},{2,4},{3,5},{4,2},{5,3},{6,0},{7,17},{8,30},{9,15},{1... | collective-permute-start | bytes 147464 | tf_op jit(solution)/shard_map/ppermute | solution.py:590
  44.0 1.7 %collective-permute-start.10 = (f32[2,48,128]{2,1,0:T(8,128)S(1)}, f32[2,48,128]{2,1,0:T(8,128)S(1)}, u32[]{:S(2)}, u32[]{:S(2)}) collective-permute-start(f32[2,48,128]{2,1,0:T(8,128)S(1)} %get-tuple-element.26.refs_4_), channel_id=1, source_target_pairs={{0,4},{17,5},{2,6},{3,7},{4,0},{5,17},{6,2},{7,3},{8,12},{9,13},{1... | collective-permute-start | bytes 147464 | tf_op jit(solution)/shard_map/ppermute | solution.py:590
  45.1 0.7 collective-permute-start.9
  45.8 21.3 %collective-permute-start.15 = (f32[8,48,128]{2,1,0:T(8,128)S(1)}, f32[8,48,128]{2,1,0:T(8,128)S(1)}, u32[]{:S(2)}, u32[]{:S(2)}) collective-permute-start(f32[8,48,128]{2,1,0:T(8,128)S(1)} %get-tuple-element.28.refs_4_), channel_id=1, source_target_pairs={{0,17},{17,0},{2,3},{3,2},{4,5},{5,4},{6,7},{7,6},{8,9},{9,8},{10,... | collective-permute-start | bytes 589832 | tf_op jit(solution)/shard_map/ppermute | solution.py:590
  46.5 15.0 %collective-permute-start.14 = (f32[8,16,128]{2,1,0:T(8,128)S(1)}, f32[8,16,128]{2,1,0:T(8,128)S(1)}, u32[]{:S(2)}, u32[]{:S(2)}) collective-permute-start(f32[8,16,128]{2,1,0:T(8,128)S(1)} %get-tuple-element.27.refs_0_), channel_id=1, source_target_pairs={{1,48},{16,32},{32,16},{48,1},{64,112},{80,96},{96,80},{112,64},{1... | collective-permute-start | bytes 196616 | tf_op jit(solution)/shard_map/ppermute | solution.py:590
  58.1 7.1 %collective-permute-start.13 = (f32[8,16,128]{2,1,0:T(8,128)S(1)}, f32[8,16,128]{2,1,0:T(8,128)S(1)}, u32[]{:S(2)}, u32[]{:S(2)}) collective-permute-start(f32[8,16,128]{2,1,0:T(8,128)S(1)} %get-tuple-element.27.refs_0_), channel_id=1, source_target_pairs={{1,32},{16,48},{32,1},{48,16},{64,96},{80,112},{96,64},{112,80},{1... | collective-permute-start | bytes 196616 | tf_op jit(solution)/shard_map/ppermute | solution.py:590
  61.5 5.6 %collective-permute-start.12 = (f32[8,16,128]{2,1,0:T(8,128)S(1)}, f32[8,16,128]{2,1,0:T(8,128)S(1)}, u32[]{:S(2)}, u32[]{:S(2)}) collective-permute-start(f32[8,16,128]{2,1,0:T(8,128)S(1)} %get-tuple-element.27.refs_0_), channel_id=1, source_target_pairs={{1,16},{16,1},{32,48},{48,32},{64,80},{80,64},{96,112},{112,96},{1... | collective-permute-start | bytes 196616 | tf_op jit(solution)/shard_map/ppermute | solution.py:590
  67.6 5.7 %collective-permute-start.16 = (f32[256,128]{1,0:T(8,128)S(1)}, f32[256,128]{1,0:T(8,128)S(1)}, u32[]{:S(2)}, u32[]{:S(2)}) collective-permute-start(f32[256,128]{1,0:T(8,128)S(1)} %edges.1), channel_id=1, source_target_pairs={{1,0},{17,1},{14,15},{30,14},{497,496},{481,497},{510,511},{494,510}} | collective-permute-start | bytes 393224 | tf_op jit(solution)/shard_map/ppermute | solution.py:647

commit v5 on v4

--- a/solution.py
+++ b/solution.py
@@ -18,6 +18,7 @@
 VERT_AT = COEF_AT + LV * COEF_ROWS
 XROWS = 184
 CORNER_AT = NG * XROWS
+FIRST = 10
 SENT = CORNER_AT + 16 * NG
 
 
@@ -71,6 +72,7 @@
     for step in range(3):
         chain_y[0, 16 * step : 16 * step + 16, :] = rows_we[step]
         square[16 * step : 16 * step + 16, 0:16] = rows_sn[step]
+    chain_x[...] = jnp.zeros((FIRST, 16, 128), jnp.float32)
     chain_x[0] = square[...].T[0:16]
     square[0:48, :] = jnp.zeros((48, 128), jnp.float32)
     square[96:112, 0:16] = fill_sn[0]
@@ -164,16 +166,16 @@
     for out, parts in ((out_x, ins[:count_x]), (out_y, ins[count_x : count_x + count_y])):
         at = 0
         for part in parts:
-            out[at : at + part.shape[0]] = part[...]
-            at += part.shape[0]
-
-
-def edge_kernel(count_x, count_y, plan_x, plan_y, ra, rb, from_low, from_high, colpack, interp, *refs):
+            size = 1 if part.shape[0] == FIRST else part.shape[0]
+            out[at : at + size] = part[0:size]
+            at += size
+
+
+def edge_kernel(count_x, count_y, plan_x, plan_y, pack, from_low, from_high, interp, *refs):
     chain_x, refs = refs[: len(plan_x)], refs[len(plan_x) :]
     chain_y, refs = refs[: len(plan_y)], refs[len(plan_y) :]
-    edges, pack = refs
+    (edges,) = refs
     nx, ny = lax.axis_index("nx"), lax.axis_index("ny")
-    odd = nx % 2 == 1
     border_x = (nx == 0) | (nx == count_x - 1)
     border_y = (ny == 0) | (ny == count_y - 1)
     inner_x = (nx == 1) | (nx == count_x - 2)
@@ -210,11 +212,6 @@
 
     @pl.when((border_y & jnp.logical_not(border_x)) | (border_x & inner_y))
     def _():
-        n = CORNER_AT + 8 * (NG - 1)
-        a, b = ra[n : n + 8, :], rb[n : n + 8, :]
-        pack[0:HX, :] = jnp.where(odd, b, a)
-        pack[HX : HX + WX, :] = colpack[...]
-        pack[HX + WX : 64, :] = jnp.where(odd, a, b)
         index = pack[:, 64:65].astype(jnp.int32)
         weight = pack[:, 65:66]
         total = jnp.zeros((64, 128), jnp.float32)
@@ -234,13 +231,10 @@
         edges[0:64, :] = total
 
 
-def main_kernel(
-    count_x, count_y, jump, state, diffuse, vertical_hbm, fill_we_hbm, ra, rb, from_low, from_high,
-    colpack, edges, brought_ref,
-    out, es, ed, ev, mv, gv, fac, strip, ey, ex, pack, vertical, fill_we, sem,
+def prepare_kernel(
+    state, diffuse, vertical_hbm, ra, rb, from_low, from_high, colpack, es, ed, ev, inv, pack, strip, vertical, sem
 ):
-    dx, dy = jump[0], jump[1]
-    nx, ny = lax.axis_index("nx"), lax.axis_index("ny")
+    nx = lax.axis_index("nx")
     copies = []
     for which, (src, dst) in enumerate(((state, es), (diffuse, ed))):
         for l in range(NG):
@@ -251,12 +245,10 @@
             copies.append(copy)
     first_copies = [
         pltpu.make_async_copy(vertical_hbm, vertical, sem.at[2 * NG]),
-        pltpu.make_async_copy(fill_we_hbm, fill_we, sem.at[2 * NG + 1]),
     ]
     for copy in first_copies:
         copy.start()
     odd = nx % 2 == 1
-    lane = lax.broadcasted_iota(jnp.int32, (8, 128), 1)
     lane64 = lax.broadcasted_iota(jnp.int32, (64, 128), 1)
 
     def beyond(at, size, l):
@@ -305,6 +297,32 @@
         lane64 < 64, strip[1, :, 256:384], pltpu.roll(strip[0, :, 256:384], 120, 1)
     )
 
+
+    @pl.loop(0, 8)
+    def _(t):
+        rows = pl.ds(pl.multiple_of(8 * t, 8), 8)
+        for l in range(NG + 1):
+            g = ev[l, rows, :]
+            inverse = 1.0 / (1.0 + g)
+            inv[0, l, rows, :] = inverse
+            for k in range(1, LV):
+                diagonal = 1.0 + (g if k == LV - 1 else 2.0 * g)
+                inverse = 1.0 / (diagonal - g * (g * inverse))
+                inv[k, l, rows, :] = inverse
+
+    for copy in copies:
+        copy.wait()
+
+
+def main_kernel(
+    count_x, count_y, jump, fill_we_hbm, from_low, from_high, es_in, ed, ev, inv, pack, edges, brought_ref,
+    out, es, mv, gv, ey, ex, fill_we, sem,
+):
+    dx, dy = jump[0], jump[1]
+    nx, ny = lax.axis_index("nx"), lax.axis_index("ny")
+    lane = lax.broadcasted_iota(jnp.int32, (8, 128), 1)
+    fetch = pltpu.make_async_copy(fill_we_hbm, fill_we, sem)
+    fetch.start()
     west, east = nx == 0, nx == count_x - 1
     south, north = ny == 0, ny == count_y - 1
 
@@ -348,8 +366,6 @@
                 col = ex[56:64, 16 * step + k : 16 * step + k + 1]
                 es[k, NG, 56:64, :] = jnp.where(lane == at, col, es[k, NG, 56:64, :])
 
-    for copy in copies:
-        copy.wait()
     ghosts(es, 0, HX - 1, HX + WX, 0)
     ghost_tail(0)
 
@@ -363,7 +379,7 @@
 
     def advance(field, at, coef_at, groups, write_source, read_source, write):
         g = [ev[l, pl.ds(coef_at, 8), :] for l in range(groups)]
-        factor, source = [None] * groups, [None] * groups
+        source = [None] * groups
         for k in range(LV):
             c = [field[k, l, pl.ds(at, 8), :] for l in range(NG + 1)]
             left, right = sideways(c)
@@ -376,20 +392,17 @@
                     - 4.0 * c[l]
                 )
                 explicit = c[l] + ed[k, l, pl.ds(coef_at, 8), :] * lap
-                diagonal = 1.0 + (g[l] if k in (0, LV - 1) else 2.0 * g[l])
                 if k > 0:
-                    diagonal = diagonal + g[l] * factor[l]
                     explicit = explicit + g[l] * source[l]
-                inverse = 1.0 / diagonal
-                factor[l] = -g[l] * inverse
-                source[l] = explicit * inverse
-                fac[k, l] = factor[l]
+                source[l] = explicit * inv[k, l, pl.ds(coef_at, 8), :]
                 if k < LV - 1:
                     write_source(k, l, source[l])
         value = source
         write(LV - 1, value)
         for k in range(LV - 2, -1, -1):
-            value = [read_source(k, l) - fac[k, l] * value[l] for l in range(groups)]
+            value = [
+                read_source(k, l) + (g[l] * inv[k, l, pl.ds(coef_at, 8), :]) * value[l] for l in range(groups)
+            ]
             write(k, value)
 
     turn = (128 - 3 * dy) % 128
@@ -432,6 +445,8 @@
                     n = 96 + 16 * side + k
                     mv[k, l, 0:56, :] = jnp.where(inside, total[:, n : n + 1], mv[k, l, 0:56, :])
 
+    fetch.wait()
+
     @pl.when((west & (dx < 0)) | (east & (dx > 0)))
     def _():
         lane16 = lax.broadcasted_iota(jnp.int32, (16, 128), 1)
@@ -442,8 +457,8 @@
                 own = fill_we[side]
                 ring = jnp.where(
                     lane16 < 64,
-                    pltpu.roll(strip[1, HX + 16 * side : HX + 16 * side + 16, 256:384], 120, 1),
-                    pltpu.roll(strip[0, HX + 16 * side : HX + 16 * side + 16, 256:384], 112, 1),
+                    pltpu.roll(from_high[16 * side : 16 * side + 16, 256:384], 120, 1),
+                    pltpu.roll(from_low[16 * side : 16 * side + 16, 256:384], 112, 1),
                 )
                 for l in range(NG + 1):
                     column = lane16 + 128 * l
@@ -531,7 +546,7 @@
         out_shape=(
             shape(WX, WY),
             shape(WX, WY),
-            shape(1, 16, 128),
+            shape(FIRST, 16, 128),
             shape(1, 48, 128),
             shape(WX, 128),
             shape(8, WY),
@@ -592,12 +607,12 @@
 
     along_x, along_y = functools.partial(along, set_x), functools.partial(along, set_y)
 
-    def join(parts_x, parts_y, name):
+    def join(parts_x, parts_y, size_x, size_y, name):
         return pl.pallas_call(
             functools.partial(join_kernel, len(parts_x), len(parts_y)),
             out_shape=(
-                shape(sum(p.shape[0] for p in parts_x), 16, 128),
-                shape(sum(p.shape[0] for p in parts_y), 48, 128),
+                shape(size_x, 16, 128),
+                shape(size_y, 48, 128),
             ),
             in_specs=[vmem] * (len(parts_x) + len(parts_y)),
             out_specs=(vmem, vmem),
@@ -625,12 +640,26 @@
     )(parts_x[-1], parts_y[-1], state, diffuse, vertical, from_low, from_high, colpack)
     ra = lax.ppermute(xa, "nx", pairs_a)
     rb = lax.ppermute(xb, "nx", pairs_b)
-    chain_x, chain_y = join(parts_x, parts_y, "join_first")
+    chain_x, chain_y = join(parts_x, parts_y, len(masks_of(rounds_x[:1])), len(masks_of(rounds_y[:1])), "join_first")
     parts_x = [chain_x] + along_x(chain_x, rounds_x[1])
     parts_y = [chain_y] + along_y(chain_y, rounds_y[1])
-    chain_x, chain_y = join(parts_x, parts_y, "join_second")
+    chain_x, chain_y = join(parts_x, parts_y, len(masks_of(rounds_x[:2])), len(masks_of(rounds_y[:2])), "join_second")
     parts_x = [chain_x] + along_x(chain_x, rounds_x[2])
     parts_y = [chain_y] + along_y(chain_y, rounds_y[2])
+    big = (LV, NG + 1, 72, 128)
+    es, ed, ev, inv, pack = pl.pallas_call(
+        prepare_kernel,
+        out_shape=(shape(*big), shape(*big), shape(NG + 1, 72, 128), shape(*big), shape(64, 128)),
+        in_specs=[hbm] * 3 + [vmem] * 5,
+        out_specs=(vmem,) * 5,
+        scratch_shapes=[
+            pltpu.VMEM((2, 64, WY), f32),
+            pltpu.VMEM((WX, WY), f32),
+            pltpu.SemaphoreType.DMA((2 * NG + 1,)),
+        ],
+        compiler_params=pltpu.CompilerParams(vmem_limit_bytes=12 << 20),
+        name="prepare",
+    )(state, diffuse, vertical, ra, rb, from_low, from_high, colpack)
     have_x, have_y = masks_of(rounds_x[:2]), masks_of(rounds_y[:2])
     plan_x = [[m ^ h for h in have_x] for m in [0] + rounds_x[2]]
     plan_y = [[m ^ h for h in have_y] for m in [0] + rounds_y[2]]
@@ -638,40 +667,30 @@
     edges = pl.pallas_call(
         functools.partial(edge_kernel, count_x, count_y, plan_x, plan_y),
         out_shape=shape(256, 128),
-        in_specs=[vmem] * (6 + len(parts_x) + len(parts_y)),
+        in_specs=[vmem] * (4 + len(parts_x) + len(parts_y)),
         out_specs=vmem,
-        scratch_shapes=[pltpu.VMEM((64, 128), f32)],
         compiler_params=pltpu.CompilerParams(vmem_limit_bytes=8 << 20),
         name="edges",
-    )(ra, rb, from_low, from_high, colpack, interp, *parts_x, *parts_y)
+    )(pack, from_low, from_high, interp, *parts_x, *parts_y)
     brought = lax.ppermute(edges, both, bring)
 
     return pl.pallas_call(
         functools.partial(main_kernel, count_x, count_y),
-        out_shape=shape(LV, WX, WY),
-        in_specs=[smem] + [hbm] * 4 + [vmem] * 7,
-        out_specs=vmem,
+        out_shape=(shape(LV, WX, WY), shape(*big)),
+        in_specs=[smem, hbm] + [vmem] * 9,
+        out_specs=(vmem, vmem),
         scratch_shapes=[
-            pltpu.VMEM((LV, NG + 1, 72, 128), f32),
-            pltpu.VMEM((LV, NG + 1, 72, 128), f32),
-            pltpu.VMEM((NG + 1, 72, 128), f32),
             pltpu.VMEM((LV, NG + 1, 64, 128), f32),
             pltpu.VMEM((LV, NG + 1, 64, 128), f32),
-            pltpu.VMEM((LV, NG + 1, 8, 128), f32),
-            pltpu.VMEM((2, 64, WY), f32),
             pltpu.VMEM((NG + 1, 48, 128), f32),
             pltpu.VMEM((64, 128), f32),
-            pltpu.VMEM((64, 128), f32),
-            pltpu.VMEM((WX, WY), f32),
             pltpu.VMEM((2, 16, 128), f32),
-            pltpu.SemaphoreType.DMA((2 * NG + 2,)),
+            pltpu.SemaphoreType.DMA,
         ],
-        compiler_params=pltpu.CompilerParams(vmem_limit_bytes=22 << 20),
+        input_output_aliases={4: 1},
+        compiler_params=pltpu.CompilerParams(vmem_limit_bytes=20 << 20),
         name="steps",
-    )(
-        jump, state, diffuse, vertical, fill_we, ra, rb, from_low, from_high,
-        colpack, edges, brought,
-    )
+    )(jump, fill_we, from_low, from_high, es, ed, ev, inv, pack, edges, brought)[0]
 
 
 def solution(mesh):

time: 83.8 us -> 81.1 us (0.968)
  waiting for transfers between devices: 12.7 us -> 6.66 us
  starting transfers between devices: 56.4 us -> 58.5 us
  Pallas kernels: 14 us -> 15.1 us
    ppermute x1, starting transfers between devices: 1.92 us -> 9.76 us  [on_device(): rb = lax.ppermute(xb, 'nx', pairs_b)]
    ppermute x12, waiting for transfers between devices: 8.89 us -> 1.11 us  [along(): lax.ppermute(chain, both, [(own[n], own[n ^ m]) for own in sets for n in...]
    pallas_call x0 -> x1, Pallas kernels: none -> 3.53 us  [on_device(): pl.pallas_call(prepare_kernel, out_shape=(shape(*big), shape(*big), shape...]
    ppermute x1, starting transfers between devices: 4.94 us -> 1.92 us  [on_device(): from_low = lax.ppermute(y_high, 'ny', up)]
    ppermute x1, starting transfers between devices: 5.14 us -> 2.41 us  [on_device(): from_high = lax.ppermute(y_low, 'ny', down)]
    ppermute x1, waiting for transfers between devices: 0.01 us -> 2.57 us  [on_device(): from_high = lax.ppermute(y_low, 'ny', down)]
    pallas_call x1, Pallas kernels: 10 us -> 7.6 us  [on_device(): pl.pallas_call(functools.partial(main_kernel, count_x, count_y), out_shap...]
    ppermute x1, starting transfers between devices: 1.92 us -> 4.33 us  [on_device(): brought = lax.ppermute(edges, both, bring)]
  transfers between devices with their start and end apart: 17 -> 17, of which waited for: 6 -> 3; matrix products, arithmetic and copies ran while one was open for 0% -> 0% of each run, Pallas kernels for 0% -> 4%
where the time goes in v5:
time: 81.1 us; the launch traced here: 80.6 us
  starting transfers between devices  58.5 us (72%)
  Pallas kernels  15.1 us (19%)
  waiting for transfers between devices  6.66 us (8%)
    ppermute x12, starting transfers between devices, along(): lax.ppermute(chain, both, [(own[n], own[n ^ m]) for own in sets for n in...  39.4 us
    ppermute x1, starting transfers between devices, on_device(): rb = lax.ppermute(xb, 'nx', pairs_b)  9.76 us
    pallas_call x1, Pallas kernels, on_device(): pl.pallas_call(functools.partial(main_kernel, count_x, count_y), out_shap...  7.6 us
    ppermute x1, starting transfers between devices, on_device(): brought = lax.ppermute(edges, both, bring)  4.33 us
    pallas_call x1, Pallas kernels, on_device(): pl.pallas_call(prepare_kernel, out_shape=(shape(*big), shape(*big), shape...  3.53 us
    ppermute x1, waiting for transfers between devices, on_device(): brought = lax.ppermute(edges, both, bring)  2.97 us
    ppermute x1, waiting for transfers between devices, on_device(): from_high = lax.ppermute(y_low, 'ny', down)  2.57 us
    ppermute x1, starting transfers between devices, on_device(): from_high = lax.ppermute(y_low, 'ny', down)  2.41 us
  transfers between devices with their start and end apart: 17, of which 3 were waited for; matrix products, arithmetic and copies ran while one was open for 0% of the time, Pallas kernels for 4%

profile of v5, /device:TPU:1, one launch (start us, length us, event | category | flops | bytes accessed | tf_op | source)
XLA Modules:
  0.0 80.6 jit_solution(8969694940345970997)
XLA Ops:
  0.0 2.1 %pack.1 = (f32[48,384]{1,0:T(8,128)S(1)}, f32[48,384]{1,0:T(8,128)S(1)}, f32[10,16,128]{2,1,0:T(8,128)S(1)}, f32[1,48,128]{2,1,0:T(8,128)S(1)}, f32[48,128]{1,0:T(8,128)S(1)}, /*index=5*/f32[8,384]{1,0:T(8,128)S(1)}) custom-call(f32[16,48,384]{2,1,0:T(8,128)} %state.1, f32[16,48,384]{2,1,0:T(8,128)} %diffuse.1, f32[48,384]{1,0:T(8,128)} %vertical_hbm.5, ...), custom_call_target="tpu_custom_call" | custom-call | tf_op jit(solution)/shard_map/pack/pallas_call | solution.py:544
  2.1 16.8 %collective-permute-start.2 = (f32[10,16,128]{2,1,0:T(8,128)S(1)}, f32[10,16,128]{2,1,0:T(8,128)S(1)}, u32[]{:S(2)}, u32[]{:S(2)}) collective-permute-start(f32[10,16,128]{2,1,0:T(8,128)S(1)} %get-tuple-element.25.refs_0_), channel_id=1, source_target_pairs={{1,256},{16,272},{32,288},{48,304},{64,320},{80,336},{96,352},{112... | collective-permute-start | bytes 245768 | tf_op jit(solution)/shard_map/ppermute | solution.py:605
  19.0 1.9 %collective-permute-start = (f32[48,384]{1,0:T(8,128)S(1)}, f32[48,384]{1,0:T(8,128)S(1)}, u32[]{:S(2)}, u32[]{:S(2)}) collective-permute-start(f32[48,384]{1,0:T(8,128)S(1)} %get-tuple-element.23), channel_id=1, source_target_pairs={{0,1},{1,2},{2,3},{3,4},{4,5},{5,6},{6,7},{7,8},{8,9},{9,10},{10,1... | collective-permute-start | bytes 221192 | tf_op jit(solution)/shard_map/ppermute | solution.py:625
  20.9 2.4 %collective-permute-start.1 = (f32[48,384]{1,0:T(8,128)S(1)}, f32[48,384]{1,0:T(8,128)S(1)}, u32[]{:S(2)}, u32[]{:S(2)}) collective-permute-start(f32[48,384]{1,0:T(8,128)S(1)} %get-tuple-element.24), channel_id=1, source_target_pairs={{1,0},{2,1},{3,2},{4,3},{5,4},{6,5},{7,6},{8,7},{9,8},{10,9},{11,1... | collective-permute-start | bytes 221192 | tf_op jit(solution)/shard_map/ppermute | solution.py:626
  23.3 0.7 collective-permute-start.3
  24.0 0.0 collective-permute-done.3.after_y.refs_3_
  24.0 0.0 collective-permute-done.from_low
  24.0 2.6 %collective-permute-done.1.from_high = f32[48,384]{1,0:T(8,128)S(1)} collective-permute-done((f32[48,384]{1,0:T(8,128)S(1)}, f32[48,384]{1,0:T(8,128)S(1)}, u32[]{:S(2)}, u32[]{:S(2)}) %collective-permute-start.1) | collective-permute-done | bytes 73760 | tf_op jit(solution)/shard_map/ppermute | solution.py:626
  26.6 0.0 collective-permute-done.2.after_x.refs_1_
  26.6 1.4 %border.1 = (f32[600,128]{1,0:T(8,128)S(1)}, f32[600,128]{1,0:T(8,128)S(1)}) custom-call(f32[10,16,128]{2,1,0:T(8,128)S(1)} %collective-permute-done.2.after_x.refs_1_, f32[1,48,128]{2,1,0:T(8,128)S(1)} %collective-permute-done.3.after_y.refs_3_, f32[16,48,384]{2,1,0:T(8,128)} %state.1, f32[16,48,384]{2,1,0:T(8,128)} %diffuse.1, f32[48,384]{1,0:T(8,128)} %vertical_hbm.5, ...), custom_call_target="tpu_custom_call" | custom-call | tf_op jit(solution)/shard_map/border/pallas_call | solution.py:627
  28.0 0.0 copy-start
  28.0 0.7 collective-permute-start.4
  28.7 9.8 %collective-permute-start.5 = (f32[600,128]{1,0:T(8,128)S(1)}, f32[600,128]{1,0:T(8,128)S(1)}, u32[]{:S(2)}, u32[]{:S(2)}) collective-permute-start(f32[600,128]{1,0:T(8,128)S(1)} %get-tuple-element.29), channel_id=1, source_target_pairs={{0,16},{32,48},{64,80},{96,112},{128,144},{160,176},{192,208},{224... | collective-permute-start | bytes 921608 | tf_op jit(solution)/shard_map/ppermute | solution.py:642
  38.4 1.9 %collective-permute-start.8 = (f32[2,16,128]{2,1,0:T(8,128)S(1)}, f32[2,16,128]{2,1,0:T(8,128)S(1)}, u32[]{:S(2)}, u32[]{:S(2)}) collective-permute-start(f32[2,16,128]{2,1,0:T(8,128)S(1)} %get-tuple-element.36.refs_0_), channel_id=1, source_target_pairs={{1,192},{16,208},{32,224},{48,240},{64,128},{80,144},{96,160},{112... | collective-permute-start | bytes 49160 | tf_op jit(solution)/shard_map/ppermute | solution.py:605
  40.4 1.9 %collective-permute-start.7 = (f32[2,16,128]{2,1,0:T(8,128)S(1)}, f32[2,16,128]{2,1,0:T(8,128)S(1)}, u32[]{:S(2)}, u32[]{:S(2)}) collective-permute-start(f32[2,16,128]{2,1,0:T(8,128)S(1)} %get-tuple-element.36.refs_0_), channel_id=1, source_target_pairs={{1,128},{16,144},{32,160},{48,176},{64,192},{80,208},{96,224},{112... | collective-permute-start | bytes 49160 | tf_op jit(solution)/shard_map/ppermute | solution.py:605
  42.3 5.7 %collective-permute-start.6 = (f32[2,16,128]{2,1,0:T(8,128)S(1)}, f32[2,16,128]{2,1,0:T(8,128)S(1)}, u32[]{:S(2)}, u32[]{:S(2)}) collective-permute-start(f32[2,16,128]{2,1,0:T(8,128)S(1)} %get-tuple-element.36.refs_0_), channel_id=1, source_target_pairs={{1,64},{16,80},{32,96},{48,112},{64,1},{80,16},{96,32},{112,48},{1... | collective-permute-start | bytes 49160 | tf_op jit(solution)/shard_map/ppermute | solution.py:605
  48.0 0.0 collective-permute-done.8.refs_3_
  48.0 0.7 collective-permute-start.11
  48.7 0.0 collective-permute-done.7.refs_2_
  48.7 0.7 collective-permute-start.10
  49.4 0.0 collective-permute-done.6.refs_1_
  49.4 0.7 collective-permute-start.9
  50.1 0.0 collective-permute-done.11.refs_7_
  50.1 0.0 collective-permute-done.10.refs_6_
  50.1 0.0 collective-permute-done.9.refs_5_
  50.1 0.7 collective-permute-start.15
  50.8 4.5 %collective-permute-start.14 = (f32[8,16,128]{2,1,0:T(8,128)S(1)}, f32[8,16,128]{2,1,0:T(8,128)S(1)}, u32[]{:S(2)}, u32[]{:S(2)}) collective-permute-start(f32[8,16,128]{2,1,0:T(8,128)S(1)} %get-tuple-element.38.refs_0_), channel_id=1, source_target_pairs={{1,48},{16,32},{32,16},{48,1},{64,112},{80,96},{96,80},{112,64},{1... | collective-permute-start | bytes 196616 | tf_op jit(solution)/shard_map/ppermute | solution.py:605
  55.3 3.4 %collective-permute-start.13 = (f32[8,16,128]{2,1,0:T(8,128)S(1)}, f32[8,16,128]{2,1,0:T(8,128)S(1)}, u32[]{:S(2)}, u32[]{:S(2)}) collective-permute-start(f32[8,16,128]{2,1,0:T(8,128)S(1)} %get-tuple-element.38.refs_0_), channel_id=1, source_target_pairs={{1,32},{16,48},{32,1},{48,16},{64,96},{80,112},{96,64},{112,80},{1... | collective-permute-start | bytes 196616 | tf_op jit(solution)/shard_map/ppermute | solution.py:605
  58.7 0.0 collective-permute-done.4.ra
  58.7 1.9 %collective-permute-start.12 = (f32[8,16,128]{2,1,0:T(8,128)S(1)}, f32[8,16,128]{2,1,0:T(8,128)S(1)}, u32[]{:S(2)}, u32[]{:S(2)}) collective-permute-start(f32[8,16,128]{2,1,0:T(8,128)S(1)} %get-tuple-element.38.refs_0_), channel_id=1, source_target_pairs={{1,16},{16,1},{32,48},{48,32},{64,80},{80,64},{96,112},{112,96},{1... | collective-permute-start | bytes 196616 | tf_op jit(solution)/shard_map/ppermute | solution.py:605
  60.6 0.0 collective-permute-done.5.rb
  60.6 3.5 %prepare.1 = (f32[16,4,72,128]{3,2,1,0:T(8,128)S(1)}, f32[16,4,72,128]{3,2,1,0:T(8,128)S(1)}, f32[4,72,128]{2,1,0:T(8,128)S(1)}, f32[16,4,72,128]{3,2,1,0:T(8,128)S(1)}, f32[64,128]{1,0:T(8,128)S(1)}) custom-call(f32[16,48,384]{2,1,0:T(8,128)} %state.1, f32[16,48,384]{2,1,0:T(8,128)} %diffuse.1, f32[48,384]{1,0:T(8,128)} %vertical_hbm.5, ...), custom_call_target="tpu_custom_call" | custom-call | tf_op jit(solution)/shard_map/prepare/pallas_call | solution.py:650
  64.1 0.0 collective-permute-done.14.refs_3_
  64.2 0.0 collective-permute-done.13.refs_2_
  64.2 1.0 %collective-permute-done.12.refs_1_ = f32[8,16,128]{2,1,0:T(8,128)S(1)} collective-permute-done((f32[8,16,128]{2,1,0:T(8,128)S(1)}, f32[8,16,128]{2,1,0:T(8,128)S(1)}, u32[]{:S(2)}, u32[]{:S(2)}) %collective-permute-start.12) | collective-permute-done | bytes 65568 | tf_op jit(solution)/shard_map/ppermute | solution.py:605
  65.2 0.0 collective-permute-done.15.refs_5_
  65.2 0.4 edges.1
  65.6 4.3 %collective-permute-start.16 = (f32[256,128]{1,0:T(8,128)S(1)}, f32[256,128]{1,0:T(8,128)S(1)}, u32[]{:S(2)}, u32[]{:S(2)}) collective-permute-start(f32[256,128]{1,0:T(8,128)S(1)} %edges.1), channel_id=1, source_target_pairs={{1,0},{17,1},{14,15},{30,14},{497,496},{481,497},{510,511},{494,510}} | collective-permute-start | bytes 393224 | tf_op jit(solution)/shard_map/ppermute | solution.py:675
  70.0 3.0 %collective-permute-done.16.brought_ref = f32[256,128]{1,0:T(8,128)S(1)} collective-permute-done((f32[256,128]{1,0:T(8,128)S(1)}, f32[256,128]{1,0:T(8,128)S(1)}, u32[]{:S(2)}, u32[]{:S(2)}) %collective-permute-start.16) | collective-permute-done | bytes 131104 | tf_op jit(solution)/shard_map/ppermute | solution.py:675
  72.9 0.0 copy-done
  72.9 7.6 %steps.1 = (f32[16,48,384]{2,1,0:T(8,128)}, f32[16,4,72,128]{3,2,1,0:T(8,128)S(1)}) custom-call(s32[2]{0:T(128)S(1)} %copy-done, f32[2,16,128]{2,1,0:T(8,128)} %fill_we_hbm.3, f32[48,384]{1,0:T(8,128)S(1)} %collective-permute-done.from_low, f32[48,384]{1,0:T(8,128)S(1)} %collective-permute-done.1.from_high, ...), custom_call_target="tpu_custom_call", output_to_operand_aliasing={{1}: (4, {})} | custom-call | tf_op jit(solution)/shard_map/steps/pallas_call | solution.py:677
  (2 shorter events, 0.0 us)
Async XLA Ops:
  2.1 24.4 %collective-permute-start.2 = (f32[10,16,128]{2,1,0:T(8,128)S(1)}, f32[10,16,128]{2,1,0:T(8,128)S(1)}, u32[]{:S(2)}, u32[]{:S(2)}) collective-permute-start(f32[10,16,128]{2,1,0:T(8,128)S(1)} %get-tuple-element.25.refs_0_), channel_id=1, source_target_pairs={{1,256},{16,272},{32,288},{48,304},{64,320},{80,336},{96,352},{112... | collective-permute-start | bytes 245768 | tf_op jit(solution)/shard_map/ppermute | solution.py:605
  19.0 5.0 %collective-permute-start = (f32[48,384]{1,0:T(8,128)S(1)}, f32[48,384]{1,0:T(8,128)S(1)}, u32[]{:S(2)}, u32[]{:S(2)}) collective-permute-start(f32[48,384]{1,0:T(8,128)S(1)} %get-tuple-element.23), channel_id=1, source_target_pairs={{0,1},{1,2},{2,3},{3,4},{4,5},{5,6},{6,7},{7,8},{8,9},{9,10},{10,1... | collective-permute-start | bytes 221192 | tf_op jit(solution)/shard_map/ppermute | solution.py:625
  20.9 5.7 %collective-permute-start.1 = (f32[48,384]{1,0:T(8,128)S(1)}, f32[48,384]{1,0:T(8,128)S(1)}, u32[]{:S(2)}, u32[]{:S(2)}) collective-permute-start(f32[48,384]{1,0:T(8,128)S(1)} %get-tuple-element.24), channel_id=1, source_target_pairs={{1,0},{2,1},{3,2},{4,3},{5,4},{6,5},{7,6},{8,7},{9,8},{10,9},{11,1... | collective-permute-start | bytes 221192 | tf_op jit(solution)/shard_map/ppermute | solution.py:626
  23.3 0.7 collective-permute-start.3
  28.0 45.0 %copy-start = (s32[2]{0:T(128)S(1)}, s32[2]{0:T(128)}, u32[]{:S(2)}) copy-start(s32[2]{0:T(128)} %jump.1) | copy-start | bytes 28
  28.0 30.7 %collective-permute-start.4 = (f32[600,128]{1,0:T(8,128)S(1)}, f32[600,128]{1,0:T(8,128)S(1)}, u32[]{:S(2)}, u32[]{:S(2)}) collective-permute-start(f32[600,128]{1,0:T(8,128)S(1)} %get-tuple-element.28), channel_id=1, source_target_pairs={{16,32},{48,64},{80,96},{112,128},{144,160},{176,192},{208,224},{2... | collective-permute-start | bytes 921608 | tf_op jit(solution)/shard_map/ppermute | solution.py:641
  28.7 31.9 %collective-permute-start.5 = (f32[600,128]{1,0:T(8,128)S(1)}, f32[600,128]{1,0:T(8,128)S(1)}, u32[]{:S(2)}, u32[]{:S(2)}) collective-permute-start(f32[600,128]{1,0:T(8,128)S(1)} %get-tuple-element.29), channel_id=1, source_target_pairs={{0,16},{32,48},{64,80},{96,112},{128,144},{160,176},{192,208},{224... | collective-permute-start | bytes 921608 | tf_op jit(solution)/shard_map/ppermute | solution.py:642
  38.4 9.6 %collective-permute-start.8 = (f32[2,16,128]{2,1,0:T(8,128)S(1)}, f32[2,16,128]{2,1,0:T(8,128)S(1)}, u32[]{:S(2)}, u32[]{:S(2)}) collective-permute-start(f32[2,16,128]{2,1,0:T(8,128)S(1)} %get-tuple-element.36.refs_0_), channel_id=1, source_target_pairs={{1,192},{16,208},{32,224},{48,240},{64,128},{80,144},{96,160},{112... | collective-permute-start | bytes 49160 | tf_op jit(solution)/shard_map/ppermute | solution.py:605
  40.4 8.3 %collective-permute-start.7 = (f32[2,16,128]{2,1,0:T(8,128)S(1)}, f32[2,16,128]{2,1,0:T(8,128)S(1)}, u32[]{:S(2)}, u32[]{:S(2)}) collective-permute-start(f32[2,16,128]{2,1,0:T(8,128)S(1)} %get-tuple-element.36.refs_0_), channel_id=1, source_target_pairs={{1,128},{16,144},{32,160},{48,176},{64,192},{80,208},{96,224},{112... | collective-permute-start | bytes 49160 | tf_op jit(solution)/shard_map/ppermute | solution.py:605
  42.3 7.1 %collective-permute-start.6 = (f32[2,16,128]{2,1,0:T(8,128)S(1)}, f32[2,16,128]{2,1,0:T(8,128)S(1)}, u32[]{:S(2)}, u32[]{:S(2)}) collective-permute-start(f32[2,16,128]{2,1,0:T(8,128)S(1)} %get-tuple-element.36.refs_0_), channel_id=1, source_target_pairs={{1,64},{16,80},{32,96},{48,112},{64,1},{80,16},{96,32},{112,48},{1... | collective-permute-start | bytes 49160 | tf_op jit(solution)/shard_map/ppermute | solution.py:605
  48.0 2.1 %collective-permute-start.11 = (f32[2,48,128]{2,1,0:T(8,128)S(1)}, f32[2,48,128]{2,1,0:T(8,128)S(1)}, u32[]{:S(2)}, u32[]{:S(2)}) collective-permute-start(f32[2,48,128]{2,1,0:T(8,128)S(1)} %get-tuple-element.37.refs_4_), channel_id=1, source_target_pairs={{0,6},{17,7},{2,4},{3,5},{4,2},{5,3},{6,0},{7,17},{8,30},{9,15},{1... | collective-permute-start | bytes 147464 | tf_op jit(solution)/shard_map/ppermute | solution.py:605
  48.7 1.4 %collective-permute-start.10 = (f32[2,48,128]{2,1,0:T(8,128)S(1)}, f32[2,48,128]{2,1,0:T(8,128)S(1)}, u32[]{:S(2)}, u32[]{:S(2)}) collective-permute-start(f32[2,48,128]{2,1,0:T(8,128)S(1)} %get-tuple-element.37.refs_4_), channel_id=1, source_target_pairs={{0,4},{17,5},{2,6},{3,7},{4,0},{5,17},{6,2},{7,3},{8,12},{9,13},{1... | collective-permute-start | bytes 147464 | tf_op jit(solution)/shard_map/ppermute | solution.py:605
  49.4 0.7 collective-permute-start.9
  50.1 15.1 %collective-permute-start.15 = (f32[8,48,128]{2,1,0:T(8,128)S(1)}, f32[8,48,128]{2,1,0:T(8,128)S(1)}, u32[]{:S(2)}, u32[]{:S(2)}) collective-permute-start(f32[8,48,128]{2,1,0:T(8,128)S(1)} %get-tuple-element.39.refs_4_), channel_id=1, source_target_pairs={{0,17},{17,0},{2,3},{3,2},{4,5},{5,4},{6,7},{7,6},{8,9},{9,8},{10,... | collective-permute-start | bytes 589832 | tf_op jit(solution)/shard_map/ppermute | solution.py:605
  50.8 13.3 %collective-permute-start.14 = (f32[8,16,128]{2,1,0:T(8,128)S(1)}, f32[8,16,128]{2,1,0:T(8,128)S(1)}, u32[]{:S(2)}, u32[]{:S(2)}) collective-permute-start(f32[8,16,128]{2,1,0:T(8,128)S(1)} %get-tuple-element.38.refs_0_), channel_id=1, source_target_pairs={{1,48},{16,32},{32,16},{48,1},{64,112},{80,96},{96,80},{112,64},{1... | collective-permute-start | bytes 196616 | tf_op jit(solution)/shard_map/ppermute | solution.py:605
  55.3 8.9 %collective-permute-start.13 = (f32[8,16,128]{2,1,0:T(8,128)S(1)}, f32[8,16,128]{2,1,0:T(8,128)S(1)}, u32[]{:S(2)}, u32[]{:S(2)}) collective-permute-start(f32[8,16,128]{2,1,0:T(8,128)S(1)} %get-tuple-element.38.refs_0_), channel_id=1, source_target_pairs={{1,32},{16,48},{32,1},{48,16},{64,96},{80,112},{96,64},{112,80},{1... | collective-permute-start | bytes 196616 | tf_op jit(solution)/shard_map/ppermute | solution.py:605
  58.7 6.5 %collective-permute-start.12 = (f32[8,16,128]{2,1,0:T(8,128)S(1)}, f32[8,16,128]{2,1,0:T(8,128)S(1)}, u32[]{:S(2)}, u32[]{:S(2)}) collective-permute-start(f32[8,16,128]{2,1,0:T(8,128)S(1)} %get-tuple-element.38.refs_0_), channel_id=1, source_target_pairs={{1,16},{16,1},{32,48},{48,32},{64,80},{80,64},{96,112},{112,96},{1... | collective-permute-start | bytes 196616 | tf_op jit(solution)/shard_map/ppermute | solution.py:605
  65.6 7.3 %collective-permute-start.16 = (f32[256,128]{1,0:T(8,128)S(1)}, f32[256,128]{1,0:T(8,128)S(1)}, u32[]{:S(2)}, u32[]{:S(2)}) collective-permute-start(f32[256,128]{1,0:T(8,128)S(1)} %edges.1), channel_id=1, source_target_pairs={{1,0},{17,1},{14,15},{30,14},{497,496},{481,497},{510,511},{494,510}} | collective-permute-start | bytes 393224 | tf_op jit(solution)/shard_map/ppermute | solution.py:675

commit v6 on v5

--- a/solution.py
+++ b/solution.py
@@ -298,7 +298,7 @@
     )
 
 
-    @pl.loop(0, 8)
+    @pl.loop(0, 8, unroll=True)
     def _(t):
         rows = pl.ds(pl.multiple_of(8 * t, 8), 8)
         for l in range(NG + 1):
@@ -407,7 +407,7 @@
 
     turn = (128 - 3 * dy) % 128
 
-    @pl.loop(0, 7)
+    @pl.loop(0, 7, unroll=True)
     def _(t):
         to = pl.multiple_of(8 * t, 8)
 
@@ -475,7 +475,7 @@
 
     ghosts(mv, 1, 1, WX + 2, HX - 2)
 
-    @pl.loop(0, 7)
+    @pl.loop(0, 7, unroll=True)
     def _(t):
         to = pl.multiple_of(8 * t, 8)
 
@@ -493,7 +493,7 @@
 
     ghosts(gv, 2, 0, WX + 1, HX - 1)
 
-    @pl.loop(0, 6)
+    @pl.loop(0, 6, unroll=True)
     def _(t):
         to = pl.multiple_of(8 * t, 8)
 

time: 81.1 us -> 78.7 us (0.970)
  Pallas kernels: 15.1 us -> 12.7 us
    pallas_call x1, Pallas kernels: 7.6 us -> 6.32 us  [on_device(): pl.pallas_call(functools.partial(main_kernel, count_x, count_y), out_shap...]
    ppermute x12, waiting for transfers between devices: 1.11 us -> 2.19 us  [along(): lax.ppermute(chain, both, [(own[n], own[n ^ m]) for own in sets for n in...]
    ppermute x1, waiting for transfers between devices: 2.97 us -> 1.89 us  [on_device(): brought = lax.ppermute(edges, both, bring)]
    pallas_call x1, Pallas kernels: 3.53 us -> 2.45 us  [on_device(): pl.pallas_call(prepare_kernel, out_shape=(shape(*big), shape(*big), shape...]
  transfers between devices with their start and end apart: 17 -> 17, of which waited for: 3 -> 3; matrix products, arithmetic and copies ran while one was open for 0% -> 0% of each run, Pallas kernels for 4% -> 3%
where the time goes in v6:
time: 78.7 us; the launch traced here: 78.2 us
  starting transfers between devices  58.5 us (74%)
  Pallas kernels  12.7 us (16%)
  waiting for transfers between devices  6.66 us (8%)
    ppermute x12, starting transfers between devices, along(): lax.ppermute(chain, both, [(own[n], own[n ^ m]) for own in sets for n in...  39.4 us
    ppermute x1, starting transfers between devices, on_device(): rb = lax.ppermute(xb, 'nx', pairs_b)  9.76 us
    pallas_call x1, Pallas kernels, on_device(): pl.pallas_call(functools.partial(main_kernel, count_x, count_y), out_shap...  6.32 us
    ppermute x1, starting transfers between devices, on_device(): brought = lax.ppermute(edges, both, bring)  4.33 us
    ppermute x1, waiting for transfers between devices, on_device(): from_high = lax.ppermute(y_low, 'ny', down)  2.57 us
    pallas_call x1, Pallas kernels, on_device(): pl.pallas_call(prepare_kernel, out_shape=(shape(*big), shape(*big), shape...  2.45 us
    ppermute x1, starting transfers between devices, on_device(): from_high = lax.ppermute(y_low, 'ny', down)  2.41 us
    ppermute x12, waiting for transfers between devices, along(): lax.ppermute(chain, both, [(own[n], own[n ^ m]) for own in sets for n in...  2.19 us
  transfers between devices with their start and end apart: 17, of which 3 were waited for; matrix products, arithmetic and copies ran while one was open for 0% of the time, Pallas kernels for 3%

profile of v6, /device:TPU:1, one launch (start us, length us, event | category | flops | bytes accessed | tf_op | source)
XLA Modules:
  0.0 78.2 jit_solution(10514900656901134600)
XLA Ops:
  0.0 2.1 %pack.1 = (f32[48,384]{1,0:T(8,128)S(1)}, f32[48,384]{1,0:T(8,128)S(1)}, f32[10,16,128]{2,1,0:T(8,128)S(1)}, f32[1,48,128]{2,1,0:T(8,128)S(1)}, f32[48,128]{1,0:T(8,128)S(1)}, /*index=5*/f32[8,384]{1,0:T(8,128)S(1)}) custom-call(f32[16,48,384]{2,1,0:T(8,128)} %state.1, f32[16,48,384]{2,1,0:T(8,128)} %diffuse.1, f32[48,384]{1,0:T(8,128)} %vertical_hbm.5, ...), custom_call_target="tpu_custom_call" | custom-call | tf_op jit(solution)/shard_map/pack/pallas_call | solution.py:544
  2.1 16.8 %collective-permute-start.2 = (f32[10,16,128]{2,1,0:T(8,128)S(1)}, f32[10,16,128]{2,1,0:T(8,128)S(1)}, u32[]{:S(2)}, u32[]{:S(2)}) collective-permute-start(f32[10,16,128]{2,1,0:T(8,128)S(1)} %get-tuple-element.25.refs_0_), channel_id=1, source_target_pairs={{1,256},{16,272},{32,288},{48,304},{64,320},{80,336},{96,352},{112... | collective-permute-start | bytes 245768 | tf_op jit(solution)/shard_map/ppermute | solution.py:605
  19.0 1.9 %collective-permute-start = (f32[48,384]{1,0:T(8,128)S(1)}, f32[48,384]{1,0:T(8,128)S(1)}, u32[]{:S(2)}, u32[]{:S(2)}) collective-permute-start(f32[48,384]{1,0:T(8,128)S(1)} %get-tuple-element.23), channel_id=1, source_target_pairs={{0,1},{1,2},{2,3},{3,4},{4,5},{5,6},{6,7},{7,8},{8,9},{9,10},{10,1... | collective-permute-start | bytes 221192 | tf_op jit(solution)/shard_map/ppermute | solution.py:625
  20.9 2.4 %collective-permute-start.1 = (f32[48,384]{1,0:T(8,128)S(1)}, f32[48,384]{1,0:T(8,128)S(1)}, u32[]{:S(2)}, u32[]{:S(2)}) collective-permute-start(f32[48,384]{1,0:T(8,128)S(1)} %get-tuple-element.24), channel_id=1, source_target_pairs={{1,0},{2,1},{3,2},{4,3},{5,4},{6,5},{7,6},{8,7},{9,8},{10,9},{11,1... | collective-permute-start | bytes 221192 | tf_op jit(solution)/shard_map/ppermute | solution.py:626
  23.3 0.7 collective-permute-start.3
  24.0 0.0 collective-permute-done.3.after_y.refs_3_
  24.0 0.0 collective-permute-done.from_low
  24.0 2.6 %collective-permute-done.1.from_high = f32[48,384]{1,0:T(8,128)S(1)} collective-permute-done((f32[48,384]{1,0:T(8,128)S(1)}, f32[48,384]{1,0:T(8,128)S(1)}, u32[]{:S(2)}, u32[]{:S(2)}) %collective-permute-start.1) | collective-permute-done | bytes 73760 | tf_op jit(solution)/shard_map/ppermute | solution.py:626
  26.6 0.0 collective-permute-done.2.after_x.refs_1_
  26.6 1.4 %border.1 = (f32[600,128]{1,0:T(8,128)S(1)}, f32[600,128]{1,0:T(8,128)S(1)}) custom-call(f32[10,16,128]{2,1,0:T(8,128)S(1)} %collective-permute-done.2.after_x.refs_1_, f32[1,48,128]{2,1,0:T(8,128)S(1)} %collective-permute-done.3.after_y.refs_3_, f32[16,48,384]{2,1,0:T(8,128)} %state.1, f32[16,48,384]{2,1,0:T(8,128)} %diffuse.1, f32[48,384]{1,0:T(8,128)} %vertical_hbm.5, ...), custom_call_target="tpu_custom_call" | custom-call | tf_op jit(solution)/shard_map/border/pallas_call | solution.py:627
  28.0 0.0 copy-start
  28.0 0.7 collective-permute-start.4
  28.7 9.8 %collective-permute-start.5 = (f32[600,128]{1,0:T(8,128)S(1)}, f32[600,128]{1,0:T(8,128)S(1)}, u32[]{:S(2)}, u32[]{:S(2)}) collective-permute-start(f32[600,128]{1,0:T(8,128)S(1)} %get-tuple-element.29), channel_id=1, source_target_pairs={{0,16},{32,48},{64,80},{96,112},{128,144},{160,176},{192,208},{224... | collective-permute-start | bytes 921608 | tf_op jit(solution)/shard_map/ppermute | solution.py:642
  38.4 1.9 %collective-permute-start.8 = (f32[2,16,128]{2,1,0:T(8,128)S(1)}, f32[2,16,128]{2,1,0:T(8,128)S(1)}, u32[]{:S(2)}, u32[]{:S(2)}) collective-permute-start(f32[2,16,128]{2,1,0:T(8,128)S(1)} %get-tuple-element.36.refs_0_), channel_id=1, source_target_pairs={{1,192},{16,208},{32,224},{48,240},{64,128},{80,144},{96,160},{112... | collective-permute-start | bytes 49160 | tf_op jit(solution)/shard_map/ppermute | solution.py:605
  40.4 1.9 %collective-permute-start.7 = (f32[2,16,128]{2,1,0:T(8,128)S(1)}, f32[2,16,128]{2,1,0:T(8,128)S(1)}, u32[]{:S(2)}, u32[]{:S(2)}) collective-permute-start(f32[2,16,128]{2,1,0:T(8,128)S(1)} %get-tuple-element.36.refs_0_), channel_id=1, source_target_pairs={{1,128},{16,144},{32,160},{48,176},{64,192},{80,208},{96,224},{112... | collective-permute-start | bytes 49160 | tf_op jit(solution)/shard_map/ppermute | solution.py:605
  42.3 5.7 %collective-permute-start.6 = (f32[2,16,128]{2,1,0:T(8,128)S(1)}, f32[2,16,128]{2,1,0:T(8,128)S(1)}, u32[]{:S(2)}, u32[]{:S(2)}) collective-permute-start(f32[2,16,128]{2,1,0:T(8,128)S(1)} %get-tuple-element.36.refs_0_), channel_id=1, source_target_pairs={{1,64},{16,80},{32,96},{48,112},{64,1},{80,16},{96,32},{112,48},{1... | collective-permute-start | bytes 49160 | tf_op jit(solution)/shard_map/ppermute | solution.py:605
  48.0 0.0 collective-permute-done.8.refs_3_
  48.0 0.7 collective-permute-start.11
  48.7 0.0 collective-permute-done.7.refs_2_
  48.7 0.7 collective-permute-start.10
  49.4 0.0 collective-permute-done.6.refs_1_
  49.4 0.7 collective-permute-start.9
  50.1 0.0 collective-permute-done.11.refs_7_
  50.1 0.0 collective-permute-done.10.refs_6_
  50.1 0.0 collective-permute-done.9.refs_5_
  50.1 0.7 collective-permute-start.15
  50.8 4.5 %collective-permute-start.14 = (f32[8,16,128]{2,1,0:T(8,128)S(1)}, f32[8,16,128]{2,1,0:T(8,128)S(1)}, u32[]{:S(2)}, u32[]{:S(2)}) collective-permute-start(f32[8,16,128]{2,1,0:T(8,128)S(1)} %get-tuple-element.38.refs_0_), channel_id=1, source_target_pairs={{1,48},{16,32},{32,16},{48,1},{64,112},{80,96},{96,80},{112,64},{1... | collective-permute-start | bytes 196616 | tf_op jit(solution)/shard_map/ppermute | solution.py:605
  55.3 3.4 %collective-permute-start.13 = (f32[8,16,128]{2,1,0:T(8,128)S(1)}, f32[8,16,128]{2,1,0:T(8,128)S(1)}, u32[]{:S(2)}, u32[]{:S(2)}) collective-permute-start(f32[8,16,128]{2,1,0:T(8,128)S(1)} %get-tuple-element.38.refs_0_), channel_id=1, source_target_pairs={{1,32},{16,48},{32,1},{48,16},{64,96},{80,112},{96,64},{112,80},{1... | collective-permute-start | bytes 196616 | tf_op jit(solution)/shard_map/ppermute | solution.py:605
  58.7 0.0 collective-permute-done.4.ra
  58.7 1.9 %collective-permute-start.12 = (f32[8,16,128]{2,1,0:T(8,128)S(1)}, f32[8,16,128]{2,1,0:T(8,128)S(1)}, u32[]{:S(2)}, u32[]{:S(2)}) collective-permute-start(f32[8,16,128]{2,1,0:T(8,128)S(1)} %get-tuple-element.38.refs_0_), channel_id=1, source_target_pairs={{1,16},{16,1},{32,48},{48,32},{64,80},{80,64},{96,112},{112,96},{1... | collective-permute-start | bytes 196616 | tf_op jit(solution)/shard_map/ppermute | solution.py:605
  60.6 0.0 collective-permute-done.5.rb
  60.6 2.4 %prepare.1 = (f32[16,4,72,128]{3,2,1,0:T(8,128)S(1)}, f32[16,4,72,128]{3,2,1,0:T(8,128)S(1)}, f32[4,72,128]{2,1,0:T(8,128)S(1)}, f32[16,4,72,128]{3,2,1,0:T(8,128)S(1)}, f32[64,128]{1,0:T(8,128)S(1)}) custom-call(f32[16,48,384]{2,1,0:T(8,128)} %state.1, f32[16,48,384]{2,1,0:T(8,128)} %diffuse.1, f32[48,384]{1,0:T(8,128)} %vertical_hbm.5, ...), custom_call_target="tpu_custom_call" | custom-call | tf_op jit(solution)/shard_map/prepare/pallas_call | solution.py:650
  63.1 0.0 collective-permute-done.14.refs_3_
  63.1 0.0 collective-permute-done.13.refs_2_
  63.1 2.1 %collective-permute-done.12.refs_1_ = f32[8,16,128]{2,1,0:T(8,128)S(1)} collective-permute-done((f32[8,16,128]{2,1,0:T(8,128)S(1)}, f32[8,16,128]{2,1,0:T(8,128)S(1)}, u32[]{:S(2)}, u32[]{:S(2)}) %collective-permute-start.12) | collective-permute-done | bytes 65568 | tf_op jit(solution)/shard_map/ppermute | solution.py:605
  65.2 0.0 collective-permute-done.15.refs_5_
  65.2 0.4 edges.1
  65.6 4.3 %collective-permute-start.16 = (f32[256,128]{1,0:T(8,128)S(1)}, f32[256,128]{1,0:T(8,128)S(1)}, u32[]{:S(2)}, u32[]{:S(2)}) collective-permute-start(f32[256,128]{1,0:T(8,128)S(1)} %edges.1), channel_id=1, source_target_pairs={{1,0},{17,1},{14,15},{30,14},{497,496},{481,497},{510,511},{494,510}} | collective-permute-start | bytes 393224 | tf_op jit(solution)/shard_map/ppermute | solution.py:675
  70.0 1.9 %collective-permute-done.16.brought_ref = f32[256,128]{1,0:T(8,128)S(1)} collective-permute-done((f32[256,128]{1,0:T(8,128)S(1)}, f32[256,128]{1,0:T(8,128)S(1)}, u32[]{:S(2)}, u32[]{:S(2)}) %collective-permute-start.16) | collective-permute-done | bytes 131104 | tf_op jit(solution)/shard_map/ppermute | solution.py:675
  71.9 0.0 copy-done
  71.9 6.3 %steps.1 = (f32[16,48,384]{2,1,0:T(8,128)}, f32[16,4,72,128]{3,2,1,0:T(8,128)S(1)}) custom-call(s32[2]{0:T(128)S(1)} %copy-done, f32[2,16,128]{2,1,0:T(8,128)} %fill_we_hbm.3, f32[48,384]{1,0:T(8,128)S(1)} %collective-permute-done.from_low, f32[48,384]{1,0:T(8,128)S(1)} %collective-permute-done.1.from_high, ...), custom_call_target="tpu_custom_call", output_to_operand_aliasing={{1}: (4, {})} | custom-call | tf_op jit(solution)/shard_map/steps/pallas_call | solution.py:677
  (2 shorter events, 0.0 us)
Async XLA Ops:
  2.1 24.4 %collective-permute-start.2 = (f32[10,16,128]{2,1,0:T(8,128)S(1)}, f32[10,16,128]{2,1,0:T(8,128)S(1)}, u32[]{:S(2)}, u32[]{:S(2)}) collective-permute-start(f32[10,16,128]{2,1,0:T(8,128)S(1)} %get-tuple-element.25.refs_0_), channel_id=1, source_target_pairs={{1,256},{16,272},{32,288},{48,304},{64,320},{80,336},{96,352},{112... | collective-permute-start | bytes 245768 | tf_op jit(solution)/shard_map/ppermute | solution.py:605
  19.0 5.0 %collective-permute-start = (f32[48,384]{1,0:T(8,128)S(1)}, f32[48,384]{1,0:T(8,128)S(1)}, u32[]{:S(2)}, u32[]{:S(2)}) collective-permute-start(f32[48,384]{1,0:T(8,128)S(1)} %get-tuple-element.23), channel_id=1, source_target_pairs={{0,1},{1,2},{2,3},{3,4},{4,5},{5,6},{6,7},{7,8},{8,9},{9,10},{10,1... | collective-permute-start | bytes 221192 | tf_op jit(solution)/shard_map/ppermute | solution.py:625
  20.9 5.7 %collective-permute-start.1 = (f32[48,384]{1,0:T(8,128)S(1)}, f32[48,384]{1,0:T(8,128)S(1)}, u32[]{:S(2)}, u32[]{:S(2)}) collective-permute-start(f32[48,384]{1,0:T(8,128)S(1)} %get-tuple-element.24), channel_id=1, source_target_pairs={{1,0},{2,1},{3,2},{4,3},{5,4},{6,5},{7,6},{8,7},{9,8},{10,9},{11,1... | collective-permute-start | bytes 221192 | tf_op jit(solution)/shard_map/ppermute | solution.py:626
  23.3 0.7 collective-permute-start.3
  28.0 43.9 %copy-start = (s32[2]{0:T(128)S(1)}, s32[2]{0:T(128)}, u32[]{:S(2)}) copy-start(s32[2]{0:T(128)} %jump.1) | copy-start | bytes 28
  28.0 30.7 %collective-permute-start.4 = (f32[600,128]{1,0:T(8,128)S(1)}, f32[600,128]{1,0:T(8,128)S(1)}, u32[]{:S(2)}, u32[]{:S(2)}) collective-permute-start(f32[600,128]{1,0:T(8,128)S(1)} %get-tuple-element.28), channel_id=1, source_target_pairs={{16,32},{48,64},{80,96},{112,128},{144,160},{176,192},{208,224},{2... | collective-permute-start | bytes 921608 | tf_op jit(solution)/shard_map/ppermute | solution.py:641
  28.7 31.9 %collective-permute-start.5 = (f32[600,128]{1,0:T(8,128)S(1)}, f32[600,128]{1,0:T(8,128)S(1)}, u32[]{:S(2)}, u32[]{:S(2)}) collective-permute-start(f32[600,128]{1,0:T(8,128)S(1)} %get-tuple-element.29), channel_id=1, source_target_pairs={{0,16},{32,48},{64,80},{96,112},{128,144},{160,176},{192,208},{224... | collective-permute-start | bytes 921608 | tf_op jit(solution)/shard_map/ppermute | solution.py:642
  38.4 9.6 %collective-permute-start.8 = (f32[2,16,128]{2,1,0:T(8,128)S(1)}, f32[2,16,128]{2,1,0:T(8,128)S(1)}, u32[]{:S(2)}, u32[]{:S(2)}) collective-permute-start(f32[2,16,128]{2,1,0:T(8,128)S(1)} %get-tuple-element.36.refs_0_), channel_id=1, source_target_pairs={{1,192},{16,208},{32,224},{48,240},{64,128},{80,144},{96,160},{112... | collective-permute-start | bytes 49160 | tf_op jit(solution)/shard_map/ppermute | solution.py:605
  40.4 8.3 %collective-permute-start.7 = (f32[2,16,128]{2,1,0:T(8,128)S(1)}, f32[2,16,128]{2,1,0:T(8,128)S(1)}, u32[]{:S(2)}, u32[]{:S(2)}) collective-permute-start(f32[2,16,128]{2,1,0:T(8,128)S(1)} %get-tuple-element.36.refs_0_), channel_id=1, source_target_pairs={{1,128},{16,144},{32,160},{48,176},{64,192},{80,208},{96,224},{112... | collective-permute-start | bytes 49160 | tf_op jit(solution)/shard_map/ppermute | solution.py:605
  42.3 7.1 %collective-permute-start.6 = (f32[2,16,128]{2,1,0:T(8,128)S(1)}, f32[2,16,128]{2,1,0:T(8,128)S(1)}, u32[]{:S(2)}, u32[]{:S(2)}) collective-permute-start(f32[2,16,128]{2,1,0:T(8,128)S(1)} %get-tuple-element.36.refs_0_), channel_id=1, source_target_pairs={{1,64},{16,80},{32,96},{48,112},{64,1},{80,16},{96,32},{112,48},{1... | collective-permute-start | bytes 49160 | tf_op jit(solution)/shard_map/ppermute | solution.py:605
  48.0 2.1 %collective-permute-start.11 = (f32[2,48,128]{2,1,0:T(8,128)S(1)}, f32[2,48,128]{2,1,0:T(8,128)S(1)}, u32[]{:S(2)}, u32[]{:S(2)}) collective-permute-start(f32[2,48,128]{2,1,0:T(8,128)S(1)} %get-tuple-element.37.refs_4_), channel_id=1, source_target_pairs={{0,6},{17,7},{2,4},{3,5},{4,2},{5,3},{6,0},{7,17},{8,30},{9,15},{1... | collective-permute-start | bytes 147464 | tf_op jit(solution)/shard_map/ppermute | solution.py:605
  48.7 1.4 %collective-permute-start.10 = (f32[2,48,128]{2,1,0:T(8,128)S(1)}, f32[2,48,128]{2,1,0:T(8,128)S(1)}, u32[]{:S(2)}, u32[]{:S(2)}) collective-permute-start(f32[2,48,128]{2,1,0:T(8,128)S(1)} %get-tuple-element.37.refs_4_), channel_id=1, source_target_pairs={{0,4},{17,5},{2,6},{3,7},{4,0},{5,17},{6,2},{7,3},{8,12},{9,13},{1... | collective-permute-start | bytes 147464 | tf_op jit(solution)/shard_map/ppermute | solution.py:605
  49.4 0.7 collective-permute-start.9
  50.1 15.1 %collective-permute-start.15 = (f32[8,48,128]{2,1,0:T(8,128)S(1)}, f32[8,48,128]{2,1,0:T(8,128)S(1)}, u32[]{:S(2)}, u32[]{:S(2)}) collective-permute-start(f32[8,48,128]{2,1,0:T(8,128)S(1)} %get-tuple-element.39.refs_4_), channel_id=1, source_target_pairs={{0,17},{17,0},{2,3},{3,2},{4,5},{5,4},{6,7},{7,6},{8,9},{9,8},{10,... | collective-permute-start | bytes 589832 | tf_op jit(solution)/shard_map/ppermute | solution.py:605
  50.8 12.3 %collective-permute-start.14 = (f32[8,16,128]{2,1,0:T(8,128)S(1)}, f32[8,16,128]{2,1,0:T(8,128)S(1)}, u32[]{:S(2)}, u32[]{:S(2)}) collective-permute-start(f32[8,16,128]{2,1,0:T(8,128)S(1)} %get-tuple-element.38.refs_0_), channel_id=1, source_target_pairs={{1,48},{16,32},{32,16},{48,1},{64,112},{80,96},{96,80},{112,64},{1... | collective-permute-start | bytes 196616 | tf_op jit(solution)/shard_map/ppermute | solution.py:605
  55.3 7.8 %collective-permute-start.13 = (f32[8,16,128]{2,1,0:T(8,128)S(1)}, f32[8,16,128]{2,1,0:T(8,128)S(1)}, u32[]{:S(2)}, u32[]{:S(2)}) collective-permute-start(f32[8,16,128]{2,1,0:T(8,128)S(1)} %get-tuple-element.38.refs_0_), channel_id=1, source_target_pairs={{1,32},{16,48},{32,1},{48,16},{64,96},{80,112},{96,64},{112,80},{1... | collective-permute-start | bytes 196616 | tf_op jit(solution)/shard_map/ppermute | solution.py:605
  58.7 6.5 %collective-permute-start.12 = (f32[8,16,128]{2,1,0:T(8,128)S(1)}, f32[8,16,128]{2,1,0:T(8,128)S(1)}, u32[]{:S(2)}, u32[]{:S(2)}) collective-permute-start(f32[8,16,128]{2,1,0:T(8,128)S(1)} %get-tuple-element.38.refs_0_), channel_id=1, source_target_pairs={{1,16},{16,1},{32,48},{48,32},{64,80},{80,64},{96,112},{112,96},{1... | collective-permute-start | bytes 196616 | tf_op jit(solution)/shard_map/ppermute | solution.py:605
  65.6 6.2 %collective-permute-start.16 = (f32[256,128]{1,0:T(8,128)S(1)}, f32[256,128]{1,0:T(8,128)S(1)}, u32[]{:S(2)}, u32[]{:S(2)}) collective-permute-start(f32[256,128]{1,0:T(8,128)S(1)} %edges.1), channel_id=1, source_target_pairs={{1,0},{17,1},{14,15},{30,14},{497,496},{481,497},{510,511},{494,510}} | collective-permute-start | bytes 393224 | tf_op jit(solution)/shard_map/ppermute | solution.py:675

commit v7 on v6

--- a/solution.py
+++ b/solution.py
@@ -637,7 +637,7 @@
         ],
         compiler_params=pltpu.CompilerParams(vmem_limit_bytes=8 << 20),
         name="border",
-    )(parts_x[-1], parts_y[-1], state, diffuse, vertical, from_low, from_high, colpack)
+    )(parts_x[-1], colpack, state, diffuse, vertical, from_low, from_high, colpack)
     ra = lax.ppermute(xa, "nx", pairs_a)
     rb = lax.ppermute(xb, "nx", pairs_b)
     chain_x, chain_y = join(parts_x, parts_y, len(masks_of(rounds_x[:1])), len(masks_of(rounds_y[:1])), "join_first")

time: 78.7 us -> 81.9 us (1.041)
  waiting for transfers between devices: 6.66 us -> 8.42 us
  starting transfers between devices: 58.5 us -> 60.1 us
    ppermute x1, starting transfers between devices: 9.76 us -> 2.46 us  [on_device(): rb = lax.ppermute(xb, 'nx', pairs_b)]
    ppermute x12, starting transfers between devices: 39.4 us -> 45.1 us  [along(): lax.ppermute(chain, both, [(own[n], own[n ^ m]) for own in sets for n in...]
    ppermute x1, starting transfers between devices: 4.33 us -> 7.51 us  [on_device(): brought = lax.ppermute(edges, both, bring)]
  transfers between devices with their start and end apart: 17 -> 17, of which waited for: 3 -> 5; matrix products, arithmetic and copies ran while one was open for 0% -> 0% of each run, Pallas kernels for 3% -> 3%
where the time goes in v7:
time: 81.9 us; the launch traced here: 81.4 us
  starting transfers between devices  60.1 us (73%)
  Pallas kernels  12.6 us (15%)
  waiting for transfers between devices  8.42 us (10%)
    ppermute x12, starting transfers between devices, along(): lax.ppermute(chain, both, [(own[n], own[n ^ m]) for own in sets for n in...  45.1 us
    ppermute x1, starting transfers between devices, on_device(): brought = lax.ppermute(edges, both, bring)  7.51 us
    pallas_call x1, Pallas kernels, on_device(): pl.pallas_call(functools.partial(main_kernel, count_x, count_y), out_shap...  6.16 us
    ppermute x1, waiting for transfers between devices, on_device(): from_high = lax.ppermute(y_low, 'ny', down)  3.25 us
    ppermute x12, waiting for transfers between devices, along(): lax.ppermute(chain, both, [(own[n], own[n ^ m]) for own in sets for n in...  2.75 us
    ppermute x1, starting transfers between devices, on_device(): rb = lax.ppermute(xb, 'nx', pairs_b)  2.46 us
    pallas_call x1, Pallas kernels, on_device(): pl.pallas_call(prepare_kernel, out_shape=(shape(*big), shape(*big), shape...  2.45 us
    ppermute x1, waiting for transfers between devices, on_device(): brought = lax.ppermute(edges, both, bring)  2.41 us
  transfers between devices with their start and end apart: 17, of which 5 were waited for; matrix products, arithmetic and copies ran while one was open for 0% of the time, Pallas kernels for 3%

profile of v7, /device:TPU:1, one launch (start us, length us, event | category | flops | bytes accessed | tf_op | source)
XLA Modules:
  0.0 81.4 jit_solution(5881000098307018119)
XLA Ops:
  0.0 2.1 %pack.1 = (f32[48,384]{1,0:T(8,128)S(1)}, f32[48,384]{1,0:T(8,128)S(1)}, f32[10,16,128]{2,1,0:T(8,128)S(1)}, f32[1,48,128]{2,1,0:T(8,128)S(1)}, f32[48,128]{1,0:T(8,128)S(1)}, /*index=5*/f32[8,384]{1,0:T(8,128)S(1)}) custom-call(f32[16,48,384]{2,1,0:T(8,128)} %state.1, f32[16,48,384]{2,1,0:T(8,128)} %diffuse.1, f32[48,384]{1,0:T(8,128)} %vertical_hbm.5, ...), custom_call_target="tpu_custom_call" | custom-call | tf_op jit(solution)/shard_map/pack/pallas_call | solution.py:544
  2.1 16.8 %collective-permute-start.2 = (f32[10,16,128]{2,1,0:T(8,128)S(1)}, f32[10,16,128]{2,1,0:T(8,128)S(1)}, u32[]{:S(2)}, u32[]{:S(2)}) collective-permute-start(f32[10,16,128]{2,1,0:T(8,128)S(1)} %get-tuple-element.25.refs_0_), channel_id=1, source_target_pairs={{1,256},{16,272},{32,288},{48,304},{64,320},{80,336},{96,352},{112... | collective-permute-start | bytes 245768 | tf_op jit(solution)/shard_map/ppermute | solution.py:605
  19.0 1.9 %collective-permute-start = (f32[48,384]{1,0:T(8,128)S(1)}, f32[48,384]{1,0:T(8,128)S(1)}, u32[]{:S(2)}, u32[]{:S(2)}) collective-permute-start(f32[48,384]{1,0:T(8,128)S(1)} %get-tuple-element.23), channel_id=1, source_target_pairs={{0,1},{1,2},{2,3},{3,4},{4,5},{5,6},{6,7},{7,8},{8,9},{9,10},{10,1... | collective-permute-start | bytes 221192 | tf_op jit(solution)/shard_map/ppermute | solution.py:625
  20.9 2.4 %collective-permute-start.1 = (f32[48,384]{1,0:T(8,128)S(1)}, f32[48,384]{1,0:T(8,128)S(1)}, u32[]{:S(2)}, u32[]{:S(2)}) collective-permute-start(f32[48,384]{1,0:T(8,128)S(1)} %get-tuple-element.24), channel_id=1, source_target_pairs={{1,0},{2,1},{3,2},{4,3},{5,4},{6,5},{7,6},{8,7},{9,8},{10,9},{11,1... | collective-permute-start | bytes 221192 | tf_op jit(solution)/shard_map/ppermute | solution.py:626
  23.3 0.0 collective-permute-done.from_low
  23.3 3.2 %collective-permute-done.1.from_high = f32[48,384]{1,0:T(8,128)S(1)} collective-permute-done((f32[48,384]{1,0:T(8,128)S(1)}, f32[48,384]{1,0:T(8,128)S(1)}, u32[]{:S(2)}, u32[]{:S(2)}) %collective-permute-start.1) | collective-permute-done | bytes 73760 | tf_op jit(solution)/shard_map/ppermute | solution.py:626
  26.6 0.0 collective-permute-done.2.after_x.refs_1_
  26.6 1.4 %border.1 = (f32[600,128]{1,0:T(8,128)S(1)}, f32[600,128]{1,0:T(8,128)S(1)}) custom-call(f32[10,16,128]{2,1,0:T(8,128)S(1)} %collective-permute-done.2.after_x.refs_1_, f32[48,128]{1,0:T(8,128)S(1)} %get-tuple-element.26.after_y.colpack, f32[16,48,384]{2,1,0:T(8,128)} %state.1, f32[16,48,384]{2,1,0:T(8,128)} %diffuse.1, f32[48,384]{1,0:T(8,128)} %vertical_hbm.5, ...), custom_call_target="tpu_custom_call" | custom-call | tf_op jit(solution)/shard_map/border/pallas_call | solution.py:627
  28.0 0.0 copy-start
  28.0 0.7 collective-permute-start.3
  28.7 2.5 %collective-permute-start.4 = (f32[600,128]{1,0:T(8,128)S(1)}, f32[600,128]{1,0:T(8,128)S(1)}, u32[]{:S(2)}, u32[]{:S(2)}) collective-permute-start(f32[600,128]{1,0:T(8,128)S(1)} %get-tuple-element.28), channel_id=1, source_target_pairs={{0,16},{32,48},{64,80},{96,112},{128,144},{160,176},{192,208},{224... | collective-permute-start | bytes 921608 | tf_op jit(solution)/shard_map/ppermute | solution.py:642
  31.1 0.7 collective-permute-start.5
  31.8 0.0 collective-permute-done.5.refs_3_
  31.8 5.4 %collective-permute-start.8 = (f32[2,16,128]{2,1,0:T(8,128)S(1)}, f32[2,16,128]{2,1,0:T(8,128)S(1)}, u32[]{:S(2)}, u32[]{:S(2)}) collective-permute-start(f32[2,16,128]{2,1,0:T(8,128)S(1)} %get-tuple-element.36.refs_0_), channel_id=1, source_target_pairs={{1,192},{16,208},{32,224},{48,240},{64,128},{80,144},{96,160},{112... | collective-permute-start | bytes 49160 | tf_op jit(solution)/shard_map/ppermute | solution.py:605
  37.3 2.5 %collective-permute-start.7 = (f32[2,16,128]{2,1,0:T(8,128)S(1)}, f32[2,16,128]{2,1,0:T(8,128)S(1)}, u32[]{:S(2)}, u32[]{:S(2)}) collective-permute-start(f32[2,16,128]{2,1,0:T(8,128)S(1)} %get-tuple-element.36.refs_0_), channel_id=1, source_target_pairs={{1,128},{16,144},{32,160},{48,176},{64,192},{80,208},{96,224},{112... | collective-permute-start | bytes 49160 | tf_op jit(solution)/shard_map/ppermute | solution.py:605
  39.8 2.1 %collective-permute-start.6 = (f32[2,16,128]{2,1,0:T(8,128)S(1)}, f32[2,16,128]{2,1,0:T(8,128)S(1)}, u32[]{:S(2)}, u32[]{:S(2)}) collective-permute-start(f32[2,16,128]{2,1,0:T(8,128)S(1)} %get-tuple-element.36.refs_0_), channel_id=1, source_target_pairs={{1,64},{16,80},{32,96},{48,112},{64,1},{80,16},{96,32},{112,48},{1... | collective-permute-start | bytes 49160 | tf_op jit(solution)/shard_map/ppermute | solution.py:605
  42.0 0.0 collective-permute-done.8.refs_3_
  42.0 0.7 collective-permute-start.11
  42.7 1.2 %collective-permute-done.7.refs_2_ = f32[2,16,128]{2,1,0:T(8,128)S(1)} collective-permute-done((f32[2,16,128]{2,1,0:T(8,128)S(1)}, f32[2,16,128]{2,1,0:T(8,128)S(1)}, u32[]{:S(2)}, u32[]{:S(2)}) %collective-permute-start.7) | collective-permute-done | bytes 16416 | tf_op jit(solution)/shard_map/ppermute | solution.py:605
  43.8 0.7 collective-permute-start.10
  44.5 0.4 collective-permute-done.6.refs_1_
  44.9 0.7 collective-permute-start.9
  45.5 0.0 collective-permute-done.11.refs_7_
  45.6 0.0 collective-permute-done.10.refs_6_
  45.6 0.0 collective-permute-done.9.refs_5_
  45.6 0.7 collective-permute-start.15
  46.3 9.6 %collective-permute-start.14 = (f32[8,16,128]{2,1,0:T(8,128)S(1)}, f32[8,16,128]{2,1,0:T(8,128)S(1)}, u32[]{:S(2)}, u32[]{:S(2)}) collective-permute-start(f32[8,16,128]{2,1,0:T(8,128)S(1)} %get-tuple-element.38.refs_0_), channel_id=1, source_target_pairs={{1,48},{16,32},{32,16},{48,1},{64,112},{80,96},{96,80},{112,64},{1... | collective-permute-start | bytes 196616 | tf_op jit(solution)/shard_map/ppermute | solution.py:605
  55.9 3.4 %collective-permute-start.13 = (f32[8,16,128]{2,1,0:T(8,128)S(1)}, f32[8,16,128]{2,1,0:T(8,128)S(1)}, u32[]{:S(2)}, u32[]{:S(2)}) collective-permute-start(f32[8,16,128]{2,1,0:T(8,128)S(1)} %get-tuple-element.38.refs_0_), channel_id=1, source_target_pairs={{1,32},{16,48},{32,1},{48,16},{64,96},{80,112},{96,64},{112,80},{1... | collective-permute-start | bytes 196616 | tf_op jit(solution)/shard_map/ppermute | solution.py:605
  59.2 0.0 collective-permute-done.3.ra
  59.3 1.9 %collective-permute-start.12 = (f32[8,16,128]{2,1,0:T(8,128)S(1)}, f32[8,16,128]{2,1,0:T(8,128)S(1)}, u32[]{:S(2)}, u32[]{:S(2)}) collective-permute-start(f32[8,16,128]{2,1,0:T(8,128)S(1)} %get-tuple-element.38.refs_0_), channel_id=1, source_target_pairs={{1,16},{16,1},{32,48},{48,32},{64,80},{80,64},{96,112},{112,96},{1... | collective-permute-start | bytes 196616 | tf_op jit(solution)/shard_map/ppermute | solution.py:605
  61.2 0.0 collective-permute-done.4.rb
  61.2 2.4 %prepare.1 = (f32[16,4,72,128]{3,2,1,0:T(8,128)S(1)}, f32[16,4,72,128]{3,2,1,0:T(8,128)S(1)}, f32[4,72,128]{2,1,0:T(8,128)S(1)}, f32[16,4,72,128]{3,2,1,0:T(8,128)S(1)}, f32[64,128]{1,0:T(8,128)S(1)}) custom-call(f32[16,48,384]{2,1,0:T(8,128)} %state.1, f32[16,48,384]{2,1,0:T(8,128)} %diffuse.1, f32[48,384]{1,0:T(8,128)} %vertical_hbm.5, ...), custom_call_target="tpu_custom_call" | custom-call | tf_op jit(solution)/shard_map/prepare/pallas_call | solution.py:650
  63.7 0.0 collective-permute-done.14.refs_3_
  63.7 0.0 collective-permute-done.13.refs_2_
  63.7 1.2 %collective-permute-done.12.refs_1_ = f32[8,16,128]{2,1,0:T(8,128)S(1)} collective-permute-done((f32[8,16,128]{2,1,0:T(8,128)S(1)}, f32[8,16,128]{2,1,0:T(8,128)S(1)}, u32[]{:S(2)}, u32[]{:S(2)}) %collective-permute-start.12) | collective-permute-done | bytes 65568 | tf_op jit(solution)/shard_map/ppermute | solution.py:605
  64.8 0.0 collective-permute-done.15.refs_5_
  64.8 0.4 edges.1
  65.3 7.5 %collective-permute-start.16 = (f32[256,128]{1,0:T(8,128)S(1)}, f32[256,128]{1,0:T(8,128)S(1)}, u32[]{:S(2)}, u32[]{:S(2)}) collective-permute-start(f32[256,128]{1,0:T(8,128)S(1)} %edges.1), channel_id=1, source_target_pairs={{1,0},{17,1},{14,15},{30,14},{497,496},{481,497},{510,511},{494,510}} | collective-permute-start | bytes 393224 | tf_op jit(solution)/shard_map/ppermute | solution.py:675
  72.8 2.4 %collective-permute-done.16.brought_ref = f32[256,128]{1,0:T(8,128)S(1)} collective-permute-done((f32[256,128]{1,0:T(8,128)S(1)}, f32[256,128]{1,0:T(8,128)S(1)}, u32[]{:S(2)}, u32[]{:S(2)}) %collective-permute-start.16) | collective-permute-done | bytes 131104 | tf_op jit(solution)/shard_map/ppermute | solution.py:675
  75.2 0.0 copy-done
  75.2 6.2 %steps.1 = (f32[16,48,384]{2,1,0:T(8,128)}, f32[16,4,72,128]{3,2,1,0:T(8,128)S(1)}) custom-call(s32[2]{0:T(128)S(1)} %copy-done, f32[2,16,128]{2,1,0:T(8,128)} %fill_we_hbm.3, f32[48,384]{1,0:T(8,128)S(1)} %collective-permute-done.from_low, f32[48,384]{1,0:T(8,128)S(1)} %collective-permute-done.1.from_high, ...), custom_call_target="tpu_custom_call", output_to_operand_aliasing={{1}: (4, {})} | custom-call | tf_op jit(solution)/shard_map/steps/pallas_call | solution.py:677
  (2 shorter events, 0.0 us)
Async XLA Ops:
  2.1 24.4 %collective-permute-start.2 = (f32[10,16,128]{2,1,0:T(8,128)S(1)}, f32[10,16,128]{2,1,0:T(8,128)S(1)}, u32[]{:S(2)}, u32[]{:S(2)}) collective-permute-start(f32[10,16,128]{2,1,0:T(8,128)S(1)} %get-tuple-element.25.refs_0_), channel_id=1, source_target_pairs={{1,256},{16,272},{32,288},{48,304},{64,320},{80,336},{96,352},{112... | collective-permute-start | bytes 245768 | tf_op jit(solution)/shard_map/ppermute | solution.py:605
  19.0 4.3 %collective-permute-start = (f32[48,384]{1,0:T(8,128)S(1)}, f32[48,384]{1,0:T(8,128)S(1)}, u32[]{:S(2)}, u32[]{:S(2)}) collective-permute-start(f32[48,384]{1,0:T(8,128)S(1)} %get-tuple-element.23), channel_id=1, source_target_pairs={{0,1},{1,2},{2,3},{3,4},{4,5},{5,6},{6,7},{7,8},{8,9},{9,10},{10,1... | collective-permute-start | bytes 221192 | tf_op jit(solution)/shard_map/ppermute | solution.py:625
  20.9 5.7 %collective-permute-start.1 = (f32[48,384]{1,0:T(8,128)S(1)}, f32[48,384]{1,0:T(8,128)S(1)}, u32[]{:S(2)}, u32[]{:S(2)}) collective-permute-start(f32[48,384]{1,0:T(8,128)S(1)} %get-tuple-element.24), channel_id=1, source_target_pairs={{1,0},{2,1},{3,2},{4,3},{5,4},{6,5},{7,6},{8,7},{9,8},{10,9},{11,1... | collective-permute-start | bytes 221192 | tf_op jit(solution)/shard_map/ppermute | solution.py:626
  28.0 47.2 %copy-start = (s32[2]{0:T(128)S(1)}, s32[2]{0:T(128)}, u32[]{:S(2)}) copy-start(s32[2]{0:T(128)} %jump.1) | copy-start | bytes 28
  28.0 31.3 %collective-permute-start.3 = (f32[600,128]{1,0:T(8,128)S(1)}, f32[600,128]{1,0:T(8,128)S(1)}, u32[]{:S(2)}, u32[]{:S(2)}) collective-permute-start(f32[600,128]{1,0:T(8,128)S(1)} %get-tuple-element.27), channel_id=1, source_target_pairs={{16,32},{48,64},{80,96},{112,128},{144,160},{176,192},{208,224},{2... | collective-permute-start | bytes 921608 | tf_op jit(solution)/shard_map/ppermute | solution.py:641
  28.7 32.5 %collective-permute-start.4 = (f32[600,128]{1,0:T(8,128)S(1)}, f32[600,128]{1,0:T(8,128)S(1)}, u32[]{:S(2)}, u32[]{:S(2)}) collective-permute-start(f32[600,128]{1,0:T(8,128)S(1)} %get-tuple-element.28), channel_id=1, source_target_pairs={{0,16},{32,48},{64,80},{96,112},{128,144},{160,176},{192,208},{224... | collective-permute-start | bytes 921608 | tf_op jit(solution)/shard_map/ppermute | solution.py:642
  31.1 0.7 collective-permute-start.5
  31.8 10.2 %collective-permute-start.8 = (f32[2,16,128]{2,1,0:T(8,128)S(1)}, f32[2,16,128]{2,1,0:T(8,128)S(1)}, u32[]{:S(2)}, u32[]{:S(2)}) collective-permute-start(f32[2,16,128]{2,1,0:T(8,128)S(1)} %get-tuple-element.36.refs_0_), channel_id=1, source_target_pairs={{1,192},{16,208},{32,224},{48,240},{64,128},{80,144},{96,160},{112... | collective-permute-start | bytes 49160 | tf_op jit(solution)/shard_map/ppermute | solution.py:605
  37.3 6.6 %collective-permute-start.7 = (f32[2,16,128]{2,1,0:T(8,128)S(1)}, f32[2,16,128]{2,1,0:T(8,128)S(1)}, u32[]{:S(2)}, u32[]{:S(2)}) collective-permute-start(f32[2,16,128]{2,1,0:T(8,128)S(1)} %get-tuple-element.36.refs_0_), channel_id=1, source_target_pairs={{1,128},{16,144},{32,160},{48,176},{64,192},{80,208},{96,224},{112... | collective-permute-start | bytes 49160 | tf_op jit(solution)/shard_map/ppermute | solution.py:605
  39.8 5.1 %collective-permute-start.6 = (f32[2,16,128]{2,1,0:T(8,128)S(1)}, f32[2,16,128]{2,1,0:T(8,128)S(1)}, u32[]{:S(2)}, u32[]{:S(2)}) collective-permute-start(f32[2,16,128]{2,1,0:T(8,128)S(1)} %get-tuple-element.36.refs_0_), channel_id=1, source_target_pairs={{1,64},{16,80},{32,96},{48,112},{64,1},{80,16},{96,32},{112,48},{1... | collective-permute-start | bytes 49160 | tf_op jit(solution)/shard_map/ppermute | solution.py:605
  42.0 3.6 %collective-permute-start.11 = (f32[2,48,128]{2,1,0:T(8,128)S(1)}, f32[2,48,128]{2,1,0:T(8,128)S(1)}, u32[]{:S(2)}, u32[]{:S(2)}) collective-permute-start(f32[2,48,128]{2,1,0:T(8,128)S(1)} %get-tuple-element.37.refs_4_), channel_id=1, source_target_pairs={{0,6},{17,7},{2,4},{3,5},{4,2},{5,3},{6,0},{7,17},{8,30},{9,15},{1... | collective-permute-start | bytes 147464 | tf_op jit(solution)/shard_map/ppermute | solution.py:605
  43.8 1.7 %collective-permute-start.10 = (f32[2,48,128]{2,1,0:T(8,128)S(1)}, f32[2,48,128]{2,1,0:T(8,128)S(1)}, u32[]{:S(2)}, u32[]{:S(2)}) collective-permute-start(f32[2,48,128]{2,1,0:T(8,128)S(1)} %get-tuple-element.37.refs_4_), channel_id=1, source_target_pairs={{0,4},{17,5},{2,6},{3,7},{4,0},{5,17},{6,2},{7,3},{8,12},{9,13},{1... | collective-permute-start | bytes 147464 | tf_op jit(solution)/shard_map/ppermute | solution.py:605
  44.9 0.7 collective-permute-start.9
  45.6 19.2 %collective-permute-start.15 = (f32[8,48,128]{2,1,0:T(8,128)S(1)}, f32[8,48,128]{2,1,0:T(8,128)S(1)}, u32[]{:S(2)}, u32[]{:S(2)}) collective-permute-start(f32[8,48,128]{2,1,0:T(8,128)S(1)} %get-tuple-element.39.refs_4_), channel_id=1, source_target_pairs={{0,17},{17,0},{2,3},{3,2},{4,5},{5,4},{6,7},{7,6},{8,9},{9,8},{10,... | collective-permute-start | bytes 589832 | tf_op jit(solution)/shard_map/ppermute | solution.py:605
  46.3 17.4 %collective-permute-start.14 = (f32[8,16,128]{2,1,0:T(8,128)S(1)}, f32[8,16,128]{2,1,0:T(8,128)S(1)}, u32[]{:S(2)}, u32[]{:S(2)}) collective-permute-start(f32[8,16,128]{2,1,0:T(8,128)S(1)} %get-tuple-element.38.refs_0_), channel_id=1, source_target_pairs={{1,48},{16,32},{32,16},{48,1},{64,112},{80,96},{96,80},{112,64},{1... | collective-permute-start | bytes 196616 | tf_op jit(solution)/shard_map/ppermute | solution.py:605
  55.9 7.8 %collective-permute-start.13 = (f32[8,16,128]{2,1,0:T(8,128)S(1)}, f32[8,16,128]{2,1,0:T(8,128)S(1)}, u32[]{:S(2)}, u32[]{:S(2)}) collective-permute-start(f32[8,16,128]{2,1,0:T(8,128)S(1)} %get-tuple-element.38.refs_0_), channel_id=1, source_target_pairs={{1,32},{16,48},{32,1},{48,16},{64,96},{80,112},{96,64},{112,80},{1... | collective-permute-start | bytes 196616 | tf_op jit(solution)/shard_map/ppermute | solution.py:605
  59.3 5.6 %collective-permute-start.12 = (f32[8,16,128]{2,1,0:T(8,128)S(1)}, f32[8,16,128]{2,1,0:T(8,128)S(1)}, u32[]{:S(2)}, u32[]{:S(2)}) collective-permute-start(f32[8,16,128]{2,1,0:T(8,128)S(1)} %get-tuple-element.38.refs_0_), channel_id=1, source_target_pairs={{1,16},{16,1},{32,48},{48,32},{64,80},{80,64},{96,112},{112,96},{1... | collective-permute-start | bytes 196616 | tf_op jit(solution)/shard_map/ppermute | solution.py:605
  65.3 9.9 %collective-permute-start.16 = (f32[256,128]{1,0:T(8,128)S(1)}, f32[256,128]{1,0:T(8,128)S(1)}, u32[]{:S(2)}, u32[]{:S(2)}) collective-permute-start(f32[256,128]{1,0:T(8,128)S(1)} %edges.1), channel_id=1, source_target_pairs={{1,0},{17,1},{14,15},{30,14},{497,496},{481,497},{510,511},{494,510}} | collective-permute-start | bytes 393224 | tf_op jit(solution)/shard_map/ppermute | solution.py:675
